TPU v7x, 32 devices: a whole 2x2x4 slice. The times are simulated.
32 devices in a mesh: dp: 8 (over y, x, core), chan: 4 (over z).
Axes of the slice: x: 2, y: 2, z: 4, core: 2. Of those that a mesh axis runs over, the one named last changes fastest.
Arguments:
- hidden_in: bfloat16 [8, 1024, 768], P('dp', None, 'chan'), may hold values from -6 to 6
- halves: int32 [8, 2], P('dp'), may hold values from 1 to 1024, as said below
- norm1_gain: float32 [768], P('chan'), may hold values from 0.25 to 1.75
- in_proj: bfloat16 [768, 3, 768], P(None, None, 'chan'), may hold values from -0.21875 to 0.21875
- short_taps: float32 [3, 3, 768], P(None, None, 'chan'), may hold values from -3 to 3
- cond_taps: float32 [3, 768], P(None, 'chan'), may hold values from -3 to 3
- filter_in: float32 [33, 64], replicated, may hold values from -2 to 2
- filter_bias: float32 [64], replicated, may hold values from -3.140625 to 3.140625
- filter_out: float32 [64, 768], P(None, 'chan'), may hold values from -0.75 to 0.75
- decay_rate: float32 [768], P('chan'), may hold values from 0.0009765625 to 0.05
- out_proj: bfloat16 [768, 768], P(None, 'chan'), may hold values from -0.21875 to 0.21875
- norm2_gain: float32 [768], P('chan'), may hold values from 0.25 to 1.75
- w_gate: bfloat16 [768, 3072], P(None, 'chan'), may hold values from -0.21875 to 0.21875
- w_up: bfloat16 [768, 3072], P(None, 'chan'), may hold values from -0.21875 to 0.21875
- w_down: bfloat16 [3072, 768], P('chan'), may hold values from -0.15625 to 0.15625
- out_grad: bfloat16 [8, 1024, 768], P('dp', None, 'chan'), may hold values from -6 to 6
Outputs:
- output: float32 [8, 1024, 768], P('dp', None, 'chan')
- input_grad: float32 [8, 1024, 768], P('dp', None, 'chan')
- norm1_gain_grad: float32 [768], P('chan')
- in_proj_grad: float32 [768, 3, 768], P(None, None, 'chan')
- short_taps_grad: float32 [3, 3, 768], P(None, None, 'chan')
- cond_taps_grad: float32 [3, 768], P(None, 'chan')
- filter_in_grad: float32 [33, 64], replicated
- filter_bias_grad: float32 [64], replicated
- filter_out_grad: float32 [64, 768], P(None, 'chan')
- decay_rate_grad: float32 [768], P('chan')
- out_proj_grad: float32 [768, 768], P(None, 'chan')
- norm2_gain_grad: float32 [768], P('chan')
- w_gate_grad: float32 [768, 3072], P(None, 'chan')
- w_up_grad: float32 [768, 3072], P(None, 'chan')
- w_down_grad: float32 [3072, 768], P('chan')
Inputs may be any that keep to these rules, and one draw needn't show every extreme that they name: `halves`: column 0 is a row's split point, column 1 its valid length; the valid length is 512 or more, and 1024 in at least one row; the split point lies between a quarter and three quarters of the valid length.
All inputs are finite; a program needn't handle non-finite values.
Results may differ from a plain program's by a relative error of at most 0.012.
The roundings to bfloat16 on the way count: a program that leaves them out, or rounds other values in their place, can miss the bound.
Values may be sent and summed in bfloat16 or wider, within the bound.
A program may use at most 192 MiB of HBM per device.

v0:
```python
import math

import jax
import jax.numpy as jnp
from jax import lax
from jax.sharding import PartitionSpec as P

highest = lax.Precision.HIGHEST
norm_eps = 1e-05


def band_features(seq_len, feat_count):
    bands = (feat_count - 1) // 2
    positions = jnp.arange(seq_len, dtype=jnp.int32)
    orders = jnp.arange(1, bands + 1, dtype=jnp.int32)
    phases = (positions[:, None] * orders[None, :] % seq_len).astype(jnp.float32) * (
        2.0 * math.pi / seq_len
    )
    position_ramp = positions.astype(jnp.float32)[:, None] / seq_len
    return jnp.concatenate([position_ramp, jnp.sin(phases), jnp.cos(phases)], axis=1)


def delayed(values, tap_weights):
    seq_len = values.shape[1]
    padded = jnp.pad(values, ((0, 0), (2, 0)) + ((0, 0),) * (values.ndim - 2))
    return (
        tap_weights[0] * padded[:, 2:]
        + tap_weights[1] * padded[:, 1 : seq_len + 1]
        + tap_weights[2] * padded[:, :seq_len]
    )


def filter_base(seq_len, filter_in, filter_bias, filter_out):
    features = band_features(seq_len, filter_in.shape[0])
    hidden_wave = jnp.sin(jnp.dot(features, filter_in, precision=highest) + filter_bias)
    return jnp.dot(hidden_wave, filter_out, precision=highest)


def wave_table(row_ids, col_ids, period):
    phases = (row_ids[:, None] * col_ids[None, :] % period).astype(jnp.float32) * (
        2.0 * math.pi / period
    )
    return (jnp.cos(phases), jnp.sin(phases))


def dft_tables(seq_len):
    period = 2 * seq_len
    outer_len = 2
    while outer_len * outer_len < period and period % (2 * outer_len) == 0:
        outer_len = outer_len * 2
    inner_len = period // outer_len
    outer_ids = jnp.arange(outer_len, dtype=jnp.int32)
    half_ids = jnp.arange(outer_len // 2, dtype=jnp.int32)
    inner_ids = jnp.arange(inner_len, dtype=jnp.int32)
    first_section = wave_table(outer_ids, half_ids, outer_len)
    twiddle = wave_table(outer_ids, inner_ids, period)
    second_section = wave_table(inner_ids, inner_ids, inner_len)
    last_section = wave_table(half_ids, outer_ids, outer_len)
    return (first_section, twiddle, second_section, last_section)


def to_spectrum(signal, tables):
    first_section, twiddle, second_section, last_section = tables
    row_count, seq_len, width = signal.shape
    outer_len = first_section[0].shape[0]
    inner_len = second_section[0].shape[0]
    grid = signal.reshape(row_count, outer_len // 2, inner_len, width)
    section_real = jnp.einsum("kn,bnac->bkac", first_section[0], grid, precision=highest)
    section_imag = -jnp.einsum("kn,bnac->bkac", first_section[1], grid, precision=highest)
    twist_cos = twiddle[0][None, :, :, None]
    twist_sin = twiddle[1][None, :, :, None]
    turned_real = section_real * twist_cos + section_imag * twist_sin
    turned_imag = section_imag * twist_cos - section_real * twist_sin
    real_part = jnp.einsum(
        "ma,bkac->bkmc", second_section[0], turned_real, precision=highest
    ) + jnp.einsum("ma,bkac->bkmc", second_section[1], turned_imag, precision=highest)
    imag_part = jnp.einsum(
        "ma,bkac->bkmc", second_section[0], turned_imag, precision=highest
    ) - jnp.einsum("ma,bkac->bkmc", second_section[1], turned_real, precision=highest)
    return (real_part, imag_part)


def from_spectrum(real_part, imag_part, tables):
    first_section, twiddle, second_section, last_section = tables
    row_count, outer_len, inner_len, width = real_part.shape
    period = outer_len * inner_len
    back_real = jnp.einsum(
        "ma,bkmc->bkac", second_section[0], real_part, precision=highest
    ) - jnp.einsum("ma,bkmc->bkac", second_section[1], imag_part, precision=highest)
    back_imag = jnp.einsum(
        "ma,bkmc->bkac", second_section[0], imag_part, precision=highest
    ) + jnp.einsum("ma,bkmc->bkac", second_section[1], real_part, precision=highest)
    twist_cos = twiddle[0][None, :, :, None]
    twist_sin = twiddle[1][None, :, :, None]
    turned_real = back_real * twist_cos - back_imag * twist_sin
    turned_imag = back_imag * twist_cos + back_real * twist_sin
    signal = jnp.einsum(
        "nk,bkac->bnac", last_section[0], turned_real, precision=highest
    ) - jnp.einsum("nk,bkac->bnac", last_section[1], turned_imag, precision=highest)
    return signal.reshape(row_count, period // 2, width) / period


def mixer_local(
    projected,
    short_taps,
    cond_taps,
    filter_in,
    filter_bias,
    filter_out,
    decay_rate,
    half_list,
    tables,
):
    seq_len = projected.shape[1]
    short_out = delayed(projected, short_taps)
    query_part = short_out[:, :, 0]
    key_part = short_out[:, :, 1]
    value_part = short_out[:, :, 2]
    conditioned = delayed(value_part, cond_taps)
    positions = jnp.arange(seq_len, dtype=jnp.float32)[:, None]
    kernel = (
        (filter_base(seq_len, filter_in, filter_bias, filter_out)[None] + jnp.tanh(conditioned))
        * jnp.exp(-decay_rate * positions)[None]
        / math.sqrt(seq_len)
    )
    source = key_part * value_part
    kernel_real, kernel_imag = to_spectrum(kernel, tables)
    mixed_out = jnp.zeros_like(source)
    for half_mask in half_list:
        source_real, source_imag = to_spectrum(source * half_mask, tables)
        prod_real = kernel_real * source_real - kernel_imag * source_imag
        prod_imag = kernel_real * source_imag + kernel_imag * source_real
        mixed_out = mixed_out + from_spectrum(prod_real, prod_imag, tables) * half_mask
    return query_part * mixed_out


def local(
    hidden_in,
    halves,
    norm1_gain,
    in_proj,
    short_taps,
    cond_taps,
    filter_in,
    filter_bias,
    filter_out,
    decay_rate,
    out_proj,
    norm2_gain,
    w_gate,
    w_up,
    w_down,
    out_grad,
):
    seq_len = hidden_in.shape[1]
    full_width = hidden_in.shape[2] * lax.axis_size("chan")
    positions = jnp.arange(seq_len, dtype=jnp.int32)[None, :]
    split_at = halves[:, 0:1]
    valid_len = halves[:, 1:2]
    first_half = (positions < split_at).astype(jnp.float32)[:, :, None]
    second_half = ((positions >= split_at) & (positions < valid_len)).astype(jnp.float32)[
        :, :, None
    ]
    valid_mask = first_half + second_half
    tables = dft_tables(seq_len)

    def moments(first_term, second_term):
        return lax.psum((jnp.sum(first_term, axis=-1), jnp.sum(second_term, axis=-1)), "chan")

    def gathered(values):
        return lax.all_gather(values, "chan", axis=2, tiled=True)

    def summed(values):
        return lax.psum_scatter(values, "chan", scatter_dimension=2, tiled=True)

    def norm_forward(values):
        total_sum, square_sum = moments(values, values * values)
        centre = total_sum[..., None] / full_width
        spread = square_sum[..., None] / full_width - centre * centre
        inverse = lax.rsqrt(spread + norm_eps)
        return ((values - centre) * inverse, inverse)

    def norm_backward(upstream, scale_gain, normed, inverse):
        scaled = upstream * scale_gain
        plain_sum, cross_sum = moments(scaled, scaled * normed)
        result = inverse * (
            scaled - plain_sum[..., None] / full_width - normed * cross_sum[..., None] / full_width
        )
        return (result, jnp.sum(upstream * normed, axis=(0, 1)))

    def mixer_call(proj_in, taps_short, taps_cond, wave_in, wave_bias, wave_out, rates):
        return mixer_local(
            proj_in,
            taps_short,
            taps_cond,
            wave_in,
            wave_bias,
            wave_out,
            rates,
            (first_half, second_half),
            tables,
        )

    inputs = hidden_in.astype(jnp.float32)
    normed1, inverse1 = norm_forward(inputs)
    norm1_full = gathered((normed1 * norm1_gain).astype(jnp.bfloat16))
    projected = jnp.einsum("bld,djc->bljc", norm1_full, in_proj, preferred_element_type=jnp.float32)
    mixer_out, mixer_pullback = jax.vjp(
        mixer_call, projected, short_taps, cond_taps, filter_in, filter_bias, filter_out, decay_rate
    )
    mixer_full = gathered(mixer_out.astype(jnp.bfloat16))
    residual = inputs + jnp.einsum(
        "bld,dc->blc", mixer_full, out_proj, preferred_element_type=jnp.float32
    )
    normed2, inverse2 = norm_forward(residual)
    norm2_full = gathered((normed2 * norm2_gain).astype(jnp.bfloat16))
    gate_val = jnp.einsum("bld,df->blf", norm2_full, w_gate, preferred_element_type=jnp.float32)
    up_val = jnp.einsum("bld,df->blf", norm2_full, w_up, preferred_element_type=jnp.float32)
    sigmoid_gate = jax.nn.sigmoid(gate_val)
    activated = gate_val * sigmoid_gate
    hidden_mid = (activated * up_val).astype(jnp.bfloat16)
    mlp_out = summed(
        jnp.einsum("blf,fd->bld", hidden_mid, w_down, preferred_element_type=jnp.float32)
    )
    output = valid_mask * (residual + mlp_out)
    grad_out = out_grad.astype(jnp.float32) * valid_mask
    grad_full = gathered(grad_out.astype(jnp.bfloat16))
    w_down_grad = jnp.einsum(
        "blf,bld->fd", hidden_mid, grad_full, preferred_element_type=jnp.float32
    )
    hidden_grad = jnp.einsum("bld,fd->blf", grad_full, w_down, preferred_element_type=jnp.float32)
    gate_grad = (
        hidden_grad * up_val * sigmoid_gate * (1.0 + gate_val * (1.0 - sigmoid_gate))
    ).astype(jnp.bfloat16)
    up_grad = (hidden_grad * activated).astype(jnp.bfloat16)
    w_gate_grad = jnp.einsum(
        "bld,blf->df", norm2_full, gate_grad, preferred_element_type=jnp.float32
    )
    w_up_grad = jnp.einsum("bld,blf->df", norm2_full, up_grad, preferred_element_type=jnp.float32)
    norm2_terms = jnp.einsum("blf,df->bld", gate_grad, w_gate, preferred_element_type=jnp.float32)
    norm2_terms = norm2_terms + jnp.einsum(
        "blf,df->bld", up_grad, w_up, preferred_element_type=jnp.float32
    )
    residual_norm_grad, norm2_gain_grad = norm_backward(
        summed(norm2_terms), norm2_gain, normed2, inverse2
    )
    residual_grad = grad_out + residual_norm_grad
    glu_sums = (w_down_grad, w_gate_grad, w_up_grad, norm2_gain_grad)
    proj_grad = residual_grad.astype(jnp.bfloat16)
    out_proj_grad = jnp.einsum(
        "bld,blc->dc", mixer_full, proj_grad, preferred_element_type=jnp.float32
    )
    mixer_grad = summed(
        jnp.einsum("blc,dc->bld", proj_grad, out_proj, preferred_element_type=jnp.float32)
    )
    (
        projected_grad,
        short_grad,
        cond_grad,
        wave_in_grad,
        wave_bias_grad,
        wave_out_grad,
        rate_grad,
    ) = mixer_pullback(mixer_grad)
    projected_low = projected_grad.astype(jnp.bfloat16)
    in_proj_grad = jnp.einsum(
        "bld,bljc->djc", norm1_full, projected_low, preferred_element_type=jnp.float32
    )
    norm1_terms = summed(
        jnp.einsum("bljc,djc->bld", projected_low, in_proj, preferred_element_type=jnp.float32)
    )
    input_norm_grad, norm1_gain_grad = norm_backward(norm1_terms, norm1_gain, normed1, inverse1)
    input_grad = residual_grad + input_norm_grad
    mixer_sums = (
        in_proj_grad,
        out_proj_grad,
        norm1_gain_grad,
        short_grad,
        cond_grad,
        wave_out_grad,
        rate_grad,
    )
    combined = tuple(
        lax.psum(
            (
                w_down_grad,
                w_gate_grad,
                w_up_grad,
                norm2_gain_grad,
                in_proj_grad,
                out_proj_grad,
                norm1_gain_grad,
                short_grad,
                cond_grad,
                wave_out_grad,
                rate_grad,
            ),
            "dp",
        )
    )
    glu_sums = combined[:4]
    mixer_sums = combined[4:]
    wave_in_sum, wave_bias_sum = lax.psum((wave_in_grad, wave_bias_grad), ("dp", "chan"))
    return (
        output,
        input_grad,
        mixer_sums[2],
        mixer_sums[0],
        mixer_sums[3],
        mixer_sums[4],
        wave_in_sum,
        wave_bias_sum,
        mixer_sums[5],
        mixer_sums[6],
        mixer_sums[1],
        glu_sums[3],
        glu_sums[1],
        glu_sums[2],
        glu_sums[0],
    )


def solution(mesh):
    in_specs = (
        P("dp", None, "chan"),
        P("dp", None),
        P("chan"),
        P(None, None, "chan"),
        P(None, None, "chan"),
        P(None, "chan"),
        P(),
        P(),
        P(None, "chan"),
        P("chan"),
        P(None, "chan"),
        P("chan"),
        P(None, "chan"),
        P(None, "chan"),
        P("chan", None),
        P("dp", None, "chan"),
    )
    out_specs = (
        P("dp", None, "chan"),
        P("dp", None, "chan"),
        P("chan"),
        P(None, None, "chan"),
        P(None, None, "chan"),
        P(None, "chan"),
        P(),
        P(),
        P(None, "chan"),
        P("chan"),
        P(None, "chan"),
        P("chan"),
        P(None, "chan"),
        P(None, "chan"),
        P("chan", None),
    )
    return jax.shard_map(local, mesh=mesh, in_specs=in_specs, out_specs=out_specs, check_vma=False)
```

profile of v0, /device:TPU:0, one launch (start us, length us, event | category | flops | bytes accessed | tf_op | source)
XLA Modules:
  0.0 1079.0 jit_solution(10203626013025986748)
XLA Ops:
  8.5 13.7 %all-reduce.26 = (f32[1,1024]{1,0:T(1,128)S(1)}, f32[1,1024]{1,0:T(1,128)S(1)}) all-reduce(f32[1,1024]{1,0:T(1,128)S(1)} %bitcast.787, f32[1,1024]{1,0:T(1,128)S(1)} %bitcast.786), channel_id=1, replica_groups=mesh['dp'=8,'chan'=4] {'chan'}, use_global_device_ids=true, to_apply=%region_3.4 | all-reduce | flops 2048 | bytes 16384 | tf_op jit(solution)/shard_map/psum | solution.py:168
  37.7 2.8 fusion.730
  40.5 20.3 %all-gather.5.cloned.1.call-done = bf16[1,1024,768]{1,2,0:T(8,128)(2,1)} async-done(((bf16[1,1024,192]{1,2,0:T(8,128)(2,1)}), bf16[1,1024,768]{1,2,0:T(8,128)(2,1)}) %all-gather.5.cloned.1.call-update) | async-done | bytes 1572880 | tf_op jit(solution)/shard_map/all_gather | solution.py:171
  70.5 3.8 fusion.248
  74.4 3.8 fusion.250
  78.2 3.9 fusion.244
  82.4 3.9 fusion.246
  90.8 3.8 fusion.252
  94.7 6.5 fusion.66
  101.3 3.3 fusion.109
  104.5 3.3 fusion.111
  107.8 3.3 fusion.101
  111.1 3.5 fusion.103
  114.7 3.3 fusion.117
  117.9 3.3 fusion.119
  121.2 3.4 fusion.134
  124.6 3.7 fusion.131
  128.3 3.4 fusion.140
  131.7 3.3 fusion.137
  135.0 3.3 fusion.125
  138.4 5.6 multiply_add_fusion.7
  158.6 4.7 fusion.54
  172.2 4.1 fusion.85
  185.5 36.1 %all-gather.7.cloned.1.call-done = bf16[1,1024,768]{1,2,0:T(8,128)(2,1)} async-done(((bf16[1,1024,192]{1,2,0:T(8,128)(2,1)}), bf16[1,1024,768]{1,2,0:T(8,128)(2,1)}) %all-gather.7.cloned.1.call-update) | async-done | bytes 1572880 | tf_op jit(solution)/shard_map/all_gather | solution.py:171
  221.6 3.0 fusion.727
  224.5 10.3 all-reduce.25
  240.9 32.3 %all-gather.9.cloned.1.call-done = bf16[1,1024,768]{1,2,0:T(8,128)(2,1)} async-done(((bf16[1,1024,192]{1,2,0:T(8,128)(2,1)}), bf16[1,1024,768]{1,2,0:T(8,128)(2,1)}) %all-gather.9.cloned.1.call-update) | async-done | bytes 1572880 | tf_op jit(solution)/shard_map/all_gather | solution.py:171
  273.2 5.0 fusion.188
  278.2 3.2 fusion.190
  281.4 29.8 %all-gather.11.cloned.1.call-done = bf16[1,1024,768]{1,2,0:T(8,128)(2,1)} async-done(((bf16[1,1024,192]{1,2,0:T(8,128)(2,1)}), bf16[1,1024,768]{1,2,0:T(8,128)(2,1)}) %all-gather.11.cloned.1.call-update) | async-done | bytes 1572880 | tf_op jit(solution)/shard_map/all_gather | solution.py:171
  311.2 6.5 multiply_convert_fusion
  319.8 3.1 add_bitcast_fusion
  322.9 8.6 copy.239
  333.5 118.1 %all-reduce.32.cloned.1.call-done = f32[1,1024,768]{1,0,2:T(1,128)} async-done(((f32[1,1024,768]{1,0,2:T(1,128)}), f32[1,1024,768]{1,0,2:T(1,128)}) %all-reduce.32.cloned.1.call-update) | async-done | bytes 3145744
  455.1 10.3 all-reduce.24
  476.7 4.4 convolution_bitcast_fusion.2
  481.2 8.8 copy.237
  489.9 40.2 %reduce-scatter.2.cloned.1.call-done = f32[1,1024,192]{1,2,0:T(8,128)} async-done(((f32[1,1024,768]{1,2,0:T(8,128)}), f32[1,1024,192]{1,2,0:T(8,128)}) %reduce-scatter.2.cloned.1.call-update) | async-done | bytes 786448 | tf_op jit(solution)/shard_map/reduce_scatter | solution.py:174
  530.2 3.1 multiply_multiply_fusion.2
  539.9 6.3 fusion.292
  546.2 6.6 fusion.294
  559.5 4.7 fusion.296
  564.2 6.6 fusion.298
  570.8 6.5 fusion.167
  577.2 6.3 fusion.164
  583.6 6.5 fusion.173
  590.1 13.1 %multiply_add_fusion.1 = (f32[64,192,32]{1,2,0:T(8,128)}, f32[64,192,32]{1,2,0:T(8,128)}, f32[64,192,32]{1,2,0:T(8,128)}, f32[64,192,32]{1,2,0:T(8,128)}, f32[64,192,32]{1,2,0:T(8,128)S(1)}, /*index=5*/f32[64,192,32]{1,2,0:T(8,128)}) fusion(f32[64,192,32]{1,2,0:T(8,128)S(1)} %copy-done.11, f32[64,192,32]{1,2,0:T(8,128)S(1)} %copy-done.13, ...), kind=kOutput, calls=%fused_computation.150 | convolution fusion | flops 163985408 | bytes 28327936 | tf_op jit(solution)/shard_map/transpose(jvp(ma,bkmc->bkac))/dot_general | solution.py:89
  603.2 3.7 fusion.356
  627.4 5.7 fusion.5
  640.0 5.7 multiply_reduce_fusion.6
  657.4 4.1 fusion.81
  675.4 2.8 multiply_reduce_fusion.2
  680.7 3.1 convolution_bitcast_fusion
  683.8 8.5 copy.278
  692.4 4.9 fusion.180
  697.3 2.8 fusion.184
  700.1 2.8 fusion.186
  709.4 2.7 fusion.731
  712.5 45.1 %all-reduce.20 = (f32[33,64]{1,0:T(8,128)}, f32[64]{0:T(128)}) all-reduce(f32[33,64]{1,0:T(8,128)S(1)} %fusion.300, f32[64]{0:T(128)S(1)} %get-tuple-element.159), channel_id=1, replica_groups=mesh['dp'=8,'chan'=4] {'dp','chan'}, use_global_device_ids=true, to_apply=%region_31.32 | all-reduce | flops 2176 | bytes 17408 | tf_op jit(solution)/shard_map/psum | solution.py:303
  758.7 158.1 %all-reduce.36.cloned.1.call-done = (f32[1,1024,768]{1,0,2:T(1,128)}, f32[1,1024,768]{1,0,2:T(1,128)}) async-done(((f32[1,1024,768]{1,0,2:T(1,128)}, f32[1,1024,768]{1,0,2:T(1,128)}), (f32[1,1024,768]{1,0,2:T(1,128)}, f32[1,1024,768]{1,0,2:T(1,128)})) %all-reduce.36.cloned.1.call-update) | async-done | bytes 6291472
  919.0 27.7 %all-reduce.21 = (f32[192]{0:T(256)}, f32[3,3,192]{2,1,0:T(4,128)}, f32[3,192]{1,0:T(4,128)}, f32[64,192]{1,0:T(8,128)}, f32[192]{0:T(256)}, /*index=5*/f32[192]{0:T(256)}) all-reduce(f32[192]{0:T(256)S(1)} %get-tuple-element.52, f32[3,3,192]{2,1,0:T(4,128)S(1)} %pad_add_fusion.5, ...), channel_id=1, replica_groups=mesh['dp'=8,'chan'=4] {'dp'}, use_global_device_ids=true, to_apply=%region_21.22 | all-reduce | flops 15168 | bytes 121344 | tf_op jit(solution)/shard_map/psum | solution.py:284
  946.7 9.5 all-reduce.23
  960.3 101.3 %all-reduce.34.cloned.1.call-done = (f32[768,3,192]{0,2,1:T(8,128)}, f32[768,192]{0,1:T(8,128)}, f32[768,768]{1,0:T(8,128)}, f32[768,768]{1,0:T(8,128)}, f32[768,768]{1,0:T(8,128)}) async-done(((f32[768,3,192]{0,2,1:T(8,128)}, f32[768,192]{0,1:T(8,128)}, f32[768,768]{1,0:T(8,128)}, f32[768,768]{1,0:T(8,128)}, f32[768,768]{1,0:T(8,128)}), (f32[768,3,192]{0,2,1:T(8,128)}, f32[768,192]{0,1:T(8,128)}, ...) | async-done | bytes 9437200 | tf_op jit(solution)/shard_map/psum | solution.py:284
  1061.6 2.9 copy.499
  (346 shorter events, 177.3 us)
Async XLA Ops:
  7.2 304.0 %copy-start = (bf16[768,768]{1,0:T(8,128)(2,1)S(1)}, bf16[768,768]{1,0:T(8,128)(2,1)}, u32[]{:S(2)}) copy-start(bf16[768,768]{1,0:T(8,128)(2,1)} %param.30) | copy-start | bytes 3538948
  7.2 53.6 %copy-start.105 = (bf16[768,3,192]{0,2,1:T(8,128)(2,1)S(1)}, bf16[768,3,192]{0,2,1:T(8,128)(2,1)}, u32[]{:S(2)}) copy-start(bf16[768,3,192]{0,2,1:T(8,128)(2,1)} %param.19) | copy-start | bytes 2654212
  7.2 53.6 %all-gather.5.cloned.1.call-start = ((), (), s32[]{:S(2)}) async-start(), calls=%async_computation.1 | async-start | bytes 1966080 | tf_op jit(solution)/shard_map/all_gather | solution.py:171
  25.3 196.2 %all-gather.7.cloned.1.call-start = ((), (), s32[]{:S(2)}) async-start(), calls=%async_computation.2 | async-start | bytes 1966080 | tf_op jit(solution)/shard_map/all_gather | solution.py:171
  30.7 32.6 %copy-start.67 = (f32[64,32]{0,1:T(8,128)}, f32[64,32]{0,1:T(8,128)S(1)}, u32[]{:S(2)}) copy-start(f32[64,32]{0,1:T(8,128)S(1)} %get-tuple-element.170) | copy-start | bytes 24580
  32.1 31.2 %copy-start.82 = (f32[1024,1]{0,1:T(1,128)}, f32[1024,1]{0,1:T(1,128)S(1)}, u32[]{:S(2)}) copy-start(f32[1024,1]{0,1:T(1,128)S(1)} %convert_multiply_fusion.2) | copy-start | bytes 12292
  65.1 465.0 %copy-start.4 = (f32[1,1024,3,192]{1,3,2,0:T(8,128)}, f32[1,1024,3,192]{1,3,2,0:T(8,128)S(1)}, u32[]{:S(2)}) copy-start(f32[1,1024,3,192]{1,3,2,0:T(8,128)S(1)} %fusion.2) | copy-start | bytes 7077892
  82.1 4.1 copy-start.37
  82.1 4.1 copy-start.53
  82.1 4.1 copy-start.66
  82.1 4.1 copy-start.80
  82.1 4.1 copy-start.87
  82.1 4.1 copy-start.89
  82.1 4.1 copy-start.91
  90.8 3.9 copy-start.27
  90.8 3.9 copy-start.28
  124.6 13.7 %copy-start.10 = (f32[64,192,32]{1,2,0:T(8,128)}, f32[64,192,32]{1,2,0:T(8,128)S(1)}, u32[]{:S(2)}) copy-start(f32[64,192,32]{1,2,0:T(8,128)S(1)} %fusion.134) | copy-start | bytes 4718596
  128.3 10.0 copy-start.12
  131.7 6.6 copy-start.14
  135.0 3.3 copy-start.16
  138.3 5.6 copy-start.18
  172.2 4.1 copy-start.29
  178.9 4.0 copy-start.84
  178.9 4.0 copy-start.85
  185.4 87.7 %all-gather.9.cloned.1.call-start = ((), (), s32[]{:S(2)}) async-start(), calls=%async_computation.3 | async-start | bytes 1966080 | tf_op jit(solution)/shard_map/all_gather | solution.py:171
  237.6 73.6 %all-gather.11.cloned.1.call-start = ((), (), s32[]{:S(2)}) async-start(), calls=%async_computation.4 | async-start | bytes 1966080 | tf_op jit(solution)/shard_map/all_gather | solution.py:171
  240.8 210.8 %all-reduce.32.cloned.1.call-start = ((), (), s32[]{:S(2)}) async-start(), calls=%async_computation.6 | async-start | bytes 6291456
  273.2 5.0 copy-start.101
  273.2 5.0 copy-start.103
  311.2 6.5 copy-start.104
  331.6 198.6 %reduce-scatter.2.cloned.1.call-start = ((), (), s32[]{:S(2)}) async-start(), calls=%async_computation.5 | async-start | bytes 3932160 | tf_op jit(solution)/shard_map/reduce_scatter | solution.py:174
  465.3 3.6 copy-start.58
  471.2 445.6 %all-reduce.36.cloned.1.call-start = ((), (), s32[]{:S(2)}) async-start(), calls=%async_computation.8 | async-start | bytes 12582912
  481.2 49.0 %copy-start.38 = (f32[1,1024,192]{1,2,0:T(8,128)S(1)}, f32[1,1024,192]{1,2,0:T(8,128)}, u32[]{:S(2)}) copy-start(f32[1,1024,192]{1,2,0:T(8,128)} %copy.221) | copy-start | bytes 2359300
  481.2 49.0 %copy-start.86 = (f32[1024]{0:T(1024)S(1)}, f32[1024]{0:T(1024)}, u32[]{:S(2)}) copy-start(f32[1024]{0:T(1024)} %get-tuple-element.166) | copy-start | bytes 12292
  539.9 6.3 copy-start.2
  564.2 6.6 copy-start.3
  564.2 6.6 copy-start.31
  570.8 6.5 copy-start.30
  583.6 6.6 copy-start.11
  583.6 6.6 copy-start.13
  583.6 6.6 copy-start.15
  583.6 6.6 copy-start.17
  603.2 3.7 copy-start.22
  640.0 5.7 copy-start.34
  657.4 4.1 copy-start.32
  692.4 4.9 copy-start.56
  692.4 369.2 %all-reduce.34.cloned.1.call-start = ((), (), s32[]{:S(2)}) async-start(), calls=%async_computation.7 | async-start | bytes 18874368 | tf_op jit(solution)/shard_map/psum | solution.py:284
  692.4 4.9 copy-start.102
  708.6 3.5 copy-start.83
  709.0 48.6 %copy-start.96 = (f32[192]{0:T(256)S(1)}, f32[192]{0:T(256)}, u32[]{:S(2)}) copy-start(f32[192]{0:T(256)} %get-tuple-element.50) | copy-start | bytes 2308
  709.0 48.6 %copy-start.97 = (f32[192]{0:T(256)S(1)}, f32[192]{0:T(256)}, u32[]{:S(2)}) copy-start(f32[192]{0:T(256)} %get-tuple-element.51) | copy-start | bytes 2308
  709.0 48.6 %copy-start.98 = (f32[192]{0:T(256)S(1)}, f32[192]{0:T(256)}, u32[]{:S(2)}) copy-start(f32[192]{0:T(256)} %get-tuple-element.56) | copy-start | bytes 2308
  709.0 48.6 %copy-start.93 = (f32[3,192]{1,0:T(4,128)S(1)}, f32[3,192]{1,0:T(4,128)}, u32[]{:S(2)}) copy-start(f32[3,192]{1,0:T(4,128)} %get-tuple-element.46) | copy-start | bytes 6916
  709.0 48.6 %copy-start.94 = (f32[3,192]{1,0:T(4,128)S(1)}, f32[3,192]{1,0:T(4,128)}, u32[]{:S(2)}) copy-start(f32[3,192]{1,0:T(4,128)} %get-tuple-element.47) | copy-start | bytes 6916
  709.0 48.6 %copy-start.54 = (f32[1024,64]{0,1:T(8,128)S(1)}, f32[1024,64]{0,1:T(8,128)}, u32[]{:S(2)}) copy-start(f32[1024,64]{0,1:T(8,128)} %get-tuple-element.153) | copy-start | bytes 786436
  709.4 209.2 %copy-start.26 = (bf16[1,1024,192]{1,2,0:T(8,128)(2,1)S(1)}, bf16[1,1024,192]{1,2,0:T(8,128)(2,1)}, u32[]{:S(2)}) copy-start(bf16[1,1024,192]{1,2,0:T(8,128)(2,1)} %param.16) | copy-start | bytes 1179652
  709.4 209.2 %copy-start.71 = (f32[1,1024]{1,0:T(1,128)S(1)}, f32[1,1024]{1,0:T(1,128)}, u32[]{:S(2)}) copy-start(f32[1,1024]{1,0:T(1,128)} %copy-done.70) | copy-start | bytes 12292
  709.4 209.2 %copy-start.73 = (f32[1024]{0:T(1024)S(1)}, f32[1024]{0:T(1024)}, u32[]{:S(2)}) copy-start(f32[1024]{0:T(1024)} %copy-done.72) | copy-start | bytes 12292
  709.4 209.2 %copy-start.95 = (f32[192]{0:T(256)S(1)}, f32[192]{0:T(256)}, u32[]{:S(2)}) copy-start(f32[192]{0:T(256)} %param.18) | copy-start | bytes 2308
  712.2 206.8 %copy-start.99 = (f32[192]{0:T(256)S(1)}, f32[192]{0:T(256)}, u32[]{:S(2)}) copy-start(f32[192]{0:T(256)} %get-tuple-element.48) | copy-start | bytes 2308
  916.8 41.1 %copy-start.9 = (f32[1,1024,192]{1,2,0:T(8,128)S(1)}, f32[1,1024,192]{1,2,0:T(8,128)}, u32[]{:S(2)}) copy-start(f32[1,1024,192]{1,2,0:T(8,128)} %get-tuple-element.158) | copy-start | bytes 2359300
  1061.6 3.8 copy-start.52
  1067.8 3.9 copy-start.1
  (53 other events, 101.7 us)
Sparse Core Ops, SparseCore 0:
  25.5 35.2 all-gather.4
  185.6 35.9 all-gather.6
  237.7 35.3 all-gather.8
  275.2 35.9 all-gather.10
  331.7 119.9 all-reduce.31
  471.3 58.8 reduce-scatter.1
  692.5 224.2 all-reduce.35
  922.2 139.2 all-reduce.33
where the time goes:
time: 1090 us; the launch traced here: 1080 us
  waiting for transfers between devices  536 us (49%)
  matrix products  270 us (25%)
  blocking collectives  117 us (11%)
  local copies, waits for them, and re-layouts  92.1 us (8%)
  other arithmetic  46.6 us (4%)
  between operations  17 us (2%)
    unnamed x10, waiting for transfers between devices  276 us
    all_gather x4, waiting for transfers between devices, gathered(): return lax.all_gather(values, 'chan', axis=2, tiled=True)  119 us
    psum x1, waiting for transfers between devices, local(): lax.psum((w_down_grad, w_gate_grad, w_up_grad, norm2_gain_grad, in_proj_g...  101 us
    psum x1, blocking collectives, local(): lax.psum((wave_in_grad, wave_bias_grad), ('dp', 'chan'))  45.1 us
    psum x4, blocking collectives, moments(): lax.psum((jnp.sum(first_term, axis=-1), jnp.sum(second_term, axis=-1)), '...  43.8 us
    reduce_scatter x1, waiting for transfers between devices, summed(): return lax.psum_scatter(values, 'chan', scatter_dimension=2, tiled=True)  40.2 us
    psum x1, blocking collectives, local(): lax.psum((w_down_grad, w_gate_grad, w_up_grad, norm2_gain_grad, in_proj_g...  27.7 us
    unnamed x227, local copies, waits for them, and re-layouts  25.8 us
  transfers between devices with their start and end apart: 8, of which 8 were waited for; matrix products, arithmetic and copies ran while one was open for 7% of the time, Pallas kernels for 0%

commit v1 on v0

v1 whole, which is shorter than its diff:
```python
import math

import jax
import jax.numpy as jnp
import numpy as np
from jax import lax
from jax.sharding import PartitionSpec as P

highest = lax.Precision.HIGHEST
norm_eps = 1e-05
f32 = jnp.float32
bf16 = jnp.bfloat16


def band_features(seq_len, feat_count):
    bands = (feat_count - 1) // 2
    positions = np.arange(seq_len)
    orders = np.arange(1, bands + 1)
    phases = (orders[:, None] * positions[None, :] % seq_len) * (2.0 * math.pi / seq_len)
    ramp = positions[None, :] / seq_len
    return np.concatenate([ramp, np.sin(phases), np.cos(phases)], axis=0).astype(np.float32)


def wave_matrix(seq_len):
    period = 3 * seq_len // 2
    freq = period // 2
    phase = (np.arange(seq_len)[:, None] * (2 * np.arange(freq)[None, :] + 1)) % (2 * period)
    angle = phase * (math.pi / period)
    return np.concatenate([np.cos(angle), np.sin(angle)], axis=1)


def nn(a, b, precision=None):
    return lax.dot_general(a, b, (((1,), (0,)), ((), ())), precision=precision, preferred_element_type=f32)


def nt(a, b, precision=None):
    return lax.dot_general(a, b, (((1,), (1,)), ((), ())), precision=precision, preferred_element_type=f32)


def tn(a, b, precision=None):
    return lax.dot_general(a, b, (((0,), (0,)), ((), ())), precision=precision, preferred_element_type=f32)


def later(values, steps):
    if steps == 0:
        return values
    return jnp.pad(values, ((0, 0), (steps, 0)))[:, : values.shape[1]]


def sooner(values, steps):
    if steps == 0:
        return values
    return jnp.pad(values, ((0, 0), (0, steps)))[:, steps:]


def local(
    hidden_in, halves, norm1_gain, in_proj, short_taps, cond_taps, filter_in, filter_bias,
    filter_out, decay_rate, out_proj, norm2_gain, w_gate, w_up, w_down, out_grad,
):
    seq_len, own = hidden_in.shape[1], hidden_in.shape[2]
    ways = lax.axis_size("chan")
    width = own * ways
    me = lax.axis_index("chan")
    block = seq_len // ways
    lags = 3 * seq_len // 4
    freq = lags

    pos = jnp.arange(seq_len, dtype=jnp.int32)[None, :]
    half1 = (pos < halves[0, 0]).astype(f32)
    half2 = ((pos >= halves[0, 0]) & (pos < halves[0, 1])).astype(f32)
    valid = half1 + half2

    def gathered(v, axis=0):
        return lax.all_gather(v, "chan", axis=axis, tiled=True)

    x_own = hidden_in[0].T
    grad_own = (out_grad[0].T.astype(f32) * valid).astype(bf16)
    x_full = gathered(x_own).astype(f32)
    grad_full = gathered(grad_own)
    out_full = gathered(out_proj, axis=1)
    gains = gathered(jnp.stack([norm1_gain, norm2_gain], axis=1))
    gain1, gain2 = gains[:, 0:1], gains[:, 1:2]

    def normed(v):
        centre = jnp.mean(v, axis=0, keepdims=True)
        spread = jnp.mean(v * v, axis=0, keepdims=True) - centre * centre
        inverse = lax.rsqrt(spread + norm_eps)
        return (v - centre) * inverse, inverse

    n1, inv1 = normed(x_full)
    norm1_out = (n1 * gain1).astype(bf16)
    in_flat = in_proj.reshape(width, 3 * own)
    proj = tn(in_flat, norm1_out)

    feats = jnp.asarray(band_features(seq_len, filter_in.shape[0]))
    arg = tn(filter_in, feats, highest) + filter_bias[:, None]
    wave = jnp.sin(arg)
    base = tn(filter_out, wave, highest)
    decay = jnp.exp(-decay_rate[:, None] * pos.astype(f32)) * (1.0 / math.sqrt(seq_len))
    ramp = pos.astype(f32)

    table = jnp.asarray(wave_matrix(seq_len).astype(np.float32)).astype(bf16)

    def spectrum(v):
        return nn(v.astype(bf16), table[: v.shape[1]])

    def signal(re, im, length):
        both = jnp.concatenate([re, im], axis=1).astype(bf16)
        return nt(both, table[:length]) * (1.0 / freq)

    parts = [proj[j * own : (j + 1) * own] for j in range(3)]
    taps = [[short_taps[i, j][:, None] for i in range(3)] for j in range(3)]
    query, key, value = [sum(taps[j][i] * later(parts[j], i) for i in range(3)) for j in range(3)]
    ctaps = [cond_taps[i][:, None] for i in range(3)]
    cond = sum(ctaps[i] * later(value, i) for i in range(3))
    squash = jnp.tanh(cond)
    kern = (base + squash) * decay
    source = key * value
    k_hat = spectrum(kern[:, :lags])
    s_hat = [spectrum(source * h) for h in (half1, half2)]
    kr, ki = k_hat[:, :freq], k_hat[:, freq:]
    mixed = 0.0
    for h, s in zip((half1, half2), s_hat):
        sr, si = s[:, :freq], s[:, freq:]
        mixed = mixed + h * signal(kr * sr - ki * si, kr * si + ki * sr, seq_len)
    mixer_own = (query * mixed).astype(bf16)
    mixer_full = gathered(mixer_own)

    resid = x_full + tn(out_full, mixer_full)
    n2, inv2 = normed(resid)
    norm2_out = (n2 * gain2).astype(bf16)
    gate = tn(w_gate, norm2_out)
    up = tn(w_up, norm2_out)
    sig = jax.nn.sigmoid(gate)
    act = gate * sig
    mid = (act * up).astype(bf16)
    hid_grad = nn(w_down, grad_full)
    gate_grad = (hid_grad * up * sig * (1.0 + gate * (1.0 - sig))).astype(bf16)
    up_grad = (hid_grad * act).astype(bf16)
    terms = (nn(w_gate, gate_grad) + nn(w_up, up_grad)).astype(bf16)
    mlp = tn(w_down, mid).astype(bf16)
    w_down_grad = nt(mid, grad_full)
    w_gate_grad = nt(norm2_out, gate_grad)
    w_up_grad = nt(norm2_out, up_grad)

    resid_own = lax.dynamic_slice_in_dim(resid, me * own, own, 0)
    mlp_own = lax.psum_scatter(mlp, "chan", scatter_dimension=0, tiled=True).astype(f32)
    output = (valid * (resid_own + mlp_own)).T[None]

    def tok(v):
        return lax.dynamic_slice_in_dim(v, me * block, block, 1)

    def norm_back(up_g, gain, n, inv):
        q = up_g * gain
        return inv * (q - jnp.mean(q, axis=0, keepdims=True) - n * jnp.mean(q * n, axis=0, keepdims=True))

    terms_own = lax.psum_scatter(terms, "chan", scatter_dimension=1, tiled=True).astype(f32)
    n2_tok, inv2_tok = tok(n2), tok(inv2)
    gain2_part = jnp.sum(terms_own * n2_tok, axis=1)
    resid_grad = tok(grad_full).astype(f32) + norm_back(terms_own, gain2, n2_tok, inv2_tok)
    proj_grad = resid_grad.astype(bf16)
    mixer_grad = nn(out_full, proj_grad).astype(bf16)
    swapped = lax.all_to_all(
        jnp.stack([mixer_grad, proj_grad]), "chan", split_axis=1, concat_axis=2, tiled=True
    )
    mixer_grad, proj_grad_own = swapped[0].astype(f32), swapped[1]
    gain2_own = lax.psum_scatter(gain2_part, "chan", scatter_dimension=0, tiled=True)
    out_proj_grad = nt(mixer_full, proj_grad_own)

    query_grad = mixer_grad * mixed
    mixed_grad = mixer_grad * query
    source_grad = 0.0
    kg_re, kg_im = 0.0, 0.0
    for h, s in zip((half1, half2), s_hat):
        m = spectrum(mixed_grad * h)
        mr, mi = m[:, :freq], m[:, freq:]
        sr, si = s[:, :freq], s[:, freq:]
        source_grad = source_grad + h * signal(kr * mr + ki * mi, kr * mi - ki * mr, seq_len)
        kg_re = kg_re + sr * mr + si * mi
        kg_im = kg_im + sr * mi - si * mr
    kern_grad = signal(kg_re, kg_im, lags)
    kern_grad = jnp.pad(kern_grad, ((0, 0), (0, seq_len - lags)))
    rate_grad = -jnp.sum(kern_grad * kern * ramp, axis=1)
    base_grad = kern_grad * decay
    cond_grad = base_grad * (1.0 - squash * squash)
    ctap_grad = jnp.stack([jnp.sum(cond_grad * later(value, i), axis=1) for i in range(3)])
    key_grad = source_grad * value
    value_grad = source_grad * key + sum(ctaps[i] * sooner(cond_grad, i) for i in range(3))
    branch = (query_grad, key_grad, value_grad)
    stap_grad = jnp.stack(
        [jnp.stack([jnp.sum(branch[j] * later(parts[j], i), axis=1) for j in range(3)]) for i in range(3)]
    )
    low = jnp.concatenate(
        [sum(taps[j][i] * sooner(branch[j], i) for i in range(3)) for j in range(3)], axis=0
    ).astype(bf16)
    fout_grad = nt(wave, base_grad, highest)
    arg_grad = nn(filter_out, base_grad, highest) * jnp.cos(arg)
    fin_grad = nt(feats, arg_grad, highest)
    fbias_grad = jnp.sum(arg_grad, axis=1)

    in_grad = nt(norm1_out, low)
    terms1 = lax.psum_scatter(nn(in_flat, low).astype(bf16), "chan", scatter_dimension=0, tiled=True).astype(f32)
    gain1_own = norm1_gain[:, None]
    n1_own = lax.dynamic_slice_in_dim(n1, me * own, own, 0)
    q1 = terms1 * gain1_own
    m0, m1 = lax.psum((jnp.sum(q1, axis=0), jnp.sum(q1 * n1_own, axis=0)), "chan")
    input_grad = proj_grad_own.astype(f32) + inv1 * (q1 - m0 / width - n1_own * (m1 / width))
    gain1_grad = jnp.sum(terms1 * n1_own, axis=1)
    input_grad = input_grad.T[None]

    big = lax.psum((w_down_grad.astype(bf16), w_gate_grad.astype(bf16), w_up_grad.astype(bf16),
                    in_grad.astype(bf16), out_proj_grad.astype(bf16)), "dp")
    wdg, wgg, wug, ing, opg = [v.astype(f32) for v in big]
    g2, g1, st, ct, fo, rt = lax.psum((gain2_own, gain1_grad, stap_grad, ctap_grad, fout_grad, rate_grad), "dp")
    fi, fb = lax.psum((fin_grad, fbias_grad), ("dp", "chan"))
    return (output, input_grad, g1, ing.reshape(width, 3, own), st, ct, fi, fb, fo, rt, opg, g2, wgg, wug, wdg)


def solution(mesh):
    rows, cols = P("dp", None, "chan"), P(None, "chan")
    in_specs = (
        rows, P("dp", None), P("chan"), P(None, None, "chan"), P(None, None, "chan"), cols, P(), P(),
        cols, P("chan"), cols, P("chan"), cols, cols, P("chan", None), rows,
    )
    out_specs = (
        rows, rows, P("chan"), P(None, None, "chan"), P(None, None, "chan"), cols, P(), P(),
        cols, P("chan"), cols, P("chan"), cols, cols, P("chan", None),
    )
    return jax.shard_map(local, mesh=mesh, in_specs=in_specs, out_specs=out_specs, check_vma=False)
```

time: 1090 us -> 459 us (0.42)
  waiting for transfers between devices: 536 us -> 205 us
  matrix products: 270 us -> 67.6 us
  local copies, waits for them, and re-layouts: 92.1 us -> 22.5 us
  blocking collectives: 117 us -> 96.6 us
    unnamed x10 -> x8, waiting for transfers between devices: 276 us -> 1.47 us
    dot_general x78 -> x35, matrix products: 265 us -> 67.6 us  [the longest x17 26.9 us: nt(): lax.dot_general(a, b, (((1,), (1,)), ((), ())), precision=precision, pref...]
    psum x1, waiting for transfers between devices: 101 us -> 34.9 us  [local(): lax.psum((w_down_grad.astype(bf16), w_gate_grad.astype(bf16), w_up_grad.a...]
    psum x6 -> x3, blocking collectives: 117 us -> 82.7 us  [the longest x1 42.2 us: local(): fi, fb = lax.psum((fin_grad, fbias_grad), ('dp', 'chan'))]
    all_gather x4, waiting for transfers between devices: 119 us -> 87.1 us  [gathered(): return lax.all_gather(v, 'chan', axis=axis, tiled=True)]
    reduce_scatter x1 -> x3, waiting for transfers between devices: 40.2 us -> 63.7 us  [the longest x1 34.2 us: local(): lax.psum_scatter(terms, 'chan', scatter_dimension=1, tiled=True).astype(f32)]
    all_to_all x0 -> x1, waiting for transfers between devices: none -> 18.1 us  [local(): lax.all_to_all(jnp.stack([mixer_grad, proj_grad]), 'chan', split_axis=1,...]
    dot_general x2 -> x0, local copies, waits for them, and re-layouts: 17.3 us -> none  [the longest x1 8.76 us: local(): jnp.einsum('blf,fd->bld', hidden_mid, w_down, preferred_element_type=jnp....]
  transfers between devices with their start and end apart: 8 -> 9, of which waited for: 8 -> 8; matrix products, arithmetic and copies ran while one was open for 7% -> 21% of each run, Pallas kernels for 0% -> 0%
where the time goes in v1:
time: 459 us; the launch traced here: 451 us
  waiting for transfers between devices  205 us (45%)
  blocking collectives  96.6 us (21%)
  matrix products  67.6 us (15%)
  other arithmetic  37.8 us (8%)
  local copies, waits for them, and re-layouts  22.5 us (5%)
  between operations  16.6 us (4%)
  starting transfers between devices  4.91 us (1%)
    all_gather x4, waiting for transfers between devices, gathered(): return lax.all_gather(v, 'chan', axis=axis, tiled=True)  87.1 us
    psum x1, blocking collectives, local(): fi, fb = lax.psum((fin_grad, fbias_grad), ('dp', 'chan'))  42.2 us
    psum x1, waiting for transfers between devices, local(): lax.psum((w_down_grad.astype(bf16), w_gate_grad.astype(bf16), w_up_grad.a...  34.9 us
    reduce_scatter x1, waiting for transfers between devices, local(): lax.psum_scatter(terms, 'chan', scatter_dimension=1, tiled=True).astype(f32)  34.2 us
    reduce_scatter x1, waiting for transfers between devices, local(): lax.psum_scatter(nn(in_flat, low).astype(bf16), 'chan', scatter_dimension...  29.4 us
    dot_general x17, matrix products, nt(): lax.dot_general(a, b, (((1,), (1,)), ((), ())), precision=precision, pref...  26.9 us
    psum x1, blocking collectives, local(): lax.psum((gain2_own, gain1_grad, stap_grad, ctap_grad, fout_grad, rate_gr...  23.7 us
    dot_general x11, matrix products, nn(): lax.dot_general(a, b, (((1,), (0,)), ((), ())), precision=precision, pref...  20.5 us
  transfers between devices with their start and end apart: 9, of which 8 were waited for; matrix products, arithmetic and copies ran while one was open for 21% of the time, Pallas kernels for 0%

profile of v1, /device:TPU:0, one launch (start us, length us, event | category | flops | bytes accessed | tf_op | source)
XLA Modules:
  0.0 451.2 jit_solution(7769585986044772134)
XLA Ops:
  8.7 1.3 fusion.105
  10.7 1.3 fusion.91
  12.0 1.3 fusion.90
  14.7 14.0 %all-gather = f32[4,192,2]{1,2,0:T(2,128)S(1)} all-gather(f32[1,192,2]{1,2,0:T(2,128)S(1)} %maximum_bitcast_fusion.3), channel_id=1, replica_groups=mesh['dp'=8,'chan'=4] {'chan'}, dimensions={0}, use_global_device_ids=true | all-gather | bytes 7680 | tf_op jit(solution)/shard_map/all_gather | solution.py:74
  28.8 1.4 fusion.103
  31.8 2.8 fusion.106
  34.7 14.9 %all-gather.6.cloned.1.call-done = bf16[768,1024]{1,0:T(8,128)(2,1)} async-done(((bf16[192,1024]{1,0:T(8,128)(2,1)}), bf16[768,1024]{1,0:T(8,128)(2,1)}) %all-gather.6.cloned.1.call-update) | async-done | bytes 1572880 | tf_op jit(solution)/shard_map/all_gather | solution.py:74
  49.5 2.0 convert_reduce_fusion
  51.5 2.3 convolution_bitcast_fusion
  54.1 1.2 copy-done.24
  55.4 1.2 multiply_add_fusion
  56.6 1.8 copy-done.2
  58.4 0.8 fusion.73
  59.4 0.9 fusion.21
  60.3 1.0 copy-done.26
  63.8 0.8 fusion.74
  65.7 0.8 copy-done.6
  67.3 2.1 multiply_convert_fusion.4
  69.5 1.3 fusion.92
  71.9 8.5 %all-gather.10.cloned.1.call-done = bf16[768,768]{0,1:T(8,128)(2,1)} async-done(((bf16[768,192]{0,1:T(8,128)(2,1)}), bf16[768,768]{0,1:T(8,128)(2,1)}) %all-gather.10.cloned.1.call-update) | async-done | bytes 1179664 | tf_op jit(solution)/shard_map/all_gather | solution.py:74
  80.4 38.4 %all-gather.8.cloned.1.call-done = bf16[768,1024]{1,0:T(8,128)(2,1)} async-done(((bf16[192,1024]{1,0:T(8,128)(2,1)}), bf16[768,1024]{1,0:T(8,128)(2,1)}) %all-gather.8.cloned.1.call-update) | async-done | bytes 1572880 | tf_op jit(solution)/shard_map/all_gather | solution.py:74
  118.8 3.7 fusion.99
  122.5 2.1 multiply_convert_fusion
  125.2 3.1 fusion.108
  128.3 3.2 fusion.109
  131.5 25.3 %all-gather.12.cloned.1.call-done = bf16[768,1024]{1,0:T(8,128)(2,1)} async-done(((bf16[192,1024]{1,0:T(8,128)(2,1)}), bf16[768,1024]{1,0:T(8,128)(2,1)}) %all-gather.12.cloned.1.call-update) | async-done | bytes 1572880 | tf_op jit(solution)/shard_map/all_gather | solution.py:74
  156.8 6.5 %fusion.5 = (bf16[768,1024]{0,1:T(8,128)(2,1)S(1)}, bf16[768,1024]{0,1:T(8,128)(2,1)S(1)}, bf16[768,1024]{0,1:T(8,128)(2,1)}) fusion(f32[1024,768]{1,0:T(8,128)} %fusion.108, f32[1024,768]{1,0:T(8,128)} %fusion.109, bf16[768,1024]{1,0:T(8,128)(2,1)} %all-gather.12.cloned.1.call-done, bf16[768,768]{1,0:T(8,128)(2,1)S(1)} %copy-done), kind=kOutput, calls=%fused_computation.11 | convolution fusion | flops 1219756032 | bytes 13762560 | tf_op jit(solution)/shard_map/dot_general | solution.py:33
  163.3 1.4 fusion.110
  165.5 2.6 fusion.12
  168.1 34.2 %reduce-scatter.6.cloned.1.call-done = bf16[768,256]{1,0:T(8,128)(2,1)} async-done(((bf16[768,1024]{1,0:T(8,128)(2,1)}), bf16[768,256]{1,0:T(8,128)(2,1)}) %reduce-scatter.6.cloned.1.call-update) | async-done | bytes 393232 | tf_op jit(solution)/shard_map/reduce_scatter | solution.py:157
  202.3 2.3 fusion.57
  204.7 1.6 fusion.55
  207.0 1.7 copy.57
  208.7 4.2 all-to-all-start
  212.9 4.0 fusion.11
  217.2 4.4 convolution_convert_fusion.3
  221.7 2.4 convolution_convert_fusion.4
  224.1 2.4 convolution_convert_fusion.2
  226.5 18.1 %all-to-all-done = bf16[2,768,256]{2,0,1:T(2,128)(2,1)} async-done(((bf16[2,768,256]{2,0,1:T(2,128)(2,1)}), bf16[2,768,256]{2,0,1:T(2,128)(2,1)}, u32[]{:S(2)}, u32[]{:S(2)}) %all-to-all-start) | async-done | bytes 786464 | tf_op jit(solution)/shard_map/all_to_all | solution.py:163
  244.6 1.8 copy.68
  246.9 1.5 copy-done.3
  248.4 0.8 fusion.75
  249.3 0.8 fusion.76
  253.7 1.8 multiply_reduce_fusion.3
  259.9 4.9 %multiply_reduce_fusion.12 = (f32[192]{0:T(256)}, f32[192]{0:T(256)}, f32[192]{0:T(256)}, f32[192]{0:T(256)}, f32[192]{0:T(256)}, /*index=5*/f32[192]{0:T(256)},...) fusion(f32[576,1024]{1,0:T(8,128)} %copy-done.24, ...), kind=kOutput, calls=%fused_computation.134 | convolution fusion | flops 308476224 | bytes 16528384 | tf_op jit(solution)/shard_map/dot_general | solution.py:37
  267.0 1.4 convolution_convert_fusion.7
  268.4 2.1 convolution_convert_fusion.5
  270.6 3.9 fusion.13
  276.3 2.2 fusion
  278.7 2.7 multiply_bitcast_fusion
  281.4 1.6 fusion.107
  283.4 42.2 %all-reduce.18 = (f32[33,64]{1,0:T(8,128)}, f32[64]{0:T(128)}) all-reduce(f32[33,64]{1,0:T(8,128)S(1)} %fusion.111, f32[64]{0:T(128)S(1)} %get-tuple-element.100), channel_id=1, replica_groups=mesh['dp'=8,'chan'=4] {'dp','chan'}, use_global_device_ids=true, to_apply=%region_30.31 | all-reduce | flops 2176 | bytes 17408 | tf_op jit(solution)/shard_map/psum | solution.py:215
  325.8 1.0 fusion.65
  326.8 34.9 %all-reduce.24.cloned.1.call-done = (bf16[768,3,192]{0,2,1:T(8,128)(2,1)}, bf16[768,192]{0,1:T(8,128)(2,1)}, bf16[768,768]{1,0:T(8,128)(2,1)}, bf16[768,768]{1,0:T(8,128)(2,1)}, bf16[768,768]{1,0:T(8,128)(2,1)}) async-done(((bf16[768,3,192]{0,2,1:T(8,128)(2,1)}, bf16[768,192]{0,1:T(8,128)(2,1)}, bf16[768,768]{1,0:T(8,128)(2,1)}, bf16[768,768]{1,0:T(8,128)(2,1)}, bf16[768,768]{1,0:T(8,128)(2,1)}), ...) | async-done | bytes 4718608 | tf_op jit(solution)/shard_map/psum | solution.py:211
  361.7 2.9 convert_element_type.234
  364.6 1.6 convert_element_type.236
  366.3 1.6 convert_element_type.238
  367.9 1.3 reshape.163
  369.3 0.9 convert_element_type.232
  370.1 29.4 %reduce-scatter.8.cloned.1.call-done = bf16[192,1024]{1,0:T(8,128)(2,1)} async-done(((bf16[768,1024]{1,0:T(8,128)(2,1)}), bf16[192,1024]{1,0:T(8,128)(2,1)}) %reduce-scatter.8.cloned.1.call-update) | async-done | bytes 393232 | tf_op jit(solution)/shard_map/reduce_scatter | solution.py:202
  399.6 1.6 fusion.63
  401.1 16.7 %all-reduce.20 = (f32[1024]{0:T(1024)S(1)}, f32[1024]{0:T(1024)S(1)}, f32[768]{0:T(1024)S(1)}) all-reduce(f32[1024]{0:T(1024)S(1)} %get-tuple-element.18, f32[1024]{0:T(1024)S(1)} %get-tuple-element.42, f32[768]{0:T(1024)S(1)} %copy-done.53), channel_id=1, replica_groups=mesh['dp'=8,'chan'=4] {'chan'}, use_global_device_ids=true, to_apply=%region_12.13 | all-reduce | flops 2816 | bytes 22528 | tf_op jit(solution)/shard_map/psum | solution.py:206
  417.9 23.7 %all-reduce.19 = (f32[192]{0:T(256)}, f32[3,3,192]{2,1,0:T(4,128)}, f32[3,192]{1,0:T(4,128)}, f32[64,192]{1,0:T(8,128)}, f32[192]{0:T(256)}, /*index=5*/f32[192]{0:T(256)}) all-reduce(f32[192]{0:T(256)S(1)} %get-tuple-element.17, f32[3,3,192]{2,1,0:T(4,128)S(1)} %pad_maximum_fusion.4, ...), channel_id=1, replica_groups=mesh['dp'=8,'chan'=4] {'dp'}, use_global_device_ids=true, to_apply=%region_14.15 | all-reduce | flops 15168 | bytes 121344 | tf_op jit(solution)/shard_map/psum | solution.py:214
  441.7 2.3 fusion.61
  (282 shorter events, 25.4 us)
Async XLA Ops:
  7.2 149.6 %copy-start = (bf16[768,768]{1,0:T(8,128)(2,1)S(1)}, bf16[768,768]{1,0:T(8,128)(2,1)}, u32[]{:S(2)}) copy-start(bf16[768,768]{1,0:T(8,128)(2,1)} %param.32) | copy-start | bytes 3538948
  7.2 42.3 %all-gather.6.cloned.1.call-start = ((), (), s32[]{:S(2)}) async-start(), calls=%async_computation.4 | async-start | bytes 1966080 | tf_op jit(solution)/shard_map/all_gather | solution.py:74
  7.9 72.5 %all-gather.10.cloned.1.call-start = ((), (), s32[]{:S(2)}) async-start(), calls=%async_computation.6 | async-start | bytes 1474560 | tf_op jit(solution)/shard_map/all_gather | solution.py:74
  8.7 110.1 %all-gather.8.cloned.1.call-start = ((), (), s32[]{:S(2)}) async-start(), calls=%async_computation.5 | async-start | bytes 1966080 | tf_op jit(solution)/shard_map/all_gather | solution.py:74
  8.7 50.6 %copy-start.54 = (f32[1024]{0:T(1024)}, f32[1024]{0:T(1024)S(1)}, u32[]{:S(2)}) copy-start(f32[1024]{0:T(1024)S(1)} %iota_convert_fusion) | copy-start | bytes 12292
  10.7 45.9 %copy-start.49 = (f32[1024]{0:T(1024)}, f32[1024]{0:T(1024)S(1)}, u32[]{:S(2)}) copy-start(f32[1024]{0:T(1024)S(1)} %fusion.88) | copy-start | bytes 12292
  14.0 53.3 %copy-start.47 = (f32[1024]{0:T(1024)}, f32[1024]{0:T(1024)S(1)}, u32[]{:S(2)}) copy-start(f32[1024]{0:T(1024)S(1)} %fusion.87) | copy-start | bytes 12292
  28.8 25.1 %copy-start.90 = (f32[768]{0:T(1024)}, f32[768]{0:T(1024)S(1)}, u32[]{:S(2)}) copy-start(f32[768]{0:T(1024)S(1)} %get-tuple-element.44) | copy-start | bytes 9220
  30.3 25.1 %copy-start.59 = (f32[1,1,192]{2,1,0:T(1,128)}, f32[1,1,192]{2,1,0:T(1,128)S(1)}, u32[]{:S(2)}) copy-start(f32[1,1,192]{2,1,0:T(1,128)S(1)} %get-tuple-element.80) | copy-start | bytes 2308
  30.3 25.1 %copy-start.61 = (f32[1,1,192]{2,1,0:T(1,128)}, f32[1,1,192]{2,1,0:T(1,128)S(1)}, u32[]{:S(2)}) copy-start(f32[1,1,192]{2,1,0:T(1,128)S(1)} %get-tuple-element.81) | copy-start | bytes 2308
  30.3 25.1 %copy-start.63 = (f32[1,1,192]{2,1,0:T(1,128)}, f32[1,1,192]{2,1,0:T(1,128)S(1)}, u32[]{:S(2)}) copy-start(f32[1,1,192]{2,1,0:T(1,128)S(1)} %get-tuple-element.82) | copy-start | bytes 2308
  30.3 25.1 %copy-start.65 = (f32[1,1,192]{2,1,0:T(1,128)}, f32[1,1,192]{2,1,0:T(1,128)S(1)}, u32[]{:S(2)}) copy-start(f32[1,1,192]{2,1,0:T(1,128)S(1)} %get-tuple-element.79) | copy-start | bytes 2308
  30.3 25.1 %copy-start.67 = (f32[1,1,192]{2,1,0:T(1,128)}, f32[1,1,192]{2,1,0:T(1,128)S(1)}, u32[]{:S(2)}) copy-start(f32[1,1,192]{2,1,0:T(1,128)S(1)} %get-tuple-element.85) | copy-start | bytes 2308
  30.3 25.1 %copy-start.69 = (f32[1,1,192]{2,1,0:T(1,128)}, f32[1,1,192]{2,1,0:T(1,128)S(1)}, u32[]{:S(2)}) copy-start(f32[1,1,192]{2,1,0:T(1,128)S(1)} %get-tuple-element.86) | copy-start | bytes 2308
  31.1 28.2 %copy-start.71 = (f32[1,192]{1,0:T(1,128)}, f32[1,192]{1,0:T(1,128)S(1)}, u32[]{:S(2)}) copy-start(f32[1,192]{1,0:T(1,128)S(1)} %get-tuple-element.89) | copy-start | bytes 2308
  31.1 28.2 %copy-start.73 = (f32[1,192]{1,0:T(1,128)}, f32[1,192]{1,0:T(1,128)S(1)}, u32[]{:S(2)}) copy-start(f32[1,192]{1,0:T(1,128)S(1)} %get-tuple-element.90) | copy-start | bytes 2308
  31.1 28.2 %copy-start.75 = (f32[1,192]{1,0:T(1,128)}, f32[1,192]{1,0:T(1,128)S(1)}, u32[]{:S(2)}) copy-start(f32[1,192]{1,0:T(1,128)S(1)} %get-tuple-element.91) | copy-start | bytes 2308
  31.8 27.5 %copy-start.86 = (f32[192]{0:T(256)}, f32[192]{0:T(256)S(1)}, u32[]{:S(2)}) copy-start(f32[192]{0:T(256)S(1)} %neg.10) | copy-start | bytes 2308
  34.7 24.7 %copy-start.43 = (f32[1024,64]{0,1:T(8,128)}, f32[1024,64]{0,1:T(8,128)S(1)}, u32[]{:S(2)}) copy-start(f32[1024,64]{0,1:T(8,128)S(1)} %get-tuple-element.96) | copy-start | bytes 786436
  55.3 12.0 %copy-start.19 = (f32[192,1024]{1,0:T(8,128)}, f32[192,1024]{1,0:T(8,128)S(1)}, u32[]{:S(2)}) copy-start(f32[192,1024]{1,0:T(8,128)S(1)} %get-tuple-element.72) | copy-start | bytes 2359300
  55.4 3.0 copy-start.2
  56.6 7.2 %copy-start.8 = (f32[192,1024]{1,0:T(8,128)}, f32[192,1024]{1,0:T(8,128)S(1)}, u32[]{:S(2)}) copy-start(f32[192,1024]{1,0:T(8,128)S(1)} %get-tuple-element.102) | copy-start | bytes 2359300
  59.3 8.0 %copy-start.12 = (f32[192,1536]{1,0:T(8,128)}, f32[192,1536]{1,0:T(8,128)S(1)}, u32[]{:S(2)}) copy-start(f32[192,1536]{1,0:T(8,128)S(1)} %fusion.73) | copy-start | bytes 3538948
  67.3 3.4 copy-start.41
  69.4 87.4 %all-gather.12.cloned.1.call-start = ((), (), s32[]{:S(2)}) async-start(), calls=%async_computation.8 | async-start | bytes 1966080 | tf_op jit(solution)/shard_map/all_gather | solution.py:74
  71.6 130.7 %reduce-scatter.6.cloned.1.call-start = ((), (), s32[]{:S(2)}) async-start(), calls=%async_computation.9 | async-start | bytes 1966080 | tf_op jit(solution)/shard_map/reduce_scatter | solution.py:157
  125.2 3.2 copy-start.32
  125.2 3.2 copy-start.104
  156.8 6.5 %copy-start.103 = (bf16[768,768]{1,0:T(8,128)(2,1)S(1)}, bf16[768,768]{1,0:T(8,128)(2,1)}, u32[]{:S(2)}) copy-start(bf16[768,768]{1,0:T(8,128)(2,1)} %param.30) | copy-start | bytes 3538948
  202.3 4.0 copy-start.36
  208.7 36.0 %all-to-all-start = ((bf16[2,768,256]{2,0,1:T(2,128)(2,1)}), bf16[2,768,256]{2,0,1:T(2,128)(2,1)}, u32[]{:S(2)}, u32[]{:S(2)}) async-start(bf16[2,768,256]{2,0,1:T(2,128)(2,1)} %copy.57), calls=%async_computation.2 | async-start | bytes 1572864 | tf_op jit(solution)/shard_map/all_to_all | solution.py:163
  212.9 65.8 %reduce-scatter.4.cloned.1.call-start = ((), (), s32[]{:S(2)}) async-start(), calls=%async_computation.7 | async-start | bytes 1966080 | tf_op jit(solution)/shard_map/reduce_scatter | solution.py:147
  217.0 144.7 %all-reduce.24.cloned.1.call-start = ((), (), s32[]{:S(2)}) async-start(), calls=%async_computation.11 | async-start | bytes 9437184 | tf_op jit(solution)/shard_map/psum | solution.py:211
  217.2 4.5 copy-start.33
  217.2 4.4 copy-start.110
  259.8 5.0 %copy-start.78 = (f32[1,1,192]{2,1,0:T(1,128)S(1)}, f32[1,1,192]{2,1,0:T(1,128)}, u32[]{:S(2)}) copy-start(f32[1,1,192]{2,1,0:T(1,128)} %get-tuple-element.78) | copy-start | bytes 2308
  259.8 5.0 %copy-start.80 = (f32[1,1,192]{2,1,0:T(1,128)S(1)}, f32[1,1,192]{2,1,0:T(1,128)}, u32[]{:S(2)}) copy-start(f32[1,1,192]{2,1,0:T(1,128)} %get-tuple-element.83) | copy-start | bytes 2308
  259.8 5.0 %copy-start.82 = (f32[1,1,192]{2,1,0:T(1,128)S(1)}, f32[1,1,192]{2,1,0:T(1,128)}, u32[]{:S(2)}) copy-start(f32[1,1,192]{2,1,0:T(1,128)} %get-tuple-element.84) | copy-start | bytes 2308
  259.8 5.8 %copy-start.66 = (f32[1,1,192]{2,1,0:T(1,128)S(1)}, f32[1,1,192]{2,1,0:T(1,128)}, u32[]{:S(2)}) copy-start(f32[1,1,192]{2,1,0:T(1,128)} %copy-done.65) | copy-start | bytes 2308
  259.9 5.8 %copy-start.68 = (f32[1,1,192]{2,1,0:T(1,128)S(1)}, f32[1,1,192]{2,1,0:T(1,128)}, u32[]{:S(2)}) copy-start(f32[1,1,192]{2,1,0:T(1,128)} %copy-done.67) | copy-start | bytes 2308
  259.9 5.8 %copy-start.70 = (f32[1,1,192]{2,1,0:T(1,128)S(1)}, f32[1,1,192]{2,1,0:T(1,128)}, u32[]{:S(2)}) copy-start(f32[1,1,192]{2,1,0:T(1,128)} %copy-done.69) | copy-start | bytes 2308
  270.5 129.0 %reduce-scatter.8.cloned.1.call-start = ((), (), s32[]{:S(2)}) async-start(), calls=%async_computation.10 | async-start | bytes 1966080 | tf_op jit(solution)/shard_map/reduce_scatter | solution.py:202
  278.5 2.9 copy-start.45
  278.5 2.9 copy-start.88
  278.5 2.9 copy-start.107
  278.5 4.5 %copy-start.40 = (f32[33,1024]{1,0:T(8,128)S(1)}, f32[33,1024]{1,0:T(8,128)}, u32[]{:S(2)}) copy-start(f32[33,1024]{1,0:T(8,128)} %constant.44.clone) | copy-start | bytes 405508
  278.5 47.1 %copy-start.83 = (f32[192]{0:T(256)S(1)}, f32[192]{0:T(256)}, u32[]{:S(2)}) copy-start(f32[192]{0:T(256)} %get-tuple-element.24) | copy-start | bytes 2308
  278.5 47.1 %copy-start.84 = (f32[192]{0:T(256)S(1)}, f32[192]{0:T(256)}, u32[]{:S(2)}) copy-start(f32[192]{0:T(256)} %get-tuple-element.25) | copy-start | bytes 2308
  278.6 47.1 %copy-start.85 = (f32[192]{0:T(256)S(1)}, f32[192]{0:T(256)}, u32[]{:S(2)}) copy-start(f32[192]{0:T(256)} %get-tuple-element.26) | copy-start | bytes 2308
  278.6 47.1 %copy-start.98 = (f32[192]{0:T(256)S(1)}, f32[192]{0:T(256)}, u32[]{:S(2)}) copy-start(f32[192]{0:T(256)} %get-tuple-element.21) | copy-start | bytes 2308
  278.6 47.1 %copy-start.99 = (f32[192]{0:T(256)S(1)}, f32[192]{0:T(256)}, u32[]{:S(2)}) copy-start(f32[192]{0:T(256)} %get-tuple-element.22) | copy-start | bytes 2308
  278.6 47.1 %copy-start.100 = (f32[192]{0:T(256)S(1)}, f32[192]{0:T(256)}, u32[]{:S(2)}) copy-start(f32[192]{0:T(256)} %get-tuple-element.23) | copy-start | bytes 2308
  278.6 47.1 %copy-start.95 = (f32[192]{0:T(256)S(1)}, f32[192]{0:T(256)}, u32[]{:S(2)}) copy-start(f32[192]{0:T(256)} %get-tuple-element.36) | copy-start | bytes 2308
  278.6 47.1 %copy-start.96 = (f32[192]{0:T(256)S(1)}, f32[192]{0:T(256)}, u32[]{:S(2)}) copy-start(f32[192]{0:T(256)} %get-tuple-element.38) | copy-start | bytes 2308
  278.6 47.1 %copy-start.97 = (f32[192]{0:T(256)S(1)}, f32[192]{0:T(256)}, u32[]{:S(2)}) copy-start(f32[192]{0:T(256)} %get-tuple-element.40) | copy-start | bytes 2308
  278.6 47.1 %copy-start.92 = (f32[192]{0:T(256)S(1)}, f32[192]{0:T(256)}, u32[]{:S(2)}) copy-start(f32[192]{0:T(256)} %get-tuple-element.35) | copy-start | bytes 2308
  278.6 47.1 %copy-start.93 = (f32[192]{0:T(256)S(1)}, f32[192]{0:T(256)}, u32[]{:S(2)}) copy-start(f32[192]{0:T(256)} %get-tuple-element.37) | copy-start | bytes 2308
  278.6 47.1 %copy-start.94 = (f32[192]{0:T(256)S(1)}, f32[192]{0:T(256)}, u32[]{:S(2)}) copy-start(f32[192]{0:T(256)} %get-tuple-element.39) | copy-start | bytes 2308
  278.7 47.1 %copy-start.44 = (f32[1024,64]{0,1:T(8,128)S(1)}, f32[1024,64]{0,1:T(8,128)}, u32[]{:S(2)}) copy-start(f32[1024,64]{0,1:T(8,128)} %copy-done.43) | copy-start | bytes 786436
  361.7 2.9 copy-start.35
  367.9 31.7 %copy-start.58 = (f32[192]{0:T(256)S(1)}, f32[192]{0:T(256)}, u32[]{:S(2)}) copy-start(f32[192]{0:T(256)} %param.20) | copy-start | bytes 2308
  369.2 31.9 %copy-start.53 = (f32[768]{0:T(1024)S(1)}, f32[768]{0:T(1024)}, u32[]{:S(2)}) copy-start(f32[768]{0:T(1024)} %get-tuple-element.15) | copy-start | bytes 9220
  369.3 74.7 %copy-start.1 = (bf16[768,768]{1,0:T(8,128)(2,1)S(1)}, bf16[768,768]{1,0:T(8,128)(2,1)}, u32[]{:S(2)}) copy-start(bf16[768,768]{1,0:T(8,128)(2,1)} %param.32) | copy-start | bytes 3538948
  399.6 42.1 %copy-start.31 = (bf16[192,1024]{1,0:T(8,128)(2,1)S(1)}, bf16[192,1024]{1,0:T(8,128)(2,1)}, u32[]{:S(2)}) copy-start(bf16[192,1024]{1,0:T(8,128)(2,1)} %reduce-scatter.8.cloned.1.call-done) | copy-start | bytes 1179652
  (58 other events, 97.3 us)
Sparse Core Ops, SparseCore 0:
  9.6 39.8 all-gather.5
  51.1 29.2 all-gather.9
  82.6 36.1 all-gather.7
  120.8 35.9 all-gather.11
  168.2 34.1 reduce-scatter.5
  217.1 39.8 reduce-scatter.3
  270.7 90.9 all-reduce.23
  364.1 35.4 reduce-scatter.7

commit v2 on v1

--- a/solution.py
+++ b/solution.py
@@ -1,9 +1,12 @@
+import functools
 import math
 
 import jax
 import jax.numpy as jnp
 import numpy as np
 from jax import lax
+from jax.experimental import pallas as pl
+from jax.experimental.pallas import tpu as pltpu
 from jax.sharding import PartitionSpec as P
 
 highest = lax.Precision.HIGHEST
@@ -52,6 +55,322 @@
         return values
     return jnp.pad(values, ((0, 0), (0, steps)))[:, steps:]
 
+
+MESH = pl.DeviceIdType.MESH
+lane_tile = 256
+row_tile = 16
+
+
+def flipped(index, bit):
+    return index + (1 << bit) * (1 - 2 * ((index // (1 << bit)) % 2))
+
+
+class Line:
+    def __init__(self, view, send_sem, recv_sem, at, ways):
+        self.view, self.send_sem, self.recv_sem, self.at, self.ways = view, send_sem, recv_sem, at, ways
+
+    def copy(self, way, hop, part, shard):
+        ref = self.view(shard, part)
+        step = 1 - 2 * way
+        return pltpu.make_async_remote_copy(
+            src_ref=ref, dst_ref=ref, send_sem=self.send_sem.at[way, hop, part],
+            recv_sem=self.recv_sem.at[way, hop, part],
+            device_id={"chan": (self.at + step + self.ways) % self.ways}, device_id_type=MESH,
+        )
+
+    def sends(self, way, hop):
+        if way == 0:
+            return jnp.logical_and(self.at >= hop, self.at < self.ways - 1)
+        return jnp.logical_and(self.at + hop <= self.ways - 1, self.at > 0)
+
+    def gets(self, way, hop):
+        if way == 0:
+            return self.at >= hop + 1
+        return self.at + hop + 1 <= self.ways - 1
+
+    def start(self, way, hop, part):
+        @pl.when(self.sends(way, hop))
+        def _():
+            self.copy(way, hop, part, self.at - hop * (1 - 2 * way)).start()
+
+    def wait_recv(self, way, hop, part):
+        @pl.when(self.gets(way, hop))
+        def _():
+            self.copy(way, hop, part, self.at - (hop + 1) * (1 - 2 * way)).wait_recv()
+
+    def wait_send(self, way, hop, part):
+        @pl.when(self.sends(way, hop))
+        def _():
+            self.copy(way, hop, part, self.at - hop * (1 - 2 * way)).wait_send()
+
+    def relay(self, hop, part):
+        for way in (0, 1):
+            self.wait_recv(way, hop - 1, part)
+            self.start(way, hop, part)
+
+
+def front_kernel(
+    cfg, x_hbm, g_hbm, mask_ref, cols_ref, gain_ref, fin_ref, in_hbm, outf_hbm, feat_ref, tab_hbm, inv_hbm,
+    xf_out, gf_out, outt_out, proj_out, mixo_out, qkv_out, squash_out, kern_out, mixed_out, hat_out, arg_out,
+    xf, gf, outt, proj, mixf, qkv, squash, kern, mixed, hat, arg,
+    in_t, tab, inv, n1o, pieces, gains, gaincol, sig, prod,
+    load_sem, line_send, line_recv, piece_send, piece_recv, gain_send, gain_recv, save_sem,
+):
+    ways, rows, seq, own, width, bits = (cfg[k] for k in ("ways", "rows", "seq", "own", "width", "bits"))
+    lags = 3 * seq // 4
+    freq = lags
+    parts = seq // lane_tile
+    z = lax.axis_index("chan")
+    r = lax.axis_index("dp")
+    group = r % (1 << bits)
+    span = pl.ds(pl.multiple_of(z * own, row_tile), own)
+
+    def load(index, src, dst):
+        copy = pltpu.make_async_copy(src, dst, load_sem.at[index])
+        copy.start()
+        return copy
+
+    own_rows = pieces.shape[2]
+    loads = [
+        load(0, x_hbm, xf.at[span]),
+        load(1, g_hbm, gf.at[span]),
+        load(2, outf_hbm.at[pl.ds(pl.multiple_of(group * own_rows, row_tile), own_rows)], pieces.at[group, z]),
+        load(3, in_hbm, in_t),
+        load(4, tab_hbm, tab),
+        load(5, inv_hbm, inv),
+    ]
+    barrier = pltpu.get_barrier_semaphore()
+    peers = [{"chan": (z + s) % ways} for s in range(1, ways)] + [{"dp": flipped(r, b)} for b in range(bits)]
+    for peer in peers:
+        pl.semaphore_signal(barrier, inc=1, device_id=peer, device_id_type=MESH)
+    pl.semaphore_wait(barrier, len(peers))
+
+    def cut(buf):
+        def view(shard, part):
+            return buf.at[
+                pl.ds(pl.multiple_of(shard * own, row_tile), own),
+                pl.ds(pl.multiple_of(part * lane_tile, lane_tile), lane_tile),
+            ]
+        return view
+
+    in_line = Line(cut(xf), line_send.at[0], line_recv.at[0], z, ways)
+    g_line = Line(cut(gf), line_send.at[1], line_recv.at[1], z, ways)
+
+    loads[0].wait()
+
+    def each_part(fn):
+        def run(part, carry):
+            fn(part)
+            return carry
+        lax.fori_loop(0, parts, run, 0)
+
+    def send_own(line):
+        def run(part):
+            for way in (0, 1):
+                line.start(way, 0, part)
+        each_part(run)
+
+    def direct(buf_view, send, recv, s, dst_z, src_z):
+        return pltpu.make_async_remote_copy(
+            src_ref=buf_view(src_z), dst_ref=buf_view(src_z), send_sem=send.at[s], recv_sem=recv.at[s],
+            device_id={"chan": dst_z}, device_id_type=MESH,
+        )
+
+    gains[z] = gain_ref[...]
+    loads[2].wait()
+    for s in range(1, ways):
+        direct(lambda at: gains.at[at], gain_send, gain_recv, s, (z + s) % ways, z).start()
+        direct(lambda at: pieces.at[group, at], piece_send, piece_recv, s, (z + s) % ways, z).start()
+    send_own(in_line)
+
+    arg[...] = nn(fin_ref[...], feat_ref[...], highest)
+    base_wave = jnp.sin(arg[...])
+    kern[...] = nn(cols_ref[:, 64:128], base_wave, highest)
+
+    for s in range(1, ways):
+        direct(lambda at: gains.at[at], gain_send, gain_recv, s, (z + s) % ways, (z + ways - s) % ways).wait_recv()
+        direct(lambda at: pieces.at[group, at], piece_send, piece_recv, s, (z + s) % ways, (z + ways - s) % ways).wait_recv()
+
+    held = [group]
+    slot = ways
+    started = []
+    for bit in reversed(range(bits)):
+        batch = []
+        for piece in held:
+            def make(which, slot=slot, bit=bit):
+                return pltpu.make_async_remote_copy(
+                    src_ref=pieces.at[which], dst_ref=pieces.at[which], send_sem=piece_send.at[slot],
+                    recv_sem=piece_recv.at[slot], device_id={"dp": flipped(r, bit)}, device_id_type=MESH,
+                )
+            make(piece).start()
+            batch.append((make, piece))
+            slot += 1
+        started.append((bit, batch))
+        if bit == bits - 1:
+            eye = lax.broadcasted_iota(jnp.int32, (own, gains.shape[2]), 0) == lax.broadcasted_iota(
+                jnp.int32, (own, gains.shape[2]), 1)
+            for s in range(ways):
+                for which in range(2):
+                    row = gains[s, which : which + 1, :]
+                    gaincol[s * own : (s + 1) * own, which : which + 1] = jnp.sum(
+                        jnp.where(eye, row, 0.0), axis=1, keepdims=True)
+        for make, piece in batch:
+            make(flipped(piece, bit)).wait_recv()
+        held = held + [flipped(piece, bit) for piece in held]
+
+    loads[1].wait()
+    loads[3].wait()
+
+    def norm_part(part):
+        for hop in range(1, ways - 1):
+            in_line.relay(hop, part)
+        for way in (0, 1):
+            in_line.wait_recv(way, ways - 2, part)
+        cols = pl.ds(pl.multiple_of(part * lane_tile, lane_tile), lane_tile)
+        values = xf[:, cols].astype(f32)
+        centre = jnp.sum(values, axis=0, keepdims=True) * (1.0 / width)
+        spread = jnp.sum(values * values, axis=0, keepdims=True) * (1.0 / width) - centre * centre
+        inverse = lax.rsqrt(spread + norm_eps)
+        low = ((values - centre) * inverse * gaincol[:, 0:1]).astype(bf16)
+        n1o[:, cols] = low
+        proj[:, cols] = nn(in_t[...], low)
+
+    each_part(norm_part)
+    send_own(g_line)
+    loads[4].wait()
+    loads[5].wait()
+
+    grain = math.gcd(own_rows, own)
+    for s in range(ways):
+        for row in range(0, own * width // 128, grain):
+            piece, inner = divmod(row, own_rows)
+            block, place = divmod(row, own)
+            outt[s * own + place : s * own + place + grain, 128 * block : 128 * block + 128] = pieces[
+                piece, s, inner : inner + grain, :]
+
+    lane = lax.broadcasted_iota(jnp.int32, (row_tile, seq), 1)
+    place = lane.astype(f32)
+    half1, half2 = mask_ref[0:1, :], mask_ref[1:2, :]
+
+    def back(values, steps):
+        if steps == 0:
+            return values
+        return jnp.where(lane >= steps, pltpu.roll(values, steps, 1), 0.0)
+
+    def mix_rows(i, carry):
+        here = pl.ds(pl.multiple_of(i * row_tile, row_tile), row_tile)
+
+        def at(j):
+            return pl.ds(pl.multiple_of(j * own + i * row_tile, row_tile), row_tile)
+
+        tap = cols_ref[here, :]
+        outs = []
+        for j in range(3):
+            part = proj[at(j), :]
+            total = sum(tap[:, 3 * k + j : 3 * k + j + 1] * back(part, k) for k in range(3))
+            qkv[at(j), :] = total
+            outs.append(total)
+        cond = sum(tap[:, 9 + k : 10 + k] * back(outs[2], k) for k in range(3))
+        bent = jnp.tanh(cond)
+        squash[here, :] = bent
+        decay = jnp.exp(-tap[:, 12:13] * place) * (1.0 / math.sqrt(seq))
+        filt = (kern[here, :] + bent) * decay
+        kern[here, :] = filt
+        source = outs[1] * outs[2]
+        sig[at(0), :] = jnp.where(lane < lags, filt, 0.0).astype(bf16)
+        sig[at(1), :] = (source * half1).astype(bf16)
+        sig[at(2), :] = (source * half2).astype(bf16)
+        return carry
+
+    lax.fori_loop(0, own // row_tile, mix_rows, 0)
+
+    def freq_tile(j, carry):
+        re_at = pl.ds(pl.multiple_of(j * lane_tile, lane_tile), lane_tile)
+        im_at = pl.ds(pl.multiple_of(freq + j * lane_tile, lane_tile), lane_tile)
+        re = nn(sig[...], tab[:, re_at])
+        im = nn(sig[...], tab[:, im_at])
+        hat[:, re_at] = re.astype(bf16)
+        hat[:, im_at] = im.astype(bf16)
+        kr, ki = re[:own], im[:own]
+        for h in range(2):
+            sr, si = re[own * (h + 1) : own * (h + 2)], im[own * (h + 1) : own * (h + 2)]
+            prod[own * h : own * (h + 1), re_at] = (kr * sr - ki * si).astype(bf16)
+            prod[own * h : own * (h + 1), im_at] = (kr * si + ki * sr).astype(bf16)
+        return carry
+
+    lax.fori_loop(0, freq // lane_tile, freq_tile, 0)
+
+    def g_relay(hop):
+        each_part(functools.partial(g_line.relay, hop))
+
+    g_relay(1)
+
+    def time_tile(j, carry):
+        cols = pl.ds(pl.multiple_of(j * lane_tile, lane_tile), lane_tile)
+        both = nn(prod[...], inv[:, cols])
+        total = (both[:own] * mask_ref[0:1, cols] + both[own:] * mask_ref[1:2, cols]) * (1.0 / freq)
+        mixed[:, cols] = total
+        mixf[:, cols] = (qkv[0:own, cols] * total).astype(bf16)
+        return carry
+
+    lax.fori_loop(0, parts, time_tile, 0)
+    for hop in range(2, ways - 1):
+        g_relay(hop)
+
+    def finish(part):
+        for way in (0, 1):
+            g_line.wait_recv(way, ways - 2, part)
+            for hop in range(ways - 1):
+                in_line.wait_send(way, hop, part)
+                g_line.wait_send(way, hop, part)
+
+    each_part(finish)
+    for s in range(1, ways):
+        direct(lambda at: gains.at[at], gain_send, gain_recv, s, (z + s) % ways, z).wait_send()
+        direct(lambda at: pieces.at[group, at], piece_send, piece_recv, s, (z + s) % ways, z).wait_send()
+    for bit, batch in started:
+        for make, piece in batch:
+            make(piece).wait_send()
+    saves = []
+    for k, (src, dst) in enumerate([
+        (xf, xf_out), (gf, gf_out), (outt, outt_out), (proj, proj_out), (mixf, mixo_out), (qkv, qkv_out),
+        (squash, squash_out), (kern, kern_out), (mixed, mixed_out), (hat, hat_out), (arg, arg_out),
+    ]):
+        copy = pltpu.make_async_copy(src, dst, save_sem.at[k])
+        copy.start()
+        saves.append(copy)
+    for copy in saves:
+        copy.wait()
+
+
+def front(cfg, x_own, g_own, masks, cols, gain_rows, fin_t, in_t, out_flat, feats, tab, inv):
+    ways, rows, seq, own, width, bits = (cfg[k] for k in ("ways", "rows", "seq", "own", "width", "bits"))
+    period = 3 * seq // 2
+    held = [
+        ((width, seq), bf16), ((width, seq), bf16), ((width, width), bf16), ((3 * own, seq), f32), ((own, seq), bf16),
+        ((3 * own, seq), f32), ((own, seq), f32), ((own, seq), f32), ((own, seq), f32), ((3 * own, period), bf16),
+        ((64, seq), f32),
+    ]
+    here = pl.BlockSpec(memory_space=pltpu.VMEM)
+    there = pl.BlockSpec(memory_space=pl.ANY)
+    dma = pltpu.SemaphoreType.DMA
+    parts = seq // lane_tile
+    extra = [
+        ((3 * own, width), bf16), ((seq, period), bf16), ((period, seq), bf16), ((width, seq), bf16),
+        ((1 << bits, ways, own * width // 128 // (1 << bits), 128), bf16), ((ways, 8, 256), f32), ((width, 128), f32),
+        ((3 * own, seq), bf16), ((2 * own, period), bf16),
+    ]
+    return pl.pallas_call(
+        functools.partial(front_kernel, cfg),
+        out_shape=[jax.ShapeDtypeStruct(s, t) for s, t in held],
+        in_specs=[there, there, here, here, here, here, there, there, here, there, there],
+        out_specs=[there] * len(held),
+        scratch_shapes=[pltpu.VMEM(s, t) for s, t in held + extra] + [
+            dma((8,)), dma((2, 2, ways - 1, parts)), dma((2, 2, ways - 1, parts)),
+            dma((ways + (1 << bits),)), dma((ways + (1 << bits),)), dma((ways,)), dma((ways,)), dma((16,)),
+        ],
+        compiler_params=pltpu.CompilerParams(collective_id=0, has_side_effects=True, vmem_limit_bytes=56 << 20),
+    )(x_own, g_own, masks, cols, gain_rows, fin_t, in_t, out_flat, feats, tab, inv)
 
 def local(
     hidden_in, halves, norm1_gain, in_proj, short_taps, cond_taps, filter_in, filter_bias,
@@ -73,11 +392,28 @@
     def gathered(v, axis=0):
         return lax.all_gather(v, "chan", axis=axis, tiled=True)
 
+    rows = lax.axis_size("dp")
+    cfg = dict(ways=ways, rows=rows, seq=seq_len, own=own, width=width, bits=min(3, rows.bit_length() - 1))
     x_own = hidden_in[0].T
     grad_own = (out_grad[0].T.astype(f32) * valid).astype(bf16)
-    x_full = gathered(x_own).astype(f32)
-    grad_full = gathered(grad_own)
-    out_full = gathered(out_proj, axis=1)
+    masks = jnp.pad(jnp.concatenate([half1, half2, valid], axis=0), ((0, 5), (0, 0)))
+    small = jnp.concatenate([short_taps.reshape(9, own), cond_taps, decay_rate[None], jnp.zeros((51, own), f32), filter_out])
+    cols = small.T
+    gain_rows = jnp.pad(jnp.stack([norm1_gain, norm2_gain]), ((0, 6), (0, 256 - own)))
+    feat_np = band_features(seq_len, filter_in.shape[0])
+    count = feat_np.shape[0]
+    feat_np = np.concatenate([feat_np, np.ones((1, seq_len), np.float32), np.zeros((63 - count, seq_len), np.float32)])
+    feats = jnp.asarray(feat_np)
+    fin_t = jnp.pad(jnp.concatenate([filter_in, filter_bias[None]]), ((0, 63 - count), (0, 0))).T
+    in_flat = in_proj.reshape(width, 3 * own)
+    out_flat = out_proj.T.reshape(own, width // 128, 128).transpose(1, 0, 2).reshape(-1, 128)
+    table_np = wave_matrix(seq_len).astype(np.float32)
+    table = jnp.asarray(table_np).astype(bf16)
+    inv_table = jnp.asarray(table_np.T).astype(bf16)
+    (xf, grad_full, out_t, proj, mixer_own, qkv, squash, kern, mixed, hat, arg) = front(
+        cfg, x_own, grad_own, masks, cols, gain_rows, fin_t, in_flat.T, out_flat, feats, table, inv_table)
+    x_full = xf.astype(f32)
+    out_full = out_t.T
     gains = gathered(jnp.stack([norm1_gain, norm2_gain], axis=1))
     gain1, gain2 = gains[:, 0:1], gains[:, 1:2]
 
@@ -89,17 +425,10 @@
 
     n1, inv1 = normed(x_full)
     norm1_out = (n1 * gain1).astype(bf16)
-    in_flat = in_proj.reshape(width, 3 * own)
-    proj = tn(in_flat, norm1_out)
-
-    feats = jnp.asarray(band_features(seq_len, filter_in.shape[0]))
-    arg = tn(filter_in, feats, highest) + filter_bias[:, None]
     wave = jnp.sin(arg)
-    base = tn(filter_out, wave, highest)
     decay = jnp.exp(-decay_rate[:, None] * pos.astype(f32)) * (1.0 / math.sqrt(seq_len))
     ramp = pos.astype(f32)
 
-    table = jnp.asarray(wave_matrix(seq_len).astype(np.float32)).astype(bf16)
 
     def spectrum(v):
         return nn(v.astype(bf16), table[: v.shape[1]])
@@ -110,20 +439,11 @@
 
     parts = [proj[j * own : (j + 1) * own] for j in range(3)]
     taps = [[short_taps[i, j][:, None] for i in range(3)] for j in range(3)]
-    query, key, value = [sum(taps[j][i] * later(parts[j], i) for i in range(3)) for j in range(3)]
+    query, key, value = [qkv[j * own : (j + 1) * own] for j in range(3)]
     ctaps = [cond_taps[i][:, None] for i in range(3)]
-    cond = sum(ctaps[i] * later(value, i) for i in range(3))
-    squash = jnp.tanh(cond)
-    kern = (base + squash) * decay
-    source = key * value
-    k_hat = spectrum(kern[:, :lags])
-    s_hat = [spectrum(source * h) for h in (half1, half2)]
-    kr, ki = k_hat[:, :freq], k_hat[:, freq:]
-    mixed = 0.0
-    for h, s in zip((half1, half2), s_hat):
-        sr, si = s[:, :freq], s[:, freq:]
-        mixed = mixed + h * signal(kr * sr - ki * si, kr * si + ki * sr, seq_len)
-    mixer_own = (query * mixed).astype(bf16)
+    hats = [hat[j * own : (j + 1) * own].astype(f32) for j in range(3)]
+    kr, ki = hats[0][:, :freq], hats[0][:, freq:]
+    s_hat = hats[1:]
     mixer_full = gathered(mixer_own)
 
     resid = x_full + tn(out_full, mixer_full)
@@ -195,8 +515,8 @@
     ).astype(bf16)
     fout_grad = nt(wave, base_grad, highest)
     arg_grad = nn(filter_out, base_grad, highest) * jnp.cos(arg)
-    fin_grad = nt(feats, arg_grad, highest)
-    fbias_grad = jnp.sum(arg_grad, axis=1)
+    both = nt(feats, arg_grad, highest)
+    fin_grad, fbias_grad = both[:count], both[count]
 
     in_grad = nt(norm1_out, low)
     terms1 = lax.psum_scatter(nn(in_flat, low).astype(bf16), "chan", scatter_dimension=0, tiled=True).astype(f32)

time: 459 us -> 436 us (0.950)
  waiting for transfers between devices: 205 us -> 123 us
  Pallas kernels: 0 us -> 74.9 us
  matrix products: 67.6 us -> 50.3 us
  local copies, waits for them, and re-layouts: 22.5 us -> 27.3 us
    pallas_call x0 -> x1, Pallas kernels: none -> 74.9 us  [front(): pl.pallas_call(functools.partial(front_kernel, cfg), out_shape=[jax.Shape...]
    all_gather x4 -> x1, waiting for transfers between devices: 87.1 us -> 22 us  [gathered(): return lax.all_gather(v, 'chan', axis=axis, tiled=True)]
    reduce_scatter x1, waiting for transfers between devices: 34.2 us -> 19.6 us  [local(): lax.psum_scatter(terms, 'chan', scatter_dimension=1, tiled=True).astype(f32)]
    dot_general x7 -> x4, matrix products: 20.2 us -> 10.6 us  [tn(): lax.dot_general(a, b, (((0,), (0,)), ((), ())), precision=precision, pref...]
    dot_general x11 -> x8, matrix products: 20.5 us -> 16.2 us  [nn(): lax.dot_general(a, b, (((1,), (0,)), ((), ())), precision=precision, pref...]
    unnamed x232 -> x189, local copies, waits for them, and re-layouts: 15.3 us -> 11.3 us
    dot_general x17 -> x13, matrix products: 26.9 us -> 23.5 us  [nt(): lax.dot_general(a, b, (((1,), (1,)), ((), ())), precision=precision, pref...]
  transfers between devices with their start and end apart: 9 -> 6, of which waited for: 8 -> 5; matrix products, arithmetic and copies ran while one was open for 21% -> 16% of each run, Pallas kernels for 0% -> 0%
where the time goes in v2:
time: 436 us; the launch traced here: 431 us
  waiting for transfers between devices  123 us (28%)
  blocking collectives  94.8 us (22%)
  Pallas kernels  74.9 us (17%)
  matrix products  50.3 us (12%)
  other arithmetic  40.3 us (9%)
  local copies, waits for them, and re-layouts  27.3 us (6%)
  between operations  16 us (4%)
  starting transfers between devices  4.62 us (1%)
    pallas_call x1, Pallas kernels, front(): pl.pallas_call(functools.partial(front_kernel, cfg), out_shape=[jax.Shape...  74.9 us
    psum x1, blocking collectives, local(): fi, fb = lax.psum((fin_grad, fbias_grad), ('dp', 'chan'))  42 us
    psum x1, waiting for transfers between devices, local(): lax.psum((w_down_grad.astype(bf16), w_gate_grad.astype(bf16), w_up_grad.a...  33.5 us
    reduce_scatter x1, waiting for transfers between devices, local(): lax.psum_scatter(nn(in_flat, low).astype(bf16), 'chan', scatter_dimension...  29.3 us
    psum x1, blocking collectives, local(): lax.psum((gain2_own, gain1_grad, stap_grad, ctap_grad, fout_grad, rate_gr...  23.7 us
    dot_general x13, matrix products, nt(): lax.dot_general(a, b, (((1,), (1,)), ((), ())), precision=precision, pref...  23.5 us
    all_gather x1, waiting for transfers between devices, gathered(): return lax.all_gather(v, 'chan', axis=axis, tiled=True)  22 us
    reduce_scatter x1, waiting for transfers between devices, local(): lax.psum_scatter(terms, 'chan', scatter_dimension=1, tiled=True).astype(f32)  19.6 us
  transfers between devices with their start and end apart: 6, of which 5 were waited for; matrix products, arithmetic and copies ran while one was open for 16% of the time, Pallas kernels for 0%

profile of v2, /device:TPU:0, one launch (start us, length us, event | category | flops | bytes accessed | tf_op | source)
XLA Modules:
  0.0 430.8 jit_solution(5740529985694436939)
XLA Ops:
  7.3 1.4 fusion.115
  8.7 1.3 and_convert_fusion
  10.0 1.3 fusion.108
  11.3 1.3 fusion.101
  12.6 1.3 reshape.191
  13.9 0.8 copy.76
  15.5 0.8 copy.71
  16.8 0.8 fusion.82.g_hbm
  19.5 0.8 concatenate.26
  20.3 74.9 %shard_map.298 = (bf16[768,1024]{1,0:T(8,128)(2,1)}, bf16[768,1024]{1,0:T(8,128)(2,1)}, bf16[768,768]{1,0:T(8,128)(2,1)}, f32[576,1024]{1,0:T(8,128)}, bf16[192,...) custom-call(bf16[192,1024]{1,0:T(8,128)(2,1)} %bitcast.183, ...), custom_call_target="tpu_custom_call" | custom-call | tf_op jit(solution)/shard_map/pallas_call | solution.py:363
  95.4 12.3 %all-gather = f32[4,192,2]{1,2,0:T(2,128)S(1)} all-gather(f32[1,192,2]{1,2,0:T(2,128)S(1)} %maximum_bitcast_fusion.3), channel_id=1, replica_groups=mesh['dp'=8,'chan'=4] {'chan'}, dimensions={0}, use_global_device_ids=true | all-gather | bytes 7680 | tf_op jit(solution)/shard_map/all_gather | solution.py:393
  108.4 22.0 %all-gather.3.cloned.1.call-done = bf16[768,1024]{1,0:T(8,128)(2,1)} async-done(((bf16[192,1024]{1,0:T(8,128)(2,1)}), bf16[768,1024]{1,0:T(8,128)(2,1)}) %all-gather.3.cloned.1.call-update) | async-done | bytes 1572880 | tf_op jit(solution)/shard_map/all_gather | solution.py:393
  130.5 3.7 fusion.109
  134.2 2.0 multiply_convert_fusion.1
  136.8 1.4 fusion.116
  138.7 1.4 fusion.117
  140.1 3.5 fusion.5
  143.6 1.4 fusion.118
  145.3 2.6 fusion.14
  148.5 2.1 slice.190
  151.2 1.9 fusion.97
  153.1 1.9 fusion.96
  157.2 3.3 fusion.111
  160.5 1.5 slice_convert_fusion.1
  162.6 19.6 %reduce-scatter.6.cloned.1.call-done = bf16[768,256]{1,0:T(8,128)(2,1)} async-done(((bf16[768,1024]{1,0:T(8,128)(2,1)}), bf16[768,256]{1,0:T(8,128)(2,1)}) %reduce-scatter.6.cloned.1.call-update) | async-done | bytes 393232 | tf_op jit(solution)/shard_map/reduce_scatter | solution.py:477
  182.2 1.7 fusion.72
  184.0 1.7 fusion.70
  186.3 1.7 copy.81
  188.0 4.2 all-to-all-start
  192.2 4.0 fusion.13
  196.5 4.4 %convolution_convert_fusion.3 = bf16[768,768]{1,0:T(8,128)(2,1)} fusion(bf16[768,1024]{1,0:T(8,128)(2,1)} %copy-done.18, bf16[768,1024]{0,1:T(8,128)(2,1)} %copy-done.89), kind=kOutput, calls=%fused_computation.31 | convolution fusion | flops 1208549376 | bytes 4325376 | tf_op jit(solution)/shard_map/dot_general | solution.py:40
  201.0 2.4 convolution_convert_fusion.4
  203.4 2.4 convolution_convert_fusion.2
  205.8 18.1 %all-to-all-done = bf16[2,768,256]{2,0,1:T(2,128)(2,1)} async-done(((bf16[2,768,256]{2,0,1:T(2,128)(2,1)}), bf16[2,768,256]{2,0,1:T(2,128)(2,1)}, u32[]{:S(2)}, u32[]{:S(2)}) %all-to-all-start) | async-done | bytes 786464 | tf_op jit(solution)/shard_map/all_to_all | solution.py:483
  223.9 1.7 copy.91
  226.1 1.5 copy-done.2
  227.6 2.1 fusion.89
  229.8 0.8 fusion.90
  231.4 0.7 fusion.93
  232.7 0.7 fusion.20
  234.3 1.4 fusion.64
  238.0 0.7 fusion.19
  239.9 4.9 %multiply_reduce_fusion.4 = (f32[192]{0:T(256)}, f32[192]{0:T(256)}, f32[192]{0:T(256)}, f32[192]{0:T(256)}, f32[192]{0:T(256)}, /*index=5*/f32[192]{0:T(256)}, ...) fusion(f32[576,1024]{1,0:T(8,128)} %get-tuple-element.34, ...), kind=kOutput, calls=%fused_computation.135 | convolution fusion | flops 308476224 | bytes 16528384 | tf_op jit(solution)/shard_map/dot_general | solution.py:40
  244.9 0.8 fusion.34
  247.0 1.4 convolution_convert_fusion.6
  248.4 2.1 fusion.16
  250.6 1.1 copy-done.25
  251.7 3.7 fusion.15
  257.3 2.4 fusion.1
  259.9 2.4 multiply_bitcast_fusion
  262.3 1.5 fusion.22
  264.3 42.0 %all-reduce.21 = (f32[33,64]{1,0:T(8,128)}, f32[64]{0:T(128)}) all-reduce(f32[33,64]{1,0:T(8,128)S(1)} %slice.247, f32[64]{0:T(128)S(1)} %slice_bitcast_fusion), channel_id=1, replica_groups=mesh['dp'=8,'chan'=4] {'dp','chan'}, use_global_device_ids=true, to_apply=%region_30.31 | all-reduce | flops 2176 | bytes 17408 | tf_op jit(solution)/shard_map/psum | solution.py:535
  306.5 1.8 fusion.80
  308.3 33.5 %all-reduce.27.cloned.1.call-done = (bf16[768,3,192]{0,2,1:T(8,128)(2,1)}, bf16[768,192]{0,1:T(8,128)(2,1)}, bf16[768,768]{1,0:T(8,128)(2,1)}, bf16[768,768]{1,0:T(8,128)(2,1)}, bf16[768,768]{1,0:T(8,128)(2,1)}) async-done(((bf16[768,3,192]{0,2,1:T(8,128)(2,1)}, bf16[768,192]{0,1:T(8,128)(2,1)}, bf16[768,768]{1,0:T(8,128)(2,1)}, bf16[768,768]{1,0:T(8,128)(2,1)}, bf16[768,768]{1,0:T(8,128)(2,1)}), ...) | async-done | bytes 4718608 | tf_op jit(solution)/shard_map/psum | solution.py:531
  341.7 2.9 convert_element_type.246
  344.7 1.6 convert_element_type.248
  346.4 1.6 convert_element_type.250
  347.9 1.4 reshape.194
  349.3 0.9 convert_element_type.244
  350.1 29.3 %reduce-scatter.8.cloned.1.call-done = bf16[192,1024]{1,0:T(8,128)(2,1)} async-done(((bf16[768,1024]{1,0:T(8,128)(2,1)}), bf16[192,1024]{1,0:T(8,128)(2,1)}) %reduce-scatter.8.cloned.1.call-update) | async-done | bytes 393232 | tf_op jit(solution)/shard_map/reduce_scatter | solution.py:522
  379.4 1.6 fusion.78
  381.0 16.7 %all-reduce.23 = (f32[1024]{0:T(1024)S(1)}, f32[1024]{0:T(1024)S(1)}, f32[768]{0:T(1024)S(1)}) all-reduce(f32[1024]{0:T(1024)S(1)} %get-tuple-element.40, f32[1024]{0:T(1024)S(1)} %get-tuple-element.64, f32[768]{0:T(1024)S(1)} %get-tuple-element.37), channel_id=1, replica_groups=mesh['dp'=8,'chan'=4] {'chan'}, use_global_device_ids=true, to_apply=%region_12.13 | all-reduce | flops 2816 | bytes 22528 | tf_op jit(solution)/shard_map/psum | solution.py:526
  397.8 23.7 %all-reduce.22 = (f32[192]{0:T(256)}, f32[3,3,192]{2,1,0:T(4,128)}, f32[3,192]{1,0:T(4,128)}, f32[64,192]{1,0:T(8,128)}, f32[192]{0:T(256)}, /*index=5*/f32[192]{0:T(256)}) all-reduce(f32[192]{0:T(256)S(1)} %get-tuple-element.39, f32[3,3,192]{2,1,0:T(4,128)S(1)} %pad_maximum_fusion.4, ...), channel_id=1, replica_groups=mesh['dp'=8,'chan'=4] {'dp'}, use_global_device_ids=true, to_apply=%region_14.15 | all-reduce | flops 15168 | bytes 121344 | tf_op jit(solution)/shard_map/psum | solution.py:534
  421.5 2.3 fusion.76
  (235 shorter events, 19.4 us)
Async XLA Ops:
  7.2 132.9 %copy-start = (bf16[768,768]{1,0:T(8,128)(2,1)S(1)}, bf16[768,768]{1,0:T(8,128)(2,1)}, u32[]{:S(2)}) copy-start(bf16[768,768]{1,0:T(8,128)(2,1)} %param.33) | copy-start | bytes 3538948
  7.2 9.1 %copy-start.61 = (f32[192]{0:T(256)S(1)}, f32[192]{0:T(256)}, u32[]{:S(2)}) copy-start(f32[192]{0:T(256)} %param.28) | copy-start | bytes 2308
  7.2 9.3 %copy-start.36 = (f32[64,192]{1,0:T(8,128)S(1)}, f32[64,192]{1,0:T(8,128)}, u32[]{:S(2)}) copy-start(f32[64,192]{1,0:T(8,128)} %param.27) | copy-start | bytes 147460
  7.2 9.3 %copy-start.39 = (f32[33,64]{1,0:T(8,128)S(1)}, f32[33,64]{1,0:T(8,128)}, u32[]{:S(2)}) copy-start(f32[33,64]{1,0:T(8,128)} %param.25) | copy-start | bytes 25348
  7.2 9.4 %copy-start.79 = (f32[64]{0:T(128)S(1)}, f32[64]{0:T(128)}, u32[]{:S(2)}) copy-start(f32[64]{0:T(128)} %param.26) | copy-start | bytes 772
  7.2 9.5 %copy-start.30 = (bf16[1,1024,192]{1,2,0:T(8,128)(2,1)S(1)}, bf16[1,1024,192]{1,2,0:T(8,128)(2,1)}, u32[]{:S(2)}) copy-start(bf16[1,1024,192]{1,2,0:T(8,128)(2,1)} %param.34) | copy-start | bytes 1179652
  7.3 11.0 %copy-start.41 = (f32[192]{0:T(256)S(1)}, f32[192]{0:T(256)}, u32[]{:S(2)}) copy-start(f32[192]{0:T(256)} %param.21) | copy-start | bytes 2308
  7.3 11.0 %copy-start.69 = (f32[192]{0:T(256)S(1)}, f32[192]{0:T(256)}, u32[]{:S(2)}) copy-start(f32[192]{0:T(256)} %param.30) | copy-start | bytes 2308
  7.3 123.2 %all-gather.3.cloned.1.call-start = ((), (), s32[]{:S(2)}) async-start(), calls=%async_computation.4 | async-start | bytes 1966080 | tf_op jit(solution)/shard_map/all_gather | solution.py:393
  95.3 86.9 %reduce-scatter.6.cloned.1.call-start = ((), (), s32[]{:S(2)}) async-start(), calls=%async_computation.6 | async-start | bytes 1966080 | tf_op jit(solution)/shard_map/reduce_scatter | solution.py:477
  134.2 2.7 copy-start.8
  134.2 2.6 copy-start.81
  147.9 7.1 %copy-start.48 = (f32[3,192]{1,0:T(4,128)S(1)}, f32[3,192]{1,0:T(4,128)}, u32[]{:S(2)}) copy-start(f32[3,192]{1,0:T(4,128)} %param.24) | copy-start | bytes 6916
  147.9 7.7 %copy-start.38 = (f32[3,3,192]{2,1,0:T(4,128)S(1)}, f32[3,3,192]{2,1,0:T(4,128)}, u32[]{:S(2)}) copy-start(f32[3,3,192]{2,1,0:T(4,128)} %param.23) | copy-start | bytes 20740
  147.9 8.3 %copy-start.6 = (bf16[768,1024]{1,0:T(8,128)(2,1)S(1)}, bf16[768,1024]{1,0:T(8,128)(2,1)}, u32[]{:S(2)}) copy-start(bf16[768,1024]{1,0:T(8,128)(2,1)} %get-tuple-element.26) | copy-start | bytes 4718596
  157.2 3.3 copy-start.16
  182.2 3.4 copy-start.83
  188.0 36.0 %all-to-all-start = ((bf16[2,768,256]{2,0,1:T(2,128)(2,1)}), bf16[2,768,256]{2,0,1:T(2,128)(2,1)}, u32[]{:S(2)}, u32[]{:S(2)}) async-start(bf16[2,768,256]{2,0,1:T(2,128)(2,1)} %copy.81), calls=%async_computation.2 | async-start | bytes 1572864 | tf_op jit(solution)/shard_map/all_to_all | solution.py:483
  192.2 67.7 %reduce-scatter.4.cloned.1.call-start = ((), (), s32[]{:S(2)}) async-start(), calls=%async_computation.5 | async-start | bytes 1966080 | tf_op jit(solution)/shard_map/reduce_scatter | solution.py:467
  196.3 145.5 %all-reduce.27.cloned.1.call-start = ((), (), s32[]{:S(2)}) async-start(), calls=%async_computation.8 | async-start | bytes 9437184 | tf_op jit(solution)/shard_map/psum | solution.py:531
  196.5 4.4 %copy-start.19 = (bf16[768,1024]{1,0:T(8,128)(2,1)S(1)}, bf16[768,1024]{1,0:T(8,128)(2,1)}, u32[]{:S(2)}) copy-start(bf16[768,1024]{1,0:T(8,128)(2,1)} %copy-done.18) | copy-start | bytes 4718596
  196.5 4.4 %copy-start.87 = (bf16[768,1024]{0,1:T(8,128)(2,1)S(1)}, bf16[768,1024]{0,1:T(8,128)(2,1)}, u32[]{:S(2)}) copy-start(bf16[768,1024]{0,1:T(8,128)(2,1)} %copy-done.86) | copy-start | bytes 4718596
  201.0 2.4 copy-start.35
  201.0 2.4 copy-start.88
  225.7 1.9 copy-start.2
  225.7 1.9 copy-start.46
  227.6 2.1 copy-start.3
  227.6 2.1 copy-start.45
  233.4 2.3 copy-start.14
  239.8 5.0 %copy-start.76 = (f32[1,1,192]{2,1,0:T(1,128)S(1)}, f32[1,1,192]{2,1,0:T(1,128)}, u32[]{:S(2)}) copy-start(f32[1,1,192]{2,1,0:T(1,128)} %get-tuple-element.101) | copy-start | bytes 2308
  239.8 5.0 %copy-start.77 = (f32[1,1,192]{2,1,0:T(1,128)S(1)}, f32[1,1,192]{2,1,0:T(1,128)}, u32[]{:S(2)}) copy-start(f32[1,1,192]{2,1,0:T(1,128)} %get-tuple-element.106) | copy-start | bytes 2308
  239.8 5.0 %copy-start.78 = (f32[1,1,192]{2,1,0:T(1,128)S(1)}, f32[1,1,192]{2,1,0:T(1,128)}, u32[]{:S(2)}) copy-start(f32[1,1,192]{2,1,0:T(1,128)} %get-tuple-element.107) | copy-start | bytes 2308
  239.9 5.9 %copy-start.73 = (f32[1,1,192]{2,1,0:T(1,128)S(1)}, f32[1,1,192]{2,1,0:T(1,128)}, u32[]{:S(2)}) copy-start(f32[1,1,192]{2,1,0:T(1,128)} %get-tuple-element.103) | copy-start | bytes 2308
  239.9 5.9 %copy-start.74 = (f32[1,1,192]{2,1,0:T(1,128)S(1)}, f32[1,1,192]{2,1,0:T(1,128)}, u32[]{:S(2)}) copy-start(f32[1,1,192]{2,1,0:T(1,128)} %get-tuple-element.104) | copy-start | bytes 2308
  239.9 5.9 %copy-start.75 = (f32[1,1,192]{2,1,0:T(1,128)S(1)}, f32[1,1,192]{2,1,0:T(1,128)}, u32[]{:S(2)}) copy-start(f32[1,1,192]{2,1,0:T(1,128)} %get-tuple-element.105) | copy-start | bytes 2308
  244.9 2.2 copy-start.80
  246.3 2.1 copy-start.31
  246.4 2.1 copy-start.7
  246.4 2.1 copy-start.47
  246.4 2.0 copy-start.68
  247.0 3.6 copy-start.32
  250.6 128.9 %reduce-scatter.8.cloned.1.call-start = ((), (), s32[]{:S(2)}) async-start(), calls=%async_computation.7 | async-start | bytes 1966080 | tf_op jit(solution)/shard_map/reduce_scatter | solution.py:522
  259.7 2.6 copy-start.15
  259.7 2.6 copy-start.37
  259.7 2.6 copy-start.63
  259.7 2.6 copy-start.84
  259.7 4.2 copy-start.24
  259.7 4.5 %copy-start.64 = (f32[192]{0:T(256)S(1)}, f32[192]{0:T(256)}, u32[]{:S(2)}) copy-start(f32[192]{0:T(256)} %get-tuple-element.100) | copy-start | bytes 2308
  259.7 46.6 %copy-start.49 = (f32[192]{0:T(256)S(1)}, f32[192]{0:T(256)}, u32[]{:S(2)}) copy-start(f32[192]{0:T(256)} %get-tuple-element.46) | copy-start | bytes 2308
  259.8 46.6 %copy-start.50 = (f32[192]{0:T(256)S(1)}, f32[192]{0:T(256)}, u32[]{:S(2)}) copy-start(f32[192]{0:T(256)} %get-tuple-element.47) | copy-start | bytes 2308
  259.8 46.5 %copy-start.51 = (f32[192]{0:T(256)S(1)}, f32[192]{0:T(256)}, u32[]{:S(2)}) copy-start(f32[192]{0:T(256)} %get-tuple-element.60) | copy-start | bytes 2308
  259.8 46.5 %copy-start.58 = (f32[192]{0:T(256)S(1)}, f32[192]{0:T(256)}, u32[]{:S(2)}) copy-start(f32[192]{0:T(256)} %get-tuple-element.43) | copy-start | bytes 2308
  259.8 46.5 %copy-start.59 = (f32[192]{0:T(256)S(1)}, f32[192]{0:T(256)}, u32[]{:S(2)}) copy-start(f32[192]{0:T(256)} %get-tuple-element.44) | copy-start | bytes 2308
  259.8 46.5 %copy-start.60 = (f32[192]{0:T(256)S(1)}, f32[192]{0:T(256)}, u32[]{:S(2)}) copy-start(f32[192]{0:T(256)} %get-tuple-element.45) | copy-start | bytes 2308
  259.8 46.6 %copy-start.55 = (f32[192]{0:T(256)S(1)}, f32[192]{0:T(256)}, u32[]{:S(2)}) copy-start(f32[192]{0:T(256)} %get-tuple-element.57) | copy-start | bytes 2308
  259.8 46.6 %copy-start.56 = (f32[192]{0:T(256)S(1)}, f32[192]{0:T(256)}, u32[]{:S(2)}) copy-start(f32[192]{0:T(256)} %get-tuple-element.59) | copy-start | bytes 2308
  259.8 46.6 %copy-start.57 = (f32[192]{0:T(256)S(1)}, f32[192]{0:T(256)}, u32[]{:S(2)}) copy-start(f32[192]{0:T(256)} %get-tuple-element.62) | copy-start | bytes 2308
  259.8 46.6 %copy-start.52 = (f32[192]{0:T(256)S(1)}, f32[192]{0:T(256)}, u32[]{:S(2)}) copy-start(f32[192]{0:T(256)} %get-tuple-element.56) | copy-start | bytes 2308
  259.8 46.6 %copy-start.53 = (f32[192]{0:T(256)S(1)}, f32[192]{0:T(256)}, u32[]{:S(2)}) copy-start(f32[192]{0:T(256)} %get-tuple-element.58) | copy-start | bytes 2308
  259.9 46.6 %copy-start.54 = (f32[192]{0:T(256)S(1)}, f32[192]{0:T(256)}, u32[]{:S(2)}) copy-start(f32[192]{0:T(256)} %get-tuple-element.61) | copy-start | bytes 2308
  341.7 2.9 copy-start.21
  347.9 31.5 %copy-start.42 = (f32[192]{0:T(256)S(1)}, f32[192]{0:T(256)}, u32[]{:S(2)}) copy-start(f32[192]{0:T(256)} %param.21) | copy-start | bytes 2308
  349.3 74.5 %copy-start.1 = (bf16[768,768]{1,0:T(8,128)(2,1)S(1)}, bf16[768,768]{1,0:T(8,128)(2,1)}, u32[]{:S(2)}) copy-start(bf16[768,768]{1,0:T(8,128)(2,1)} %param.33) | copy-start | bytes 3538948
  379.4 42.1 %copy-start.17 = (bf16[192,1024]{1,0:T(8,128)(2,1)S(1)}, bf16[192,1024]{1,0:T(8,128)(2,1)}, u32[]{:S(2)}) copy-start(bf16[192,1024]{1,0:T(8,128)(2,1)} %reduce-scatter.8.cloned.1.call-done) | copy-start | bytes 1179652
  (32 other events, 48.0 us)
Sparse Core Ops, SparseCore 0:
  95.4 34.9 all-gather.2
  148.0 34.1 reduce-scatter.5
  196.4 39.8 reduce-scatter.3
  250.7 90.9 all-reduce.26
  344.0 35.4 reduce-scatter.7

commit v3 on v1

v3 whole, which is shorter than its diff:
```python
import functools
import math

import jax
import jax.numpy as jnp
import numpy as np
from jax import lax
from jax.experimental import pallas as pl
from jax.experimental.pallas import tpu as pltpu
from jax.sharding import PartitionSpec as P

highest = lax.Precision.HIGHEST
norm_eps = 1e-05
f32 = jnp.float32
bf16 = jnp.bfloat16


def band_features(seq_len, feat_count):
    bands = (feat_count - 1) // 2
    positions = np.arange(seq_len)
    orders = np.arange(1, bands + 1)
    phases = (orders[:, None] * positions[None, :] % seq_len) * (2.0 * math.pi / seq_len)
    ramp = positions[None, :] / seq_len
    return np.concatenate([ramp, np.sin(phases), np.cos(phases)], axis=0).astype(np.float32)


def wave_matrix(seq_len):
    period = 3 * seq_len // 2
    freq = period // 2
    phase = (np.arange(seq_len)[:, None] * (2 * np.arange(freq)[None, :] + 1)) % (2 * period)
    angle = phase * (math.pi / period)
    return np.concatenate([np.cos(angle), np.sin(angle)], axis=1)


def nn(a, b, precision=None):
    return lax.dot_general(a, b, (((1,), (0,)), ((), ())), precision=precision, preferred_element_type=f32)


def nt(a, b, precision=None):
    return lax.dot_general(a, b, (((1,), (1,)), ((), ())), precision=precision, preferred_element_type=f32)


def tn(a, b, precision=None):
    return lax.dot_general(a, b, (((0,), (0,)), ((), ())), precision=precision, preferred_element_type=f32)


MESH = pl.DeviceIdType.MESH
lane_tile = 256
row_tile = 16


def flipped(index, bit):
    return index + (1 << bit) * (1 - 2 * ((index // (1 << bit)) % 2))


class Line:
    def __init__(self, view, send_sem, recv_sem, at, ways):
        self.view, self.send_sem, self.recv_sem, self.at, self.ways = view, send_sem, recv_sem, at, ways

    def copy(self, way, hop, part, shard):
        ref = self.view(shard, part)
        step = 1 - 2 * way
        return pltpu.make_async_remote_copy(
            src_ref=ref, dst_ref=ref, send_sem=self.send_sem.at[way, hop, part],
            recv_sem=self.recv_sem.at[way, hop, part],
            device_id={"chan": (self.at + step + self.ways) % self.ways}, device_id_type=MESH,
        )

    def sends(self, way, hop):
        if way == 0:
            return jnp.logical_and(self.at >= hop, self.at < self.ways - 1)
        return jnp.logical_and(self.at + hop <= self.ways - 1, self.at > 0)

    def gets(self, way, hop):
        if way == 0:
            return self.at >= hop + 1
        return self.at + hop + 1 <= self.ways - 1

    def order(self, way, index):
        return index if way == 0 else self.ways - 1 - index

    def far_side(self):
        return (2 * self.at) // self.ways

    def send_own(self, wanted=True):
        for index in range(self.ways):
            for way in (0, 1):
                @pl.when(jnp.logical_and(self.sends(way, 0), wanted))
                def _():
                    self.copy(way, 0, self.order(way, index), self.at).start()

    def relay(self, way, index, wanted, hops=None):
        part, step = self.order(way, index), 1 - 2 * way
        for hop in range(1, self.ways - 1) if hops is None else hops:
            @pl.when(jnp.logical_and(self.sends(way, hop), wanted))
            def _():
                self.copy(way, hop - 1, part, self.at - hop * step).wait_recv()
                self.copy(way, hop, part, self.at - hop * step).start()

    def short_way(self, index):
        for way in (0, 1):
            self.relay(way, index, self.far_side() == way)

    def long_way(self, index, hops=None):
        for way in (0, 1):
            self.relay(way, index, self.far_side() != way, hops)

    def take(self, index):
        for way in (0, 1):
            for hop in range(self.ways - 1):
                last = self.gets(way, hop)
                if hop + 1 < self.ways - 1:
                    last = jnp.logical_and(last, jnp.logical_not(self.sends(way, hop + 1)))

                @pl.when(last)
                def _():
                    self.copy(way, hop, self.order(way, index), self.at - (hop + 1) * (1 - 2 * way)).wait_recv()

    def drain(self):
        for way in (0, 1):
            for hop in range(self.ways - 1):
                for part in range(self.ways):
                    @pl.when(self.sends(way, hop))
                    def _():
                        self.copy(way, hop, part, self.at - hop * (1 - 2 * way)).wait_send()


class LineSum:
    def __init__(self, mine, inbox, send_sem, recv_sem, at, ways, subs):
        self.mine, self.inbox, self.send_sem, self.recv_sem = mine, inbox, send_sem, recv_sem
        self.at, self.ways, self.subs = at, ways, subs

    def dest(self, way, k):
        return self.ways - 1 - k if way == 0 else k

    def sends(self, way, k):
        return self.dest(way, k) > self.at if way == 0 else self.dest(way, k) < self.at

    def gets(self, way, k):
        dest = self.dest(way, k)
        if way == 0:
            return jnp.logical_and(dest >= self.at, self.at > 0)
        return jnp.logical_and(dest <= self.at, self.at < self.ways - 1)

    def copy(self, way, k, sub):
        step = 1 - 2 * way
        return pltpu.make_async_remote_copy(
            src_ref=self.mine(self.dest(way, k), sub), dst_ref=self.inbox(way, k, sub),
            send_sem=self.send_sem.at[way, k, sub], recv_sem=self.recv_sem.at[way, k, sub],
            device_id={"chan": (self.at + step + self.ways) % self.ways}, device_id_type=MESH,
        )

    def first(self, k, sub):
        for way in (0, 1):
            @pl.when(jnp.logical_and(self.sends(way, k), jnp.logical_not(self.gets(way, k))))
            def _():
                self.copy(way, k, sub[way]).start()

    def onward(self, way, k, sub, wanted):
        @pl.when(jnp.logical_and(jnp.logical_and(self.sends(way, k), self.gets(way, k)), wanted))
        def _():
            self.copy(way, k, sub).wait_recv()
            mine, inbox = self.mine(self.dest(way, k), sub), self.inbox(way, k, sub)
            mine[...] = (mine[...].astype(f32) + inbox[...].astype(f32)).astype(bf16)
            self.copy(way, k, sub).start()

    def near(self, k, sub):
        for way in (0, 1):
            self.onward(way, k, sub[way], (2 * self.at) // self.ways == way)

    def far(self, k, sub):
        for way in (0, 1):
            self.onward(way, k, sub[way], (2 * self.at) // self.ways != way)

    def take(self, way, sub, total):
        k = self.ways - 1 - self.at if way == 0 else self.at

        @pl.when(self.at > 0 if way == 0 else self.at < self.ways - 1)
        def _():
            self.copy(way, k, sub).wait_recv()
            total[...] += self.inbox(way, k, sub)[...].astype(f32)

    def drain(self):
        for way in (0, 1):
            for k in range(self.ways):
                for sub in range(self.subs):
                    @pl.when(self.sends(way, k))
                    def _():
                        self.copy(way, k, sub).wait_send()


class RowSum:
    tile = 96

    def __init__(self, buf, result, box, extra_box, send_sem, recv_sem, r, total_bits):
        self.buf, self.result, self.box, self.extra_box = buf, result, box, extra_box
        self.send_sem, self.recv_sem = send_sem, recv_sem
        self.total_bits, self.r = total_bits, r
        height = buf.shape[0]
        core = r % 2
        steps = [1, 2 + 2 * core, 4 - 2 * core]
        self.levels = []
        base, size = 0, height
        inbox_at = 0
        for step in steps:
            size = size // 2
            bit = (r // step) % 2
            keep, give = base + bit * size, base + (1 - bit) * size
            self.levels.append((r + step * (1 - 2 * bit), keep, give, size, inbox_at))
            base = keep
            inbox_at += size

    def rows(self, at, size, buf=None):
        return (self.buf if buf is None else buf).at[pl.ds(pl.multiple_of(at, 32), size)]

    def halve(self, level):
        partner, keep, give, size, inbox_at = self.levels[level]
        return pltpu.make_async_remote_copy(
            src_ref=self.rows(give, size), dst_ref=self.box.at[pl.ds(inbox_at, size)],
            send_sem=self.send_sem.at[level], recv_sem=self.recv_sem.at[level],
            device_id={"dp": partner}, device_id_type=MESH,
        )

    def double(self, level, arriving=False):
        partner, keep, give, size, inbox_at = self.levels[level]
        part = self.rows(give if arriving else keep, size, self.result)
        return pltpu.make_async_remote_copy(
            src_ref=part, dst_ref=part, send_sem=self.send_sem.at[3 + level], recv_sem=self.recv_sem.at[3 + level],
            device_id={"dp": partner}, device_id_type=MESH,
        )

    def add(self, level, target=None):
        partner, keep, give, size, inbox_at = self.levels[level]
        target = self.buf if target is None else target
        self.halve(level).wait_recv()

        def run(i, carry):
            at = pl.ds(pl.multiple_of(keep + i * self.tile, 32), self.tile)
            there = pl.ds(pl.multiple_of(inbox_at + i * self.tile, 32), self.tile)
            target[at, :] = (self.buf[at, :].astype(f32) + self.box[there, :].astype(f32)).astype(bf16)
            return carry

        lax.fori_loop(0, size // self.tile, run, 0)

    def extra(self):
        partner, keep, give, size, inbox_at = self.levels[2]
        for bit in range(3, self.total_bits):
            copy = pltpu.make_async_remote_copy(
                src_ref=self.rows(keep, size, self.result), dst_ref=self.extra_box.at[bit - 3], send_sem=self.send_sem.at[3 + bit],
                recv_sem=self.recv_sem.at[3 + bit], device_id={"dp": flipped(self.r, bit)}, device_id_type=MESH,
            )
            copy.start()
            copy.wait()
            at = pl.ds(pl.multiple_of(keep, 32), size)
            self.result[at, :] = (self.result[at, :].astype(f32) + self.extra_box[bit - 3].astype(f32)).astype(bf16)

    def tasks(self, done):
        def second():
            self.add(0)
            self.halve(1).start()

        def third():
            self.add(1)
            self.halve(2).start()

        def turn():
            self.add(2, self.result)
            self.extra()
            self.double(2).start()

        def wider():
            self.double(2, True).wait_recv()
            self.double(1).start()

        def widest():
            self.double(1, True).wait_recv()
            self.double(0).start()

        def last():
            self.double(0, True).wait_recv()
            done()

        return [self.halve(0).start, second, third, turn, wider, widest, last]

    def drain(self):
        for level in range(3):
            self.halve(level).wait_send()
            self.double(level).wait_send()


def layer_kernel(
    cfg,
    x_hbm, g_hbm, outp_hbm, in_hbm, tab_hbm, wg_hbm, wu_hbm, wd_hbm, halves_ref, gain1_ref, gain2_ref, short_ref, cond_ref,
    rate_ref, fin_ref, fbias_ref, fout_ref, feat_ref,
    out_hbm, igrad_hbm, big_hbm, proj_hbm, small_hbm, zsum_hbm, *scratch,
):
    ways, seq, own, width, hidden, bits, all_bits = cfg
    (
        xf, gf, outt, proj, mixf, query, kv, squash, kern, mixed, hat, arg, in_t, tab, n1o, masks, cols, prow, frow,
        pieces, gains, gaincol, stat1, sig, prod, weights, n2o, mid, gg, ug, tbuf, tin, mbuf, ein,
        gb, rb, rbx, rb2, rbx2, n2own, inv2, rres, resown, pgb, mgb, mgf, pgo, sgr, kgr, sm, smbox, zbox, mom, gsum,
        load_sem, line_send, line_recv, piece_send, piece_recv, gain_send, gain_recv, save_sem,
        fs_send, fs_recv, es_send, es_recv, hs_send, hs_recv, sw_send, sw_recv,
        ar_send, ar_recv, sm_send, sm_recv, z_send, z_recv, mom_send, mom_recv,
    ) = scratch
    lags = 3 * seq // 4
    freq = lags
    block = seq // ways
    z = lax.axis_index("chan")
    r = lax.axis_index("dp")
    side = (2 * z) // ways
    inner = ((z + ways - 1) // ways) * ((2 * ways - 2 - z) // ways)
    group = r % (1 << bits)

    wd, wg, wu = (weights.at[pl.ds(at, size)] for at, size in ((0, hidden), (hidden, width), (hidden + width, width)))

    def own_rows(at):
        return pl.ds(pl.multiple_of(at * own, row_tile), own)

    def token(at):
        return pl.ds(pl.multiple_of(at * block, block), block)

    span = own_rows(z)
    saves = []

    def load(index, src, dst):
        copy = pltpu.make_async_copy(src, dst, load_sem.at[index])
        copy.start()
        return copy

    def save(src, dst):
        copy = pltpu.make_async_copy(src, dst, save_sem.at[len(saves)])
        copy.start()
        saves.append(copy)

    grain = 48
    per_piece = pieces.shape[2] // grain
    x_load = load(0, x_hbm, xf.at[span])
    g_load = load(1, g_hbm, gf.at[span])
    in_load = load(2, in_hbm, in_t)

    def piece_from(i):
        at = group * per_piece + i
        return outp_hbm.at[
            pl.ds(pl.multiple_of((at % (own // grain)) * grain, row_tile), grain),
            pl.ds(pl.multiple_of((at // (own // grain)) * 128, 128), 128)]

    piece_loads = [load(8 + i, piece_from(i), pieces.at[group, z, pl.ds(i * grain, grain)]) for i in range(per_piece)]
    tab_load = load(3, tab_hbm, tab)
    weight_loads = [load(4, wg_hbm, wg), load(5, wu_hbm, wu), load(6, wd_hbm, wd)]
    barrier = pltpu.get_barrier_semaphore()
    peers = [{"chan": (z + s) % ways} for s in range(1, ways)] + [{"dp": flipped(r, b)} for b in range(all_bits)]
    for peer in peers:
        pl.semaphore_signal(barrier, inc=1, device_id=peer, device_id_type=MESH)
    pl.semaphore_wait(barrier, len(peers))

    def cut(buf):
        return lambda shard, part: buf.at[own_rows(shard), token(part)]

    in_line, g_line, mix_line = (
        Line(cut(buf), line_send.at[i], line_recv.at[i], z, ways) for i, buf in enumerate((xf, gf, mixf)))

    class Direct:
        def __init__(self, view_src, view_dst, send, recv):
            self.view_src, self.view_dst, self.send, self.recv = view_src, view_dst, send, recv

        def copy(self, s, arriving):
            there = (z + s) % ways
            src = (z + ways - s) % ways
            dst = self.view_dst(src if arriving else z)
            return pltpu.make_async_remote_copy(
                src_ref=dst if arriving else self.view_src(there), dst_ref=dst, send_sem=self.send.at[s],
                recv_sem=self.recv.at[s], device_id={"chan": there}, device_id_type=MESH,
            )

        def start(self, wanted=None):
            for s in range(1, ways):
                if wanted is None:
                    self.copy(s, False).start()
                else:
                    @pl.when(wanted((z + s) % ways))
                    def _():
                        self.copy(s, False).start()

        def wait_recv(self):
            for s in range(1, ways):
                self.copy(s, True).wait_recv()

        def drain(self):
            for s in range(1, ways):
                self.copy(s, False).wait_send()

    gain_msg = Direct(lambda to: gains.at[z], lambda at: gains.at[at], gain_send, gain_recv)
    piece_msg = Direct(lambda to: pieces.at[group, z], lambda at: pieces.at[group, at], piece_send, piece_recv)

    gains[z] = jnp.zeros(gains.shape[1:], f32)
    gains[z, 0:1, 0:own] = gain1_ref[...]
    gains[z, 1:2, 0:own] = gain2_ref[...]
    gain_msg.start()
    x_load.wait()
    in_line.send_own()

    def inside(at):
        return jnp.logical_and(at > 0, at < ways - 1)

    def early(there):
        return jnp.logical_or(inside(there), inner == 0)

    for copy in piece_loads:
        copy.wait()
    piece_msg.start(early)

    line_at = lax.broadcasted_iota(jnp.int32, (1, seq), 1)
    split, valid = halves_ref[0, 0], halves_ref[0, 1]
    masks[0:1, :] = jnp.where(line_at < split, 1.0, 0.0)
    masks[1:2, :] = jnp.where(jnp.logical_and(line_at >= split, line_at < valid), 1.0, 0.0)
    masks[2:3, :] = masks[0:1, :] + masks[1:2, :]
    prow[...] = jnp.zeros(prow.shape, f32)
    for i in range(3):
        for j in range(3):
            prow[3 * i + j : 3 * i + j + 1, 0:own] = short_ref[i, j : j + 1, :]
    prow[9:12, 0:own] = cond_ref[...]
    prow[12:13, 0:own] = rate_ref[...]
    prow[64:128, 0:own] = fout_ref[...]
    cols[...] = prow[...].T[0:own, :]
    frow[...] = jnp.zeros(frow.shape, f32)
    frow[0 : fin_ref.shape[0], :] = fin_ref[...]
    frow[fin_ref.shape[0] : fin_ref.shape[0] + 1, :] = fbias_ref[...]
    g_load.wait()
    gf[span, :] = (gf[span, :].astype(f32) * masks[2:3, :]).astype(bf16)

    arg[...] = tn(frow[...], feat_ref[...], highest)
    kern[...] = nn(cols[:, 64:128], jnp.sin(arg[...]), highest)

    gain_msg.wait_recv()
    eye = lax.broadcasted_iota(jnp.int32, (own, gains.shape[2]), 0) == lax.broadcasted_iota(
        jnp.int32, (own, gains.shape[2]), 1)
    for s in range(ways):
        for which in range(2):
            row = gains[s, which : which + 1, :]
            gaincol[s * own : (s + 1) * own, which : which + 1] = jnp.sum(jnp.where(eye, row, 0.0), axis=1, keepdims=True)
    in_load.wait()

    def moments(values):
        centre = jnp.sum(values, axis=0, keepdims=True) * (1.0 / width)
        spread = jnp.sum(values * values, axis=0, keepdims=True) * (1.0 / width) - centre * centre
        return centre, lax.rsqrt(spread + norm_eps)

    def in_order(index):
        return side * index + (1 - side) * (ways - 1 - index)

    def norm1(q):
        at = token(q)
        values = xf[:, at].astype(f32)
        centre, inverse = moments(values)
        stat1[0:1, at] = centre
        stat1[1:2, at] = inverse
        low = ((values - centre) * inverse * gaincol[:, 0:1]).astype(bf16)
        n1o[:, at] = low
        proj[:, at] = nn(in_t[...], low)

    for index in range(ways):
        in_line.short_way(index)
        if index < 2:
            in_line.long_way(index)
    for index in range(ways):
        if index + 2 < ways:
            in_line.long_way(index + 2)
        in_line.take(index)
        norm1(in_order(index))
    g_line.send_own(inner == 0)

    piece_sends = []

    def piece_step(bit, held, slot):
        batch = []
        for i, piece in enumerate(held):
            def make(which, slot=slot + i):
                return pltpu.make_async_remote_copy(
                    src_ref=pieces.at[which], dst_ref=pieces.at[which], send_sem=piece_send.at[slot],
                    recv_sem=piece_recv.at[slot], device_id={"dp": flipped(r, bit)}, device_id_type=MESH,
                )
            make(piece).start()
            batch.append((make, piece))
            piece_sends.append((make, piece))

        def finish():
            for make, piece in batch:
                make(flipped(piece, bit)).wait_recv()
        return finish, held + [flipped(piece, bit) for piece in held], slot + len(held)

    tab_load.wait()

    lane = lax.broadcasted_iota(jnp.int32, (row_tile, seq), 1)
    place = lane.astype(f32)
    half1, half2 = masks[0:1, :], masks[1:2, :]

    def back(values, steps):
        if steps == 0:
            return values
        return jnp.where(lane >= steps, pltpu.roll(values, steps, 1), 0.0)

    def ahead(values, steps):
        if steps == 0:
            return values
        return jnp.where(lane < seq - steps, pltpu.roll(values, seq - steps, 1), 0.0)

    def row_at(j, i):
        return pl.ds(pl.multiple_of(j * own + i * row_tile, row_tile), row_tile)

    def decay_of(tap):
        return jnp.exp(-tap[:, 12:13] * place) * (1.0 / math.sqrt(seq))

    def mix_rows(i, carry):
        here = row_at(0, i)
        tap = cols[here, :]
        outs = []
        for j in range(3):
            part = proj[row_at(j, i), :]
            outs.append(sum(tap[:, 3 * k + j : 3 * k + j + 1] * back(part, k) for k in range(3)))
        query[here, :] = outs[0]
        kv[here, :] = outs[1]
        kv[row_at(1, i), :] = outs[2]
        cond = sum(tap[:, 9 + k : 10 + k] * back(outs[2], k) for k in range(3))
        bent = jnp.tanh(cond)
        squash[here, :] = bent
        filt = (kern[here, :] + bent) * decay_of(tap)
        kern[here, :] = filt
        source = outs[1] * outs[2]
        sig[row_at(0, i), :] = jnp.where(lane < lags, filt, 0.0).astype(bf16)
        sig[row_at(1, i), :] = (source * half1).astype(bf16)
        sig[row_at(2, i), :] = (source * half2).astype(bf16)
        return carry

    lax.fori_loop(0, own // row_tile, mix_rows, 0)
    def freq_at(j):
        return (pl.ds(pl.multiple_of(j * lane_tile, lane_tile), lane_tile),
                pl.ds(pl.multiple_of(freq + j * lane_tile, lane_tile), lane_tile))

    def freq_tile(j, carry):
        re_at, im_at = freq_at(j)
        re = nn(sig[...], tab[:, re_at])
        im = nn(sig[...], tab[:, im_at])
        hat[:, re_at] = re.astype(bf16)
        hat[:, im_at] = im.astype(bf16)
        kr, ki = re[:own], im[:own]
        for h in range(2):
            sr, si = re[own * (h + 1) : own * (h + 2)], im[own * (h + 1) : own * (h + 2)]
            prod[own * h : own * (h + 1), re_at] = (kr * sr - ki * si).astype(bf16)
            prod[own * h : own * (h + 1), im_at] = (kr * si + ki * sr).astype(bf16)
        return carry

    lax.fori_loop(0, freq // lane_tile, freq_tile, 0)
    g_line.send_own(inner == 1)
    piece_msg.start(lambda there: jnp.logical_not(early(there)))

    def time_tile(j, carry):
        at = token(j)
        both = nt(prod[0 : 2 * own, :], tab[at, :])
        total = (both[:own] * masks[0:1, at] + both[own:] * masks[1:2, at]) * (1.0 / freq)
        mixed[:, at] = total
        mixf[span, at] = (query[:, at] * total).astype(bf16)
        return carry

    lax.fori_loop(0, ways, time_tile, 0)

    mix_line.send_own()
    piece_msg.wait_recv()
    held, slot = [group], ways
    for bit in reversed(range(bits)):
        finish, held, slot = piece_step(bit, held, slot)
        if bit == bits - 1:
            for index in range(ways):
                g_line.short_way(index)
        finish()
    next_hops, last_hops = range(1, 2), range(2, ways - 1)
    mix_line.long_way(0, next_hops)
    mix_line.short_way(0)
    mix_line.long_way(0, last_hops)
    for s in range(ways):
        for block_at in range(own * width // 128 // grain):
            piece, inside_at = divmod(block_at, per_piece)
            column, down = divmod(block_at, own // grain)
            outt[s * own + down * grain : s * own + (down + 1) * grain, 128 * column : 128 * column + 128] = pieces[
                piece, s, inside_at * grain : (inside_at + 1) * grain, :]
    for copy in weight_loads:
        copy.wait()
    g_line.long_way(0)
    mix_line.short_way(1)
    mix_line.long_way(1)
    g_line.long_way(1)
    for index in range(2, ways):
        mix_line.short_way(index)

    half_block = block // 2

    def half_token(at, sub):
        return pl.ds(pl.multiple_of(at * block + sub * half_block, half_block), half_block)

    f_sum = LineSum(
        lambda dest, sub: tbuf.at[:, half_token(dest, sub)],
        lambda way, k, sub: tin.at[way, k, :, pl.ds(sub * half_block, half_block)],
        fs_send, fs_recv, z, ways, 2)
    e_sum = LineSum(
        lambda dest, sub: mbuf.at[own_rows(dest), token(sub)],
        lambda way, k, sub: ein.at[way, k, :, token(sub)],
        es_send, es_recv, z, ways, ways)

    def by_end(index):
        return (ways - 1 - index, index)

    halves_of = [(sub, sub) for sub in range(2)]
    plain_order = [(sub, sub) for sub in range(ways)]

    def tiles(count, fn):
        def run(j, carry):
            fn(pl.ds(pl.multiple_of(j * lane_tile, lane_tile), lane_tile))
            return carry
        lax.fori_loop(0, count // lane_tile, run, 0)

    def forward(q):
        at = token(q)
        rres[...] = xf[:, at].astype(f32) + nn(outt[...], mixf[:, at])
        resown[:, at] = rres[span, :]
        centre, inverse = moments(rres[...])
        n2o[:, at] = ((rres[...] - centre) * inverse * gaincol[:, 1:2]).astype(bf16)

        @pl.when(q == z)
        def _():
            n2own[...] = (rres[...] - centre) * inverse
            inv2[0:1, :] = inverse

        def hidden_tile(fs):
            low = n2o[:, at]
            gate = tn(wg[:, fs], low)
            up = tn(wu[:, fs], low)
            bent = jax.nn.sigmoid(gate)
            act = gate * bent
            mid[fs, at] = (act * up).astype(bf16)
            gg[fs, at] = (up * bent * (1.0 + gate * (1.0 - bent))).astype(bf16)
            ug[fs, at] = act.astype(bf16)

        tiles(hidden, hidden_tile)

        def mlp_tile(ds):
            mbuf[ds, at] = tn(wd[:, ds], mid[:, at]).astype(bf16)

        tiles(width, mlp_tile)

    def backward(q):
        at = token(q)

        def back_tile(fs):
            grad = nn(wd[fs, :], gf[:, at])
            gg[fs, at] = (grad * gg[fs, at].astype(f32)).astype(bf16)
            ug[fs, at] = (grad * ug[fs, at].astype(f32)).astype(bf16)

        tiles(hidden, back_tile)

        def term_tile(ds):
            tbuf[ds, at] = (nn(wg[ds, :], gg[:, at]) + nn(wu[ds, :], ug[:, at])).astype(bf16)

        tiles(width, term_tile)

    def turn_of(index):
        if index == ways - 2:
            return index + inner
        if index == ways - 1:
            return index - inner
        return index

    for index in range(ways):
        if 0 < index < ways - 1:
            mix_line.long_way(index + 1)
            g_line.long_way(index + 1)
        q = in_order(turn_of(index))
        mix_line.take(index)
        forward(q)
        if index == 0:
            for k in range(ways - 1):
                e_sum.first(k, by_end(0))
        if index == 2:
            f_sum.near(0, halves_of[1])
        if index == 3:
            f_sum.far(0, halves_of[1])
            f_sum.near(1, halves_of[0])
        g_line.take(index)
        backward(q)
        if index < ways - 1:
            for sub in halves_of:
                f_sum.first(index, sub)
        if index == 1:
            f_sum.near(0, halves_of[0])
        if index == 2:
            f_sum.far(0, halves_of[0])
    f_sum.near(1, halves_of[1])
    for k in range(ways - 1):
        e_sum.first(k, by_end(1))

    def weight_grad(lhs, rhs, place_at):
        def run(j, carry):
            at = pl.ds(pl.multiple_of(j * lane_tile, lane_tile), lane_tile)
            gb[pl.ds(pl.multiple_of(place_at + j * lane_tile, lane_tile), lane_tile), :] = nt(
                lhs[at, :], rhs[...]).astype(bf16)
            return carry
        lax.fori_loop(0, lhs.shape[0] // lane_tile, run, 0)

    def weight_grads():
        weight_grad(mid, gf, 0)
        weight_grad(n2o, gg, hidden)
        weight_grad(n2o, ug, hidden + width)

    pl.when(inner == 1)(weight_grads)
    big = RowSum(gb, weights, rb, rbx, ar_send.at[0], ar_recv.at[0], r, all_bits)
    big_tasks = big.tasks(lambda: save(weights, big_hbm))

    rres[...] = tbuf[:, token(z)].astype(f32)
    for sub in range(2):
        for way in (0, 1):
            f_sum.take(way, sub, rres.at[:, pl.ds(sub * half_block, half_block)])
    upstream = rres[...] * gaincol[:, 1:2]
    normed = n2own[...]
    plain = jnp.sum(upstream, axis=0, keepdims=True) * (1.0 / width)
    cross = jnp.sum(upstream * normed, axis=0, keepdims=True) * (1.0 / width)
    pgb[...] = (gf[:, token(z)].astype(f32) + inv2[0:1, :] * (upstream - plain - normed * cross)).astype(bf16)
    mgb[...] = tn(outt[...], pgb[...]).astype(bf16)
    swap_mix = Direct(lambda to: mgb.at[own_rows(to)], lambda at: mgf.at[:, token(at)], sw_send.at[0], sw_recv.at[0])
    swap_proj = Direct(lambda to: pgb.at[own_rows(to)], lambda at: pgo.at[:, token(at)], sw_send.at[1], sw_recv.at[1])
    swap_mix.start()
    swap_proj.start()
    mgf[:, token(z)] = mgb[span, :]
    pgo[:, token(z)] = pgb[span, :]
    ones = jnp.ones((8, block), bf16)
    gsum[ways] = nt(ones, (rres[...] * normed).astype(bf16))

    for index in range(2, ways):
        for k in range(ways - 1):
            e_sum.first(k, by_end(index))
    pl.when(inner == 0)(weight_grads)
    big_tasks.pop(0)()
    swap_mix.wait_recv()

    def grad_rows(i, carry):
        here = row_at(0, i)
        down = mgf[here, :].astype(f32) * query[here, :]
        sig[row_at(0, i), :] = (down * half1).astype(bf16)
        sig[row_at(1, i), :] = (down * half2).astype(bf16)
        return carry

    lax.fori_loop(0, own // row_tile, grad_rows, 0)

    def grad_freq(j, carry):
        re_at, im_at = freq_at(j)
        re = nn(sig[0 : 2 * own, :], tab[:, re_at])
        im = nn(sig[0 : 2 * own, :], tab[:, im_at])
        hr, hi = hat[:, re_at].astype(f32), hat[:, im_at].astype(f32)
        kr, ki = hr[:own], hi[:own]
        kg_re, kg_im = 0.0, 0.0
        for h in range(2):
            mr, mi = re[own * h : own * (h + 1)], im[own * h : own * (h + 1)]
            sr, si = hr[own * (h + 1) : own * (h + 2)], hi[own * (h + 1) : own * (h + 2)]
            prod[own * h : own * (h + 1), re_at] = (kr * mr + ki * mi).astype(bf16)
            prod[own * h : own * (h + 1), im_at] = (kr * mi - ki * mr).astype(bf16)
            kg_re = kg_re + sr * mr + si * mi
            kg_im = kg_im + sr * mi - si * mr
        prod[2 * own : 3 * own, re_at] = kg_re.astype(bf16)
        prod[2 * own : 3 * own, im_at] = kg_im.astype(bf16)
        return carry

    lax.fori_loop(0, freq // lane_tile, grad_freq, 0)
    big_tasks.pop(0)()

    def grad_time(j, carry):
        at = token(j)
        all3 = nt(prod[...], tab[at, :])
        sgr[:, at] = (all3[:own] * masks[0:1, at] + all3[own : 2 * own] * masks[1:2, at]) * (1.0 / freq)
        kgr[:, at] = all3[2 * own :] * (1.0 / freq)
        return carry

    lax.fori_loop(0, ways, grad_time, 0)

    def chain_rows(i, carry):
        here = row_at(0, i)
        tap = cols[here, :]
        stat = jnp.zeros((row_tile, 128), f32)
        column = lax.broadcasted_iota(jnp.int32, (row_tile, 128), 1)

        def note(stat, index, values):
            return jnp.where(column == index, jnp.sum(values, axis=1, keepdims=True), stat)

        key, value = kv[here, :], kv[row_at(1, i), :]
        kgrad = jnp.where(lane < lags, kgr[here, :], 0.0)
        base_grad = kgrad * decay_of(tap)
        kgr[here, :] = base_grad
        stat = note(stat, 12, -kgrad * kern[here, :] * place)
        bent = squash[here, :]
        cond_grad = base_grad * (1.0 - bent * bent)
        sgrad = sgr[here, :]
        value_grad = sgrad * key
        for k in range(3):
            moved = ahead(cond_grad, k)
            stat = note(stat, 9 + k, moved * value)
            value_grad = value_grad + tap[:, 9 + k : 10 + k] * moved
        branch = (mgf[here, :].astype(f32) * mixed[here, :], sgrad * value, value_grad)
        for j in range(3):
            part = proj[row_at(j, i), :]
            total = 0.0
            for k in range(3):
                moved = ahead(branch[j], k)
                stat = note(stat, 3 * k + j, moved * part)
                total = total + tap[:, 3 * k + j : 3 * k + j + 1] * moved
            sig[row_at(j, i), :] = total.astype(bf16)
        sm[here, :] = stat
        return carry

    lax.fori_loop(0, own // row_tile, chain_rows, 0)

    h_sum = LineSum(
        lambda dest, sub: tbuf.at[own_rows(dest), token(sub)],
        lambda way, k, sub: tin.at[way, k, own_rows(sub), :],
        hs_send, hs_recv, z, ways, ways)
    f_sum.drain()
    mom_msg = Direct(lambda to: mom.at[z], lambda at: mom.at[at], mom_send, mom_recv)

    def in_back(tile):
        at = token(tile)
        rres[...] = tn(in_t[...], sig[:, at])
        tbuf[:, at] = rres[...].astype(bf16)
        h_sum.first(0, plain_order[tile])
        normed = (xf[:, at].astype(f32) - stat1[0:1, at]) * stat1[1:2, at]
        upstream = rres[...] * gaincol[:, 0:1]
        mom[z, 0:1, at] = jnp.sum(upstream, axis=0, keepdims=True)
        mom[z, 1:2, at] = jnp.sum(upstream * normed, axis=0, keepdims=True)
        gsum[tile] = nt(ones, (rres[...] * normed).astype(bf16))

    gb2 = gg.at[0 : 4 * own, 0:width]
    sum2 = mid.at[0 : 4 * own, 0:width]

    def proj_grad(lhs, rhs, place_at):
        gb2[place_at : place_at + lhs.shape[0], :] = nt(lhs[...], rhs[...]).astype(bf16)

    two = RowSum(gb2, sum2, rb2, rbx2, ar_send.at[1], ar_recv.at[1], r, all_bits)
    two_tasks = two.tasks(lambda: save(sum2, proj_hbm))

    def small_copy(b):
        return pltpu.make_async_remote_copy(
            src_ref=sm, dst_ref=smbox.at[b], send_sem=sm_send.at[b], recv_sem=sm_recv.at[b],
            device_id={"dp": flipped(r, b)}, device_id_type=MESH,
        )

    def small_step(b):
        small_copy(b).wait()
        sm[...] += smbox[b]
        if b + 1 < all_bits:
            small_copy(b + 1).start()

    def near(summer, k, index):
        summer.near(k, by_end(index) if summer is e_sum else plain_order[index])

    def far(summer, k, index):
        summer.far(k, by_end(index) if summer is e_sum else plain_order[index])

    total = rres.at[0:own, :]

    def output_part(tile):
        at = token(tile)
        total[...] = mbuf[span, at].astype(f32)
        for way in (0, 1):
            e_sum.take(way, tile, total)
        resown[:, at] = (resown[:, at] + total[...]) * masks[2:3, at]
        save(resown.at[:, at], out_hbm.at[:, at])

    def input_part(tile):
        at = token(tile)
        total[...] = tbuf[span, at].astype(f32)
        for way in (0, 1):
            h_sum.take(way, tile, total)
        sums = sum(mom[s, :, at] for s in range(ways)) * (1.0 / width)
        inverse = stat1[1:2, at]
        normed = (xf[span, at].astype(f32) - stat1[0:1, at]) * inverse
        upstream = total[...] * gaincol[span, 0:1]
        sgr[:, at] = pgo[:, at].astype(f32) + inverse * (upstream - sums[0:1, :] - normed * sums[1:2, :])
        save(sgr.at[:, at], igrad_hbm.at[:, at])

    for index in range(ways):
        near(e_sum, 0, index)
    in_back(0)
    in_back(1)
    swap_proj.wait_recv()
    proj_grad(sig, n1o, 0)
    proj_grad(pgo, mixf, 3 * own)
    two_tasks.pop(0)()
    near(h_sum, 0, 0)
    in_back(2)
    near(h_sum, 0, 1)
    in_back(3)
    for k in range(1, ways - 1):
        for tile in range(ways):
            h_sum.first(k, plain_order[tile])
    mom_msg.start()
    for index in range(ways):
        near(e_sum, 1, index)
    for index in range(ways):
        far(e_sum, 0, index)
    near(h_sum, 0, 2)
    two_tasks.pop(0)()
    far(h_sum, 0, 0)
    big_tasks.pop(0)()

    wave_grad = tn(cols[:, 64:128], kgr[...], highest) * jnp.cos(arg[...])
    sm[0:own, 64:128] = nt(kgr[...], jnp.sin(arg[...]), highest)
    near(h_sum, 0, 3)
    far(h_sum, 0, 1)
    sm[own : own + 64, 0:64] = nt(feat_ref[...], wave_grad, highest)
    sm[own : own + 64, 64:128] = jnp.zeros((64, 64), f32)
    sm[own + 64 :, :] = jnp.zeros((16, 128), f32)
    for b in range(width // 128):
        lanes = slice(128 * b, 128 * b + 128)
        sm[own + 64 + b : own + 65 + b, :] = sum(gsum[tile, 0:1, lanes] for tile in range(ways))
        sm[own + 72 + b : own + 73 + b, :] = gsum[ways, 0:1, lanes]
    small_copy(0).start()
    far(h_sum, 0, 2)
    two_tasks.pop(0)()
    near(h_sum, 1, 0)
    far(h_sum, 0, 3)
    small_step(0)
    near(h_sum, 1, 1)
    big_tasks.pop(0)()
    for tile in range(ways):
        output_part(tile)
    near(h_sum, 1, 2)
    two_tasks.pop(0)()
    small_step(1)
    near(h_sum, 1, 3)
    two_tasks.pop(0)()
    big_tasks.pop(0)()
    for b in range(2, all_bits):
        small_step(b)
    z_msg = Direct(lambda to: zbox.at[z], lambda at: zbox.at[at], z_send, z_recv)
    zbox[z] = sm[own:, :]
    z_msg.start()
    save(sm, small_hbm)
    mom_msg.wait_recv()
    input_part(0)
    two_tasks.pop(0)()
    input_part(1)
    big_tasks.pop(0)()
    two_tasks.pop(0)()
    input_part(2)
    big_tasks.pop(0)()
    z_msg.wait_recv()
    zsum = zbox[0]
    for s in range(1, ways):
        zsum = zsum + zbox[s]
    zout = kern.at[0 : zsum.shape[0], 0:128]
    zout[...] = zsum
    save(zout, zsum_hbm)
    input_part(3)

    for line in (in_line, g_line, mix_line, e_sum, h_sum, gain_msg, piece_msg, swap_mix, swap_proj, mom_msg, z_msg, big, two):
        line.drain()
    for make, piece in piece_sends:
        make(piece).wait_send()
    for copy in saves:
        copy.wait()


def layer(cfg, x_own, g_own, out_t, in_t, table, w_gate, w_up, w_down, halves, gain1, gain2, short_taps, cond_taps, rates,
          filter_in, filter_bias, filter_out, feats):
    ways, seq, own, width, hidden, bits, all_bits = cfg
    period = 3 * seq // 2
    block = seq // ways
    big_rows = hidden + 2 * width
    assert hidden == width
    held = dict(
        xf=((width, seq), bf16), gf=((width, seq), bf16), outt=((width, width), bf16), proj=((3 * own, seq), f32),
        mixf=((width, seq), bf16), query=((own, seq), f32), kv=((2 * own, seq), f32), squash=((own, seq), f32), kern=((own, seq), f32),
        mixed=((own, seq), f32), hat=((3 * own, period), bf16), arg=((64, seq), f32), in_t=((3 * own, width), bf16),
        tab=((seq, period), bf16), n1o=((width, seq), bf16), masks=((8, seq), f32), cols=((own, 128), f32),
        prow=((128, 256), f32), frow=((64, 64), f32),
        pieces=((1 << bits, ways, own * width // 128 // (1 << bits), 128), bf16), gains=((ways, 8, 256), f32),
        gaincol=((width, 128), f32), stat1=((8, seq), f32), sig=((3 * own, seq), bf16), prod=((3 * own, period), bf16),
        weights=((big_rows, width), bf16), n2o=((width, seq), bf16),
        mid=((hidden, seq), bf16), gg=((hidden, seq), bf16), ug=((hidden, seq), bf16), tbuf=((width, seq), bf16),
        tin=((2, ways - 1, width, block), bf16), mbuf=((width, seq), bf16), ein=((2, ways - 1, own, seq), bf16),
        gb=((big_rows, width), bf16), rb=((big_rows * 7 // 8, width), bf16),
        rbx=((max(all_bits - 3, 1), big_rows // 8 if all_bits > 3 else 16, width), bf16),
        rb2=((4 * own * 7 // 8, width), bf16),
        rbx2=((max(all_bits - 3, 1), 4 * own // 8 if all_bits > 3 else 16, width), bf16),
        n2own=((width, block), f32), inv2=((8, block), f32), rres=((width, block), f32), resown=((own, seq), f32),
        pgb=((width, block), bf16), mgb=((width, block), bf16), mgf=((own, seq), bf16), pgo=((own, seq), bf16),
        sgr=((own, seq), f32), kgr=((own, seq), f32), sm=((own + 80, 128), f32),
        smbox=((all_bits, own + 80, 128), f32), zbox=((ways, 80, 128), f32),
        mom=((ways, 8, seq), f32), gsum=((ways + 1, 8, width), f32),
    )
    hops = (3, 2, ways - 1, ways)
    sems = dict(
        load_sem=(16,), line_send=hops, line_recv=hops, piece_send=(ways + (1 << bits),), piece_recv=(ways + (1 << bits),),
        gain_send=(ways,), gain_recv=(ways,), save_sem=(24,), fs_send=(2, ways, 2), fs_recv=(2, ways, 2),
        es_send=(2, ways, ways), es_recv=(2, ways, ways), hs_send=(2, ways, ways), hs_recv=(2, ways, ways),
        sw_send=(2, ways), sw_recv=(2, ways), ar_send=(2, 3 + max(all_bits, 3)), ar_recv=(2, 3 + max(all_bits, 3)),
        sm_send=(all_bits,), sm_recv=(all_bits,), z_send=(ways,), z_recv=(ways,), mom_send=(ways,), mom_recv=(ways,),
    )
    here = pl.BlockSpec(memory_space=pltpu.VMEM)
    there = pl.BlockSpec(memory_space=pl.ANY)
    outs = [
        ((own, seq), f32), ((own, seq), f32), ((big_rows, width), bf16), ((4 * own, width), bf16),
        ((own + 80, 128), f32), ((80, 128), f32),
    ]
    return pl.pallas_call(
        functools.partial(layer_kernel, cfg),
        out_shape=[jax.ShapeDtypeStruct(s, t) for s, t in outs],
        in_specs=[there] * 8 + [pl.BlockSpec(memory_space=pltpu.SMEM)] + [here] * 9,
        out_specs=[there] * len(outs),
        scratch_shapes=[pltpu.VMEM(s, t) for s, t in held.values()] + [
            pltpu.SemaphoreType.DMA(s) for s in sems.values()],
        compiler_params=pltpu.CompilerParams(collective_id=0, has_side_effects=True, vmem_limit_bytes=64 << 20),
    )(x_own, g_own, out_t, in_t, table, w_gate, w_up, w_down, halves, gain1, gain2, short_taps, cond_taps, rates,
      filter_in, filter_bias, filter_out, feats)


def local(
    hidden_in, halves, norm1_gain, in_proj, short_taps, cond_taps, filter_in, filter_bias,
    filter_out, decay_rate, out_proj, norm2_gain, w_gate, w_up, w_down, out_grad,
):
    seq, own = hidden_in.shape[1], hidden_in.shape[2]
    ways, rows = lax.axis_size("chan"), lax.axis_size("dp")
    width, hidden = own * ways, w_gate.shape[1]
    z = lax.axis_index("chan")
    all_bits = rows.bit_length() - 1
    cfg = (ways, seq, own, width, hidden, 3, all_bits)
    count = filter_in.shape[0]
    feat_np = np.concatenate([
        band_features(seq, count), np.ones((1, seq), np.float32), np.zeros((63 - count, seq), np.float32)])
    table = jnp.asarray(wave_matrix(seq).astype(np.float32)).astype(bf16)

    output, input_grad, big, two, small, zsum = layer(
        cfg, hidden_in[0].T, out_grad[0].T, out_proj.T, in_proj.transpose(1, 2, 0).reshape(3 * own, width), table,
        w_gate, w_up, w_down, halves, norm1_gain[None], norm2_gain[None], short_taps, cond_taps, decay_rate[None],
        filter_in, filter_bias[None], filter_out, jnp.asarray(feat_np))

    stats = small[:own].T
    gain_sums = zsum[64:].reshape(2, 8 * 128)
    mine = lax.dynamic_slice_in_dim(gain_sums, z * own, own, 1)
    in_grad = two[: 3 * own].astype(f32).reshape(3, own, width).transpose(2, 0, 1)
    out_grad_sum = two[3 * own :].astype(f32).T
    return (
        output.T[None], input_grad.T[None], mine[0], in_grad, stats[:9].reshape(3, 3, own),
        stats[9:12], zsum[:count, :64], zsum[count, :64], stats[64:128], stats[12], out_grad_sum, mine[1],
        big[hidden : hidden + width].astype(f32), big[hidden + width :].astype(f32), big[:hidden].astype(f32),
    )


def solution(mesh):
    rows, cols = P("dp", None, "chan"), P(None, "chan")
    in_specs = (
        rows, P("dp", None), P("chan"), P(None, None, "chan"), P(None, None, "chan"), cols, P(), P(),
        cols, P("chan"), cols, P("chan"), cols, cols, P("chan", None), rows,
    )
    out_specs = (
        rows, rows, P("chan"), P(None, None, "chan"), P(None, None, "chan"), cols, P(), P(),
        cols, P("chan"), cols, P("chan"), cols, cols, P("chan", None),
    )
    return jax.shard_map(local, mesh=mesh, in_specs=in_specs, out_specs=out_specs, check_vma=False)
```

time: 459 us -> 215 us (0.47)
  the two profiles are of different devices: /device:TPU:0 before, /device:TPU:9 now
where the time goes in v3:
time: 215 us
  Pallas kernels  199 us (93%)
  local copies, waits for them, and re-layouts  8.21 us (4%)
  other arithmetic  7.41 us (3%)
    pallas_call x1, Pallas kernels, layer(): pl.pallas_call(functools.partial(layer_kernel, cfg), out_shape=[jax.Shape...  199 us
    convert_element_type x1, other arithmetic, local(): big[:hidden].astype(f32)  5.21 us

profile of v3, /device:TPU:9, one launch (start us, length us, event | category | flops | bytes accessed | tf_op | source)
XLA Modules:
  0.0 215.1 jit_solution(6202179003304595792)
XLA Ops:
  0.7 198.8 %shard_map.289 = (f32[192,1024]{1,0:T(8,128)}, f32[192,1024]{1,0:T(8,128)}, bf16[2304,768]{1,0:T(8,128)(2,1)}, bf16[768,768]{1,0:T(8,128)(2,1)}, f32[272,128]{1,0:T(8,128)}, /*index=5*/f32[80,128]{1,0:T(8,128)}) custom-call(bf16[192,1024]{1,0:T(8,128)(2,1)} %bitcast.38, bf16[192,1024]{1,0:T(8,128)(2,1)} %bitcast.39, bf16[192,768]{1,0:T(8,128)(2,1)} %bitcast.40, ...), custom_call_target="tpu_custom_call" | custom-call | tf_op jit(solution)/shard_map/pallas_call | solution.py:1010
  199.4 0.7 slice.45
  200.1 0.6 fusion
  200.8 0.9 slice_bitcast_fusion
  201.7 0.1 slice.62
  201.8 0.7 copy.38
  202.5 0.1 slice.61
  202.6 0.7 copy.37
  203.3 0.1 copy.36
  203.3 0.6 reshape.46
  204.0 0.7 slice_reduce_fusion
  204.7 0.0 copy-start.3
  204.7 0.0 copy-start
  204.7 5.2 %slice_convert_fusion = (f32[768,768]{1,0:T(8,128)}, f32[768,768]{1,0:T(8,128)}, f32[768,768]{1,0:T(8,128)}) fusion(bf16[2304,768]{1,0:T(8,128)(2,1)} %get-tuple-element.26), kind=kLoop, calls=%fused_computation.1 | loop fusion | flops 1769472 | bytes 10616832 | tf_op jit(solution)/shard_map/convert_element_type | solution.py:1050
  209.9 0.0 copy-done.3
  209.9 0.6 slice.51
  210.5 0.5 slice_bitcast_fusion.1
  211.0 0.0 copy-done
  211.1 0.1 slice.47
  211.1 0.0 copy-start.2
  211.1 1.4 convert_bitcast_fusion
  212.5 0.0 copy-start.1
  212.5 0.9 convert_bitcast_fusion.1
  213.3 0.0 copy-done.2
  213.3 0.9 copy.41
  214.2 0.0 copy-done.1
  214.2 0.9 copy.42
  (1 shorter events, 0.0 us)
Async XLA Ops:
  204.7 5.2 %copy-start.3 = (f32[80,128]{1,0:T(8,128)S(1)}, f32[80,128]{1,0:T(8,128)}, u32[]{:S(2)}) copy-start(f32[80,128]{1,0:T(8,128)} %get-tuple-element.23) | copy-start | bytes 122884
  204.7 6.3 %copy-start = (bf16[768,768]{1,0:T(8,128)(2,1)S(1)}, bf16[768,768]{1,0:T(8,128)(2,1)}, u32[]{:S(2)}) copy-start(bf16[768,768]{1,0:T(8,128)(2,1)} %get-tuple-element.24) | copy-start | bytes 3538948
  211.1 2.2 %copy-start.2 = (f32[192,1024]{1,0:T(8,128)S(1)}, f32[192,1024]{1,0:T(8,128)}, u32[]{:S(2)}) copy-start(f32[192,1024]{1,0:T(8,128)} %get-tuple-element.21) | copy-start | bytes 2359300
  212.5 1.7 copy-start.1

commit v4 on v3

--- a/solution.py
+++ b/solution.py
@@ -53,9 +53,16 @@
     return index + (1 << bit) * (1 - 2 * ((index // (1 << bit)) % 2))
 
 
+def both(first, second):
+    if second is True:
+        return first
+    return second if first is True else jnp.logical_and(first, second)
+
+
 class Line:
     def __init__(self, view, send_sem, recv_sem, at, ways):
         self.view, self.send_sem, self.recv_sem, self.at, self.ways = view, send_sem, recv_sem, at, ways
+        self.pending, self.arrived = {}, set()
 
     def copy(self, way, hop, part, shard):
         ref = self.view(shard, part)
@@ -82,28 +89,60 @@
     def far_side(self):
         return (2 * self.at) // self.ways
 
-    def send_own(self, wanted=True):
-        for index in range(self.ways):
+    def launch(self, hop, way, index, wanted, wait_first):
+        part, step = self.order(way, index), 1 - 2 * way
+
+        @pl.when(both(self.sends(way, hop), wanted()))
+        def _():
+            if wait_first:
+                self.copy(way, hop - 1, part, self.at - hop * step).wait_recv()
+            self.copy(way, hop, part, self.at - hop * step).start()
+
+        def left(also):
+            @pl.when(both(both(self.sends(way, hop), wanted()), also))
+            def _():
+                self.copy(way, hop, part, self.at - hop * step).wait_send()
+
+        self.pending.setdefault((hop, way, index), []).append(left)
+
+    def settle(self, hops, indices, wanted=True):
+        for key in [k for k in self.pending if k[0] in hops and k[2] in indices]:
+            before = self.pending.pop(key)
+            for left in before:
+                left(wanted)
+            if wanted is not True:
+                self.pending[key] = [
+                    lambda also, left=left: left(both(jnp.logical_not(wanted), also)) for left in before]
+
+    def send_own(self, indices, wanted, inward=None):
+        for index in indices:
             for way in (0, 1):
-                @pl.when(jnp.logical_and(self.sends(way, 0), wanted))
-                def _():
-                    self.copy(way, 0, self.order(way, index), self.at).start()
-
-    def relay(self, way, index, wanted, hops=None):
-        part, step = self.order(way, index), 1 - 2 * way
+                def ok(way=way):
+                    if inward is None:
+                        return wanted
+                    facing = self.far_side() == way
+                    return both(wanted, facing if inward else jnp.logical_not(facing))
+                self.launch(0, way, index, ok, False)
+
+    def relay(self, way, index, wanted, hops=None, wait_first=True):
         for hop in range(1, self.ways - 1) if hops is None else hops:
-            @pl.when(jnp.logical_and(self.sends(way, hop), wanted))
-            def _():
-                self.copy(way, hop - 1, part, self.at - hop * step).wait_recv()
-                self.copy(way, hop, part, self.at - hop * step).start()
+            self.launch(hop, way, index, wanted, wait_first)
 
     def short_way(self, index):
         for way in (0, 1):
-            self.relay(way, index, self.far_side() == way)
+            self.relay(way, index, lambda way=way: self.far_side() == way)
 
     def long_way(self, index, hops=None):
         for way in (0, 1):
-            self.relay(way, index, self.far_side() != way, hops)
+            self.relay(way, index, lambda way=way: self.far_side() != way, hops, index not in self.arrived)
+
+    def arrive(self, index):
+        self.arrived.add(index)
+        for way in (0, 1):
+            for hop in range(1, self.ways - 1):
+                @pl.when(jnp.logical_and(self.sends(way, hop), self.far_side() != way))
+                def _():
+                    self.copy(way, hop - 1, self.order(way, index), self.at - hop * (1 - 2 * way)).wait_recv()
 
     def take(self, index):
         for way in (0, 1):
@@ -117,18 +156,14 @@
                     self.copy(way, hop, self.order(way, index), self.at - (hop + 1) * (1 - 2 * way)).wait_recv()
 
     def drain(self):
-        for way in (0, 1):
-            for hop in range(self.ways - 1):
-                for part in range(self.ways):
-                    @pl.when(self.sends(way, hop))
-                    def _():
-                        self.copy(way, hop, part, self.at - hop * (1 - 2 * way)).wait_send()
+        self.settle(range(self.ways), range(self.ways))
 
 
 class LineSum:
     def __init__(self, mine, inbox, send_sem, recv_sem, at, ways, subs):
         self.mine, self.inbox, self.send_sem, self.recv_sem = mine, inbox, send_sem, recv_sem
         self.at, self.ways, self.subs = at, ways, subs
+        self.pending = {}
 
     def dest(self, way, k):
         return self.ways - 1 - k if way == 0 else k
@@ -150,14 +185,44 @@
             device_id={"chan": (self.at + step + self.ways) % self.ways}, device_id_type=MESH,
         )
 
-    def first(self, k, sub):
+    def first(self, k, sub, noted=True):
         for way in (0, 1):
-            @pl.when(jnp.logical_and(self.sends(way, k), jnp.logical_not(self.gets(way, k))))
+            def starts(way=way):
+                return jnp.logical_and(self.sends(way, k), jnp.logical_not(self.gets(way, k)))
+
+            @pl.when(starts())
             def _():
                 self.copy(way, k, sub[way]).start()
+            if noted:
+                self.note(way, k, sub[way], starts)
+
+    def note_first(self, k, sub):
+        for way in (0, 1):
+            self.note(way, k, sub[way], lambda way=way: jnp.logical_and(
+                self.sends(way, k), jnp.logical_not(self.gets(way, k))))
+
+    def note(self, way, k, sub, going):
+        def left(also):
+            @pl.when(both(going(), also))
+            def _():
+                self.copy(way, k, sub).wait_send()
+        self.pending.setdefault(k, []).append(left)
+
+    def settle(self, k, wanted=True):
+        before = self.pending.pop(k, [])
+        for left in before:
+            left(wanted)
+        if wanted is not True:
+            self.pending[k] = [
+                lambda also, left=left: left(both(jnp.logical_not(wanted), also)) for left in before]
 
     def onward(self, way, k, sub, wanted):
-        @pl.when(jnp.logical_and(jnp.logical_and(self.sends(way, k), self.gets(way, k)), wanted))
+        def going():
+            return both(jnp.logical_and(self.sends(way, k), self.gets(way, k)), wanted())
+
+        self.note(way, k, sub, going)
+
+        @pl.when(going())
         def _():
             self.copy(way, k, sub).wait_recv()
             mine, inbox = self.mine(self.dest(way, k), sub), self.inbox(way, k, sub)
@@ -166,11 +231,11 @@
 
     def near(self, k, sub):
         for way in (0, 1):
-            self.onward(way, k, sub[way], (2 * self.at) // self.ways == way)
+            self.onward(way, k, sub[way], lambda way=way: (2 * self.at) // self.ways == way)
 
     def far(self, k, sub):
         for way in (0, 1):
-            self.onward(way, k, sub[way], (2 * self.at) // self.ways != way)
+            self.onward(way, k, sub[way], lambda way=way: (2 * self.at) // self.ways != way)
 
     def take(self, way, sub, total):
         k = self.ways - 1 - self.at if way == 0 else self.at
@@ -181,16 +246,12 @@
             total[...] += self.inbox(way, k, sub)[...].astype(f32)
 
     def drain(self):
-        for way in (0, 1):
-            for k in range(self.ways):
-                for sub in range(self.subs):
-                    @pl.when(self.sends(way, k))
-                    def _():
-                        self.copy(way, k, sub).wait_send()
+        for k in list(self.pending):
+            self.settle(k)
 
 
 class RowSum:
-    tile = 96
+    tile = 48
 
     def __init__(self, buf, result, box, extra_box, send_sem, recv_sem, r, total_bits):
         self.buf, self.result, self.box, self.extra_box = buf, result, box, extra_box
@@ -211,7 +272,7 @@
             inbox_at += size
 
     def rows(self, at, size, buf=None):
-        return (self.buf if buf is None else buf).at[pl.ds(pl.multiple_of(at, 32), size)]
+        return (self.buf if buf is None else buf).at[pl.ds(pl.multiple_of(at, 16), size)]
 
     def halve(self, level):
         partner, keep, give, size, inbox_at = self.levels[level]
@@ -235,8 +296,8 @@
         self.halve(level).wait_recv()
 
         def run(i, carry):
-            at = pl.ds(pl.multiple_of(keep + i * self.tile, 32), self.tile)
-            there = pl.ds(pl.multiple_of(inbox_at + i * self.tile, 32), self.tile)
+            at = pl.ds(pl.multiple_of(keep + i * self.tile, 16), self.tile)
+            there = pl.ds(pl.multiple_of(inbox_at + i * self.tile, 16), self.tile)
             target[at, :] = (self.buf[at, :].astype(f32) + self.box[there, :].astype(f32)).astype(bf16)
             return carry
 
@@ -251,10 +312,10 @@
             )
             copy.start()
             copy.wait()
-            at = pl.ds(pl.multiple_of(keep, 32), size)
+            at = pl.ds(pl.multiple_of(keep, 16), size)
             self.result[at, :] = (self.result[at, :].astype(f32) + self.extra_box[bit - 3].astype(f32)).astype(bf16)
 
-    def tasks(self, done):
+    def tasks(self):
         def second():
             self.add(0)
             self.halve(1).start()
@@ -278,7 +339,6 @@
 
         def last():
             self.double(0, True).wait_recv()
-            done()
 
         return [self.halve(0).start, second, third, turn, wider, widest, last]
 
@@ -398,7 +458,11 @@
     gains[z, 1:2, 0:own] = gain2_ref[...]
     gain_msg.start()
     x_load.wait()
-    in_line.send_own()
+    every, outer, middle = range(ways), inner == 0, inner == 1
+    first_two, last_two = range(ways // 2), range(ways // 2, ways)
+    next_hops, last_hops = range(1, 2), range(2, ways - 1)
+    in_line.send_own(first_two, True)
+    in_line.send_own(last_two, middle)
 
     def inside(at):
         return jnp.logical_and(at > 0, at < ways - 1)
@@ -409,6 +473,12 @@
     for copy in piece_loads:
         copy.wait()
     piece_msg.start(early)
+
+    def clear(j, carry):
+        gb[pl.ds(pl.multiple_of(j * 96, 96), 96), :] = jnp.zeros((96, width), bf16)
+        return carry
+
+    lax.fori_loop(0, gb.shape[0] // 96, clear, 0)
 
     line_at = lax.broadcasted_iota(jnp.int32, (1, seq), 1)
     split, valid = halves_ref[0, 0], halves_ref[0, 1]
@@ -432,6 +502,8 @@
     arg[...] = tn(frow[...], feat_ref[...], highest)
     kern[...] = nn(cols[:, 64:128], jnp.sin(arg[...]), highest)
 
+    in_line.settle([0], first_two)
+    in_line.send_own(last_two, outer)
     gain_msg.wait_recv()
     eye = lax.broadcasted_iota(jnp.int32, (own, gains.shape[2]), 0) == lax.broadcasted_iota(
         jnp.int32, (own, gains.shape[2]), 1)
@@ -459,16 +531,29 @@
         n1o[:, at] = low
         proj[:, at] = nn(in_t[...], low)
 
-    for index in range(ways):
+    for index in first_two:
         in_line.short_way(index)
-        if index < 2:
-            in_line.long_way(index)
-    for index in range(ways):
-        if index + 2 < ways:
-            in_line.long_way(index + 2)
+    for index in every:
+        in_line.long_way(index, next_hops)
+    for index in last_two:
+        in_line.short_way(index)
+    in_line.settle([0], last_two)
+    g_line.send_own(every, outer)
+    for index in first_two:
+        in_line.long_way(index, last_hops)
+    g_line.send_own(every, middle, inward=True)
+    for index in last_two:
+        in_line.long_way(index, last_hops)
+
+    def norm_turn(index, carry):
         in_line.take(index)
         norm1(in_order(index))
-    g_line.send_own(inner == 0)
+        return carry
+
+    lax.fori_loop(0, ways, norm_turn, 0)
+    piece_msg.start(lambda there: jnp.logical_not(early(there)))
+    for index in every:
+        g_line.short_way(index)
 
     piece_sends = []
 
@@ -491,48 +576,47 @@
 
     tab_load.wait()
 
-    lane = lax.broadcasted_iota(jnp.int32, (row_tile, seq), 1)
-    place = lane.astype(f32)
     half1, half2 = masks[0:1, :], masks[1:2, :]
 
     def back(values, steps):
         if steps == 0:
             return values
-        return jnp.where(lane >= steps, pltpu.roll(values, steps, 1), 0.0)
-
-    def ahead(values, steps):
-        if steps == 0:
-            return values
-        return jnp.where(lane < seq - steps, pltpu.roll(values, seq - steps, 1), 0.0)
+        return jnp.where(lane2 >= steps, pltpu.roll(values, steps, 1), 0.0)
 
     def row_at(j, i):
         return pl.ds(pl.multiple_of(j * own + i * row_tile, row_tile), row_tile)
 
-    def decay_of(tap):
-        return jnp.exp(-tap[:, 12:13] * place) * (1.0 / math.sqrt(seq))
+    tall = 2 * row_tile
+    lane2 = lax.broadcasted_iota(jnp.int32, (tall, seq), 1)
+    place2 = lane2.astype(f32)
 
     def mix_rows(i, carry):
-        here = row_at(0, i)
+        here, here1, here2 = (pl.ds(pl.multiple_of(j * own + i * tall, tall), tall) for j in range(3))
         tap = cols[here, :]
         outs = []
         for j in range(3):
-            part = proj[row_at(j, i), :]
+            part = proj[(here, here1, here2)[j], :]
             outs.append(sum(tap[:, 3 * k + j : 3 * k + j + 1] * back(part, k) for k in range(3)))
         query[here, :] = outs[0]
         kv[here, :] = outs[1]
-        kv[row_at(1, i), :] = outs[2]
+        kv[here1, :] = outs[2]
         cond = sum(tap[:, 9 + k : 10 + k] * back(outs[2], k) for k in range(3))
         bent = jnp.tanh(cond)
         squash[here, :] = bent
-        filt = (kern[here, :] + bent) * decay_of(tap)
+        filt = (kern[here, :] + bent) * (jnp.exp(-tap[:, 12:13] * place2) * (1.0 / math.sqrt(seq)))
         kern[here, :] = filt
         source = outs[1] * outs[2]
-        sig[row_at(0, i), :] = jnp.where(lane < lags, filt, 0.0).astype(bf16)
-        sig[row_at(1, i), :] = (source * half1).astype(bf16)
-        sig[row_at(2, i), :] = (source * half2).astype(bf16)
+        sig[here, :] = jnp.where(lane2 < lags, filt, 0.0).astype(bf16)
+        sig[here1, :] = (source * half1).astype(bf16)
+        sig[here2, :] = (source * half2).astype(bf16)
         return carry
 
-    lax.fori_loop(0, own // row_tile, mix_rows, 0)
+    lax.fori_loop(0, own // tall, mix_rows, 0)
+    g_line.send_own(first_two, middle, inward=False)
+    piece_msg.wait_recv()
+    bit_list = list(reversed(range(bits)))
+    finish, held, slot = piece_step(bit_list[0], [group], ways)
+
     def freq_at(j):
         return (pl.ds(pl.multiple_of(j * lane_tile, lane_tile), lane_tile),
                 pl.ds(pl.multiple_of(freq + j * lane_tile, lane_tile), lane_tile))
@@ -551,8 +635,6 @@
         return carry
 
     lax.fori_loop(0, freq // lane_tile, freq_tile, 0)
-    g_line.send_own(inner == 1)
-    piece_msg.start(lambda there: jnp.logical_not(early(there)))
 
     def time_tile(j, carry):
         at = token(j)
@@ -562,21 +644,25 @@
         mixf[span, at] = (query[:, at] * total).astype(bf16)
         return carry
 
-    lax.fori_loop(0, ways, time_tile, 0)
-
-    mix_line.send_own()
-    piece_msg.wait_recv()
-    held, slot = [group], ways
-    for bit in reversed(range(bits)):
-        finish, held, slot = piece_step(bit, held, slot)
-        if bit == bits - 1:
-            for index in range(ways):
-                g_line.short_way(index)
-        finish()
-    next_hops, last_hops = range(1, 2), range(2, ways - 1)
-    mix_line.long_way(0, next_hops)
-    mix_line.short_way(0)
-    mix_line.long_way(0, last_hops)
+    def time_turn(index, carry):
+        time_tile(side * (ways - 1 - index) + (1 - side) * index, 0)
+        for early_index in first_two:
+            @pl.when(index == early_index)
+            def _():
+                mix_line.send_own([early_index], True, inward=True)
+        return carry
+
+    lax.fori_loop(0, ways, time_turn, 0)
+    mix_line.send_own(first_two, middle, inward=False)
+    finish()
+    finish, held, slot = piece_step(bit_list[1], held, slot)
+    for index in first_two:
+        g_line.long_way(index)
+    mix_line.settle([0], first_two, outer)
+    mix_line.send_own(last_two, outer)
+    finish()
+    finish, held, slot = piece_step(bit_list[2], held, slot)
+    finish()
     for s in range(ways):
         for block_at in range(own * width // 128 // grain):
             piece, inside_at = divmod(block_at, per_piece)
@@ -585,11 +671,18 @@
                 piece, s, inside_at * grain : (inside_at + 1) * grain, :]
     for copy in weight_loads:
         copy.wait()
-    g_line.long_way(0)
-    mix_line.short_way(1)
-    mix_line.long_way(1)
-    g_line.long_way(1)
-    for index in range(2, ways):
+
+    def pass_set(index):
+        for line in (g_line, mix_line):
+            line.send_own([index], middle, inward=False)
+            line.long_way(index)
+
+    mix_line.long_way(0, next_hops)
+    for index in first_two:
+        mix_line.short_way(index)
+    mix_line.long_way(0, last_hops)
+    mix_line.send_own(last_two, middle, inward=True)
+    for index in last_two:
         mix_line.short_way(index)
 
     half_block = block // 2
@@ -620,7 +713,10 @@
 
     def forward(q):
         at = token(q)
-        rres[...] = xf[:, at].astype(f32) + nn(outt[...], mixf[:, at])
+        def resid_tile(ds):
+            rres[ds, :] = xf[ds, at].astype(f32) + nn(outt[ds, :], mixf[:, at])
+
+        tiles(width, resid_tile)
         resown[:, at] = rres[span, :]
         centre, inverse = moments(rres[...])
         n2o[:, at] = ((rres[...] - centre) * inverse * gaincol[:, 1:2]).astype(bf16)
@@ -662,57 +758,91 @@
 
         tiles(width, term_tile)
 
-    def turn_of(index):
-        if index == ways - 2:
-            return index + inner
-        if index == ways - 1:
-            return index - inner
-        return index
-
-    for index in range(ways):
-        if 0 < index < ways - 1:
-            mix_line.long_way(index + 1)
-            g_line.long_way(index + 1)
-        q = in_order(turn_of(index))
+    def turn_tokens(index):
+        late = index // (ways - 2)
+        return in_order(index + inner * late * (1 - 2 * (index - (ways - 2))))
+
+    def weight_grads(turn, carry):
+        at = token(turn_tokens(turn))
+        for lhs, rhs, place_at in ((mid, gf, 0), (n2o, gg, hidden), (n2o, ug, hidden + width)):
+            def run(j, carry):
+                rows_at = pl.ds(pl.multiple_of(j * lane_tile, lane_tile), lane_tile)
+                to = pl.ds(pl.multiple_of(place_at + j * lane_tile, lane_tile), lane_tile)
+                gb[to, :] = (nt(lhs[rows_at, at], rhs[:, at]) + gb[to, :].astype(f32)).astype(bf16)
+                return carry
+            lax.fori_loop(0, lhs.shape[0] // lane_tile, run, 0)
+        return carry
+
+    big_rows = hidden + 2 * width
+
+    def feed_forward_turn(index, carry):
+        def at_turn(which):
+            return pl.when(index == which)
+
+        q = turn_tokens(index)
         mix_line.take(index)
+
+        @at_turn(ways - 1)
+        def _():
+            for early_index in first_two:
+                for k in range(ways - 2):
+                    e_sum.first(k, by_end(early_index))
+
         forward(q)
-        if index == 0:
-            for k in range(ways - 1):
-                e_sum.first(k, by_end(0))
-        if index == 2:
-            f_sum.near(0, halves_of[1])
-        if index == 3:
-            f_sum.far(0, halves_of[1])
-            f_sum.near(1, halves_of[0])
+        for which in every:
+            @at_turn(which)
+            def _():
+                if which == 0:
+                    mix_line.long_way(1)
+                elif which + 1 < ways:
+                    for line in (g_line, mix_line):
+                        line.settle(range(ways - 1), range(which + 1))
+                    pass_set(which + 1)
+                if which == ways - 3:
+                    g_line.arrive(ways - 1)
+                    mix_line.arrive(ways - 1)
+                if which == ways - 2:
+                    for sub in halves_of:
+                        f_sum.near(0, sub)
         g_line.take(index)
         backward(q)
-        if index < ways - 1:
-            for sub in halves_of:
-                f_sum.first(index, sub)
-        if index == 1:
-            f_sum.near(0, halves_of[0])
-        if index == 2:
-            f_sum.far(0, halves_of[0])
-    f_sum.near(1, halves_of[1])
-    for k in range(ways - 1):
-        e_sum.first(k, by_end(1))
-
-    def weight_grad(lhs, rhs, place_at):
-        def run(j, carry):
-            at = pl.ds(pl.multiple_of(j * lane_tile, lane_tile), lane_tile)
-            gb[pl.ds(pl.multiple_of(place_at + j * lane_tile, lane_tile), lane_tile), :] = nt(
-                lhs[at, :], rhs[...]).astype(bf16)
-            return carry
-        lax.fori_loop(0, lhs.shape[0] // lane_tile, run, 0)
-
-    def weight_grads():
-        weight_grad(mid, gf, 0)
-        weight_grad(n2o, gg, hidden)
-        weight_grad(n2o, ug, hidden + width)
-
-    pl.when(inner == 1)(weight_grads)
-    big = RowSum(gb, weights, rb, rbx, ar_send.at[0], ar_recv.at[0], r, all_bits)
-    big_tasks = big.tasks(lambda: save(weights, big_hbm))
+        for which in every:
+            @at_turn(which)
+            def _():
+                if which < ways - 1:
+                    for sub in halves_of:
+                        f_sum.first(which, sub)
+                if which == ways - 1:
+                    for sub in halves_of:
+                        f_sum.near(1, sub)
+                    for sub in halves_of:
+                        f_sum.far(0, sub)
+        seen = (index + ways - 1) // ways
+        behind = seen * (1 - (index + ways - 2) // ways)
+        lax.fori_loop(index - behind * index, seen * (index + 1), weight_grads, 0)
+        return carry
+
+    lax.fori_loop(0, ways, feed_forward_turn, 0)
+
+    first_rows = big_rows // 2
+    big_parts = []
+    for i, at in enumerate((0, first_rows)):
+        def cut_rows(buf, at=at, size=first_rows):
+            return buf.at[pl.ds(at, size)]
+        big = RowSum(
+            cut_rows(gb), cut_rows(weights), cut_rows(rb, at * 7 // 8, first_rows * 7 // 8),
+            rbx.at[:, pl.ds(i * (rbx.shape[1] // 2), rbx.shape[1] // 2)], ar_send.at[i], ar_recv.at[i], r, all_bits)
+        big.halve(0).start()
+        big_parts.append(big)
+    big_left = [[big.tasks()[1:] for big in big_parts] for _ in range(2)]
+
+    def big_step(inside_line):
+        steps = [left.pop(0) for left in big_left[inside_line]]
+
+        @pl.when(inner == inside_line)
+        def _():
+            for step in steps:
+                step()
 
     rres[...] = tbuf[:, token(z)].astype(f32)
     for sub in range(2):
@@ -723,22 +853,27 @@
     plain = jnp.sum(upstream, axis=0, keepdims=True) * (1.0 / width)
     cross = jnp.sum(upstream * normed, axis=0, keepdims=True) * (1.0 / width)
     pgb[...] = (gf[:, token(z)].astype(f32) + inv2[0:1, :] * (upstream - plain - normed * cross)).astype(bf16)
-    mgb[...] = tn(outt[...], pgb[...]).astype(bf16)
+    def mix_grad_tile(ds):
+        mgb[ds, :] = tn(outt[:, ds], pgb[...]).astype(bf16)
+
+    tiles(width, mix_grad_tile)
     swap_mix = Direct(lambda to: mgb.at[own_rows(to)], lambda at: mgf.at[:, token(at)], sw_send.at[0], sw_recv.at[0])
     swap_proj = Direct(lambda to: pgb.at[own_rows(to)], lambda at: pgo.at[:, token(at)], sw_send.at[1], sw_recv.at[1])
     swap_mix.start()
-    swap_proj.start()
     mgf[:, token(z)] = mgb[span, :]
     pgo[:, token(z)] = pgb[span, :]
     ones = jnp.ones((8, block), bf16)
     gsum[ways] = nt(ones, (rres[...] * normed).astype(bf16))
 
-    for index in range(2, ways):
-        for k in range(ways - 1):
-            e_sum.first(k, by_end(index))
-    pl.when(inner == 0)(weight_grads)
-    big_tasks.pop(0)()
+    big_step(0)
+    big_step(1)
     swap_mix.wait_recv()
+    swap_proj.start()
+    for k in range(ways - 2):
+        e_sum.first(k, by_end(2))
+    for index in first_two:
+        for k in range(ways - 2):
+            e_sum.near(k, by_end(index))
 
     def grad_rows(i, carry):
         here = row_at(0, i)
@@ -768,7 +903,7 @@
         return carry
 
     lax.fori_loop(0, freq // lane_tile, grad_freq, 0)
-    big_tasks.pop(0)()
+    big_step(1)
 
     def grad_time(j, carry):
         at = token(j)
@@ -779,41 +914,67 @@
 
     lax.fori_loop(0, ways, grad_time, 0)
 
+    def sum_slot(index, at, size):
+        if index < seq // 128:
+            return query.at[pl.ds(at, size), 128 * index : 128 * index + 128]
+        index = index - seq // 128
+        return n2own.at[pl.ds(own * (index % ways) + at, size), 128 * (index // ways) : 128 * (index // ways) + 128]
+
+    def ahead2(values, steps):
+        if steps == 0:
+            return values
+        return jnp.where(lane2 < seq - steps, pltpu.roll(values, seq - steps, 1), 0.0)
+
     def chain_rows(i, carry):
-        here = row_at(0, i)
+        at = pl.multiple_of(i * tall, tall)
+        here, here1, here2 = (pl.ds(pl.multiple_of(j * own + i * tall, tall), tall) for j in range(3))
         tap = cols[here, :]
-        stat = jnp.zeros((row_tile, 128), f32)
-        column = lax.broadcasted_iota(jnp.int32, (row_tile, 128), 1)
-
-        def note(stat, index, values):
-            return jnp.where(column == index, jnp.sum(values, axis=1, keepdims=True), stat)
-
-        key, value = kv[here, :], kv[row_at(1, i), :]
-        kgrad = jnp.where(lane < lags, kgr[here, :], 0.0)
-        base_grad = kgrad * decay_of(tap)
+
+        def note(index, values):
+            sum_slot(index, at, tall)[...] = sum(values[:, 128 * b : 128 * b + 128] for b in range(seq // 128))
+
+        key, value = kv[here, :], kv[here1, :]
+        kgrad = jnp.where(lane2 < lags, kgr[here, :], 0.0)
+        base_grad = kgrad * (jnp.exp(-tap[:, 12:13] * place2) * (1.0 / math.sqrt(seq)))
         kgr[here, :] = base_grad
-        stat = note(stat, 12, -kgrad * kern[here, :] * place)
+        note(12, -kgrad * kern[here, :] * place2)
         bent = squash[here, :]
         cond_grad = base_grad * (1.0 - bent * bent)
         sgrad = sgr[here, :]
         value_grad = sgrad * key
         for k in range(3):
-            moved = ahead(cond_grad, k)
-            stat = note(stat, 9 + k, moved * value)
+            moved = ahead2(cond_grad, k)
+            note(9 + k, moved * value)
             value_grad = value_grad + tap[:, 9 + k : 10 + k] * moved
         branch = (mgf[here, :].astype(f32) * mixed[here, :], sgrad * value, value_grad)
-        for j in range(3):
-            part = proj[row_at(j, i), :]
+        for j, rows_at in enumerate((here, here1, here2)):
+            part = proj[rows_at, :]
             total = 0.0
             for k in range(3):
-                moved = ahead(branch[j], k)
-                stat = note(stat, 3 * k + j, moved * part)
+                moved = ahead2(branch[j], k)
+                note(3 * k + j, moved * part)
                 total = total + tap[:, 3 * k + j : 3 * k + j + 1] * moved
-            sig[row_at(j, i), :] = total.astype(bf16)
-        sm[here, :] = stat
+            sig[rows_at, :] = total.astype(bf16)
         return carry
 
-    lax.fori_loop(0, own // row_tile, chain_rows, 0)
+    lax.fori_loop(0, own // tall, chain_rows, 0)
+    big_step(0)
+    big_step(1)
+
+    def finish_sums():
+        ones_square = jnp.ones((128, 128), f32)
+
+        def run(i, carry):
+            at = pl.multiple_of(i * 64, 64)
+            column = lax.broadcasted_iota(jnp.int32, (64, 128), 1)
+            stat = jnp.zeros((64, 128), f32)
+            for index in range(13):
+                stat = jnp.where(column == index, nn(sum_slot(index, at, 64)[...], ones_square, highest), stat)
+            sm[pl.ds(at, 64), :] = stat
+            return carry
+
+        lax.fori_loop(0, own // 64, run, 0)
+
 
     h_sum = LineSum(
         lambda dest, sub: tbuf.at[own_rows(dest), token(sub)],
@@ -826,7 +987,7 @@
         at = token(tile)
         rres[...] = tn(in_t[...], sig[:, at])
         tbuf[:, at] = rres[...].astype(bf16)
-        h_sum.first(0, plain_order[tile])
+        h_sum.first(0, (tile, tile), False)
         normed = (xf[:, at].astype(f32) - stat1[0:1, at]) * stat1[1:2, at]
         upstream = rres[...] * gaincol[:, 0:1]
         mom[z, 0:1, at] = jnp.sum(upstream, axis=0, keepdims=True)
@@ -837,10 +998,15 @@
     sum2 = mid.at[0 : 4 * own, 0:width]
 
     def proj_grad(lhs, rhs, place_at):
-        gb2[place_at : place_at + lhs.shape[0], :] = nt(lhs[...], rhs[...]).astype(bf16)
-
-    two = RowSum(gb2, sum2, rb2, rbx2, ar_send.at[1], ar_recv.at[1], r, all_bits)
-    two_tasks = two.tasks(lambda: save(sum2, proj_hbm))
+        def run(j, carry):
+            gb2[pl.ds(pl.multiple_of(place_at + j * own, row_tile), own), :] = nt(
+                lhs[pl.ds(pl.multiple_of(j * own, row_tile), own), :], rhs[...]).astype(bf16)
+            return carry
+
+        lax.fori_loop(0, lhs.shape[0] // own, run, 0)
+
+    two = RowSum(gb2, sum2, rb2, rbx2, ar_send.at[2], ar_recv.at[2], r, all_bits)
+    two_tasks = two.tasks()
 
     def small_copy(b):
         return pltpu.make_async_remote_copy(
@@ -868,7 +1034,6 @@
         for way in (0, 1):
             e_sum.take(way, tile, total)
         resown[:, at] = (resown[:, at] + total[...]) * masks[2:3, at]
-        save(resown.at[:, at], out_hbm.at[:, at])
 
     def input_part(tile):
         at = token(tile)
@@ -882,35 +1047,32 @@
         sgr[:, at] = pgo[:, at].astype(f32) + inverse * (upstream - sums[0:1, :] - normed * sums[1:2, :])
         save(sgr.at[:, at], igrad_hbm.at[:, at])
 
-    for index in range(ways):
-        near(e_sum, 0, index)
-    in_back(0)
-    in_back(1)
+    def in_turn(tile, carry):
+        in_back(tile)
+        return carry
+
+    lax.fori_loop(0, ways, in_turn, 0)
+    for index in every:
+        h_sum.note_first(0, plain_order[index])
+    mom_msg.start()
     swap_proj.wait_recv()
     proj_grad(sig, n1o, 0)
     proj_grad(pgo, mixf, 3 * own)
     two_tasks.pop(0)()
-    near(h_sum, 0, 0)
-    in_back(2)
-    near(h_sum, 0, 1)
-    in_back(3)
-    for k in range(1, ways - 1):
-        for tile in range(ways):
-            h_sum.first(k, plain_order[tile])
-    mom_msg.start()
-    for index in range(ways):
-        near(e_sum, 1, index)
-    for index in range(ways):
+    for index in every:
+        h_sum.first(1, plain_order[index])
+    for index in first_two:
         far(e_sum, 0, index)
-    near(h_sum, 0, 2)
-    two_tasks.pop(0)()
-    far(h_sum, 0, 0)
-    big_tasks.pop(0)()
+    for k in range(ways - 2):
+        near(e_sum, k, 2)
+    big_step(0)
+    big_step(1)
 
     wave_grad = tn(cols[:, 64:128], kgr[...], highest) * jnp.cos(arg[...])
+    finish_sums()
+    for index in every:
+        near(h_sum, 0, index)
     sm[0:own, 64:128] = nt(kgr[...], jnp.sin(arg[...]), highest)
-    near(h_sum, 0, 3)
-    far(h_sum, 0, 1)
     sm[own : own + 64, 0:64] = nt(feat_ref[...], wave_grad, highest)
     sm[own : own + 64, 64:128] = jnp.zeros((64, 64), f32)
     sm[own + 64 :, :] = jnp.zeros((16, 128), f32)
@@ -919,35 +1081,45 @@
         sm[own + 64 + b : own + 65 + b, :] = sum(gsum[tile, 0:1, lanes] for tile in range(ways))
         sm[own + 72 + b : own + 73 + b, :] = gsum[ways, 0:1, lanes]
     small_copy(0).start()
-    far(h_sum, 0, 2)
     two_tasks.pop(0)()
-    near(h_sum, 1, 0)
-    far(h_sum, 0, 3)
     small_step(0)
-    near(h_sum, 1, 1)
-    big_tasks.pop(0)()
-    for tile in range(ways):
-        output_part(tile)
-    near(h_sum, 1, 2)
+    for k in range(ways - 2):
+        e_sum.first(k, by_end(3))
+    for index in every:
+        far(h_sum, 0, index)
+    small_step(1)
+    for index in every:
+        h_sum.first(2, plain_order[index])
+    for index in every:
+        near(h_sum, 1, index)
     two_tasks.pop(0)()
-    small_step(1)
-    near(h_sum, 1, 3)
-    two_tasks.pop(0)()
-    big_tasks.pop(0)()
+    big_step(0)
+    for index in every:
+        e_sum.first(ways - 2, by_end(index))
+    far(e_sum, 0, 2)
+    big_step(1)
     for b in range(2, all_bits):
         small_step(b)
     z_msg = Direct(lambda to: zbox.at[z], lambda at: zbox.at[at], z_send, z_recv)
     zbox[z] = sm[own:, :]
     z_msg.start()
     save(sm, small_hbm)
+    two_tasks.pop(0)()
+    for k in range(ways - 2):
+        near(e_sum, k, 3)
+    two_tasks.pop(0)()
+    big_step(0)
+    two_tasks.pop(0)()
+    far(e_sum, 0, 3)
+    big_step(1)
+    big_step(0)
+    save(weights, big_hbm)
     mom_msg.wait_recv()
     input_part(0)
+    input_part(1)
     two_tasks.pop(0)()
-    input_part(1)
-    big_tasks.pop(0)()
-    two_tasks.pop(0)()
+    save(sum2, proj_hbm)
     input_part(2)
-    big_tasks.pop(0)()
     z_msg.wait_recv()
     zsum = zbox[0]
     for s in range(1, ways):
@@ -956,8 +1128,14 @@
     zout[...] = zsum
     save(zout, zsum_hbm)
     input_part(3)
-
-    for line in (in_line, g_line, mix_line, e_sum, h_sum, gain_msg, piece_msg, swap_mix, swap_proj, mom_msg, z_msg, big, two):
+    def output_turn(tile, carry):
+        output_part(tile)
+        return carry
+
+    lax.fori_loop(0, ways, output_turn, 0)
+    save(resown, out_hbm)
+
+    for line in (in_line, g_line, mix_line, e_sum, h_sum, gain_msg, piece_msg, swap_mix, swap_proj, mom_msg, z_msg, big_parts[0], big_parts[1], two):
         line.drain()
     for make, piece in piece_sends:
         make(piece).wait_send()
@@ -984,7 +1162,7 @@
         mid=((hidden, seq), bf16), gg=((hidden, seq), bf16), ug=((hidden, seq), bf16), tbuf=((width, seq), bf16),
         tin=((2, ways - 1, width, block), bf16), mbuf=((width, seq), bf16), ein=((2, ways - 1, own, seq), bf16),
         gb=((big_rows, width), bf16), rb=((big_rows * 7 // 8, width), bf16),
-        rbx=((max(all_bits - 3, 1), big_rows // 8 if all_bits > 3 else 16, width), bf16),
+        rbx=((max(all_bits - 3, 1), big_rows // 8 if all_bits > 3 else 32, width), bf16),
         rb2=((4 * own * 7 // 8, width), bf16),
         rbx2=((max(all_bits - 3, 1), 4 * own // 8 if all_bits > 3 else 16, width), bf16),
         n2own=((width, block), f32), inv2=((8, block), f32), rres=((width, block), f32), resown=((own, seq), f32),
@@ -998,7 +1176,7 @@
         load_sem=(16,), line_send=hops, line_recv=hops, piece_send=(ways + (1 << bits),), piece_recv=(ways + (1 << bits),),
         gain_send=(ways,), gain_recv=(ways,), save_sem=(24,), fs_send=(2, ways, 2), fs_recv=(2, ways, 2),
         es_send=(2, ways, ways), es_recv=(2, ways, ways), hs_send=(2, ways, ways), hs_recv=(2, ways, ways),
-        sw_send=(2, ways), sw_recv=(2, ways), ar_send=(2, 3 + max(all_bits, 3)), ar_recv=(2, 3 + max(all_bits, 3)),
+        sw_send=(2, ways), sw_recv=(2, ways), ar_send=(3, 3 + max(all_bits, 3)), ar_recv=(3, 3 + max(all_bits, 3)),
         sm_send=(all_bits,), sm_recv=(all_bits,), z_send=(ways,), z_recv=(ways,), mom_send=(ways,), mom_recv=(ways,),
     )
     here = pl.BlockSpec(memory_space=pltpu.VMEM)
@@ -1019,6 +1197,73 @@
       filter_in, filter_bias, filter_out, feats)
 
 
+def widen_kernel(
+    cfg, count, out_in, igrad_in, big_in, two_in, small_ref, zsum_ref,
+    out_hbm, igrad_hbm, wd_hbm, wg_hbm, wu_hbm, in_hbm, outp_hbm, gain1_ref, gain2_ref, short_ref, cond_ref, rate_ref,
+    fin_ref, fbias_ref, fout_ref, low, wide, through, in_sem, out_sem, copy_sem,
+):
+    ways, seq, own, width, hidden, bits, all_bits = cfg
+    step = own
+    sources = [(big_in, at) for at in range(0, hidden + 2 * width, step)] + [(two_in, at) for at in range(0, 4 * own, step)]
+    targets = [
+        (ref, at) for ref, size in ((wd_hbm, hidden), (wg_hbm, width), (wu_hbm, width), (in_hbm, 3 * own), (outp_hbm, own))
+        for at in range(0, size, step)]
+    loads = [
+        pltpu.make_async_copy(src.at[pl.ds(at, step)], low.at[i], in_sem.at[i]) for i, (src, at) in enumerate(sources)]
+    for copy in loads:
+        copy.start()
+    ins = [pltpu.make_async_copy(src, through.at[i], copy_sem.at[i]) for i, src in enumerate((out_in, igrad_in))]
+    for copy in ins:
+        copy.start()
+    moves = []
+    stats = small_ref[0:own, :].T
+    for i in range(3):
+        for j in range(3):
+            short_ref[i, j : j + 1, :] = stats[3 * i + j : 3 * i + j + 1, :]
+    cond_ref[...] = stats[9:12, :]
+    rate_ref[...] = stats[12:13, :]
+    fout_ref[...] = stats[64:128, :]
+    fin_ref[...] = zsum_ref[0:count, 0:64]
+    fbias_ref[...] = zsum_ref[count : count + 1, 0:64]
+    shift = (width - own * lax.axis_index("chan")) % width
+    for first, ref in ((64, gain1_ref), (72, gain2_ref)):
+        row = jnp.concatenate([zsum_ref[first + b : first + b + 1, :] for b in range(width // 128)], axis=1)
+        ref[...] = pltpu.roll(jnp.broadcast_to(row, (8, width)), shift, 1)[0:1, 0:own]
+    for i, ref in enumerate((out_hbm, igrad_hbm)):
+        ins[i].wait()
+        copy = pltpu.make_async_copy(through.at[i], ref, copy_sem.at[2 + i])
+        copy.start()
+        moves.append(copy)
+    for i, (ref, at) in enumerate(targets):
+        loads[i].wait()
+        wide[i] = low[i].astype(f32)
+        copy = pltpu.make_async_copy(wide.at[i], ref.at[pl.ds(at, step)], out_sem.at[i])
+        copy.start()
+        moves.append(copy)
+    for copy in moves:
+        copy.wait()
+
+
+def widen(cfg, count, output, input_grad, big, two, small, zsum):
+    ways, seq, own, width, hidden, bits, all_bits = cfg
+    here = pl.BlockSpec(memory_space=pltpu.VMEM)
+    there = pl.BlockSpec(memory_space=pl.ANY)
+    far = [(own, seq), (own, seq), (hidden, width), (width, hidden), (width, hidden), (3 * own, width), (own, width)]
+    near = [(1, own), (1, own), (3, 3, own), (3, own), (1, own), (count, 64), (1, 64), (64, own)]
+    steps = (hidden + 2 * width + 4 * own) // own
+    dma = pltpu.SemaphoreType.DMA
+    return pl.pallas_call(
+        functools.partial(widen_kernel, cfg, count),
+        out_shape=[jax.ShapeDtypeStruct(shape, f32) for shape in far + near],
+        in_specs=[there] * 4 + [here] * 2,
+        out_specs=[there] * len(far) + [here] * len(near),
+        scratch_shapes=[
+            pltpu.VMEM((steps, own, width), bf16), pltpu.VMEM((steps, own, width), f32),
+            pltpu.VMEM((2, own, seq), f32), dma((steps,)), dma((steps,)), dma((4,))],
+        compiler_params=pltpu.CompilerParams(vmem_limit_bytes=64 << 20),
+    )(output, input_grad, big, two, small, zsum)
+
+
 def local(
     hidden_in, halves, norm1_gain, in_proj, short_taps, cond_taps, filter_in, filter_bias,
     filter_out, decay_rate, out_proj, norm2_gain, w_gate, w_up, w_down, out_grad,
@@ -1039,15 +1284,11 @@
         w_gate, w_up, w_down, halves, norm1_gain[None], norm2_gain[None], short_taps, cond_taps, decay_rate[None],
         filter_in, filter_bias[None], filter_out, jnp.asarray(feat_np))
 
-    stats = small[:own].T
-    gain_sums = zsum[64:].reshape(2, 8 * 128)
-    mine = lax.dynamic_slice_in_dim(gain_sums, z * own, own, 1)
-    in_grad = two[: 3 * own].astype(f32).reshape(3, own, width).transpose(2, 0, 1)
-    out_grad_sum = two[3 * own :].astype(f32).T
+    (output, input_grad, wd_sum, wg_sum, wu_sum, in_sum, out_sum, gain1, gain2, short, cond, rates, fin, fbias, fout) = widen(
+        cfg, count, output, input_grad, big, two, small, zsum)
     return (
-        output.T[None], input_grad.T[None], mine[0], in_grad, stats[:9].reshape(3, 3, own),
-        stats[9:12], zsum[:count, :64], zsum[count, :64], stats[64:128], stats[12], out_grad_sum, mine[1],
-        big[hidden : hidden + width].astype(f32), big[hidden + width :].astype(f32), big[:hidden].astype(f32),
+        output.T[None], input_grad.T[None], gain1[0], in_sum.reshape(3, own, width).transpose(2, 0, 1), short, cond, fin,
+        fbias[0], fout, rates[0], out_sum.T, gain2[0], wg_sum, wu_sum, wd_sum,
     )
 
 

time: 215 us -> 178 us (0.83)
  the two profiles are of different devices: /device:TPU:9 before, /device:TPU:0 now
where the time goes in v4:
time: 178 us
  Pallas kernels  177 us (99%)
    pallas_call x1, Pallas kernels, layer(): pl.pallas_call(functools.partial(layer_kernel, cfg), out_shape=[jax.Shape...  168 us
    pallas_call x1, Pallas kernels, widen(): pl.pallas_call(functools.partial(widen_kernel, cfg, count), out_shape=[ja...  8.57 us

profile of v4, /device:TPU:0, one launch (start us, length us, event | category | flops | bytes accessed | tf_op | source)
XLA Modules:
  0.0 177.9 jit_solution(15525843153954332016)
XLA Ops:
  0.7 168.5 %shard_map.289 = (f32[192,1024]{1,0:T(8,128)}, f32[192,1024]{1,0:T(8,128)}, bf16[2304,768]{1,0:T(8,128)(2,1)}, bf16[768,768]{1,0:T(8,128)(2,1)}, f32[272,128]{1,0:T(8,128)}, /*index=5*/f32[80,128]{1,0:T(8,128)}) custom-call(bf16[192,1024]{1,0:T(8,128)(2,1)} %bitcast.29, bf16[192,1024]{1,0:T(8,128)(2,1)} %bitcast.30, bf16[192,768]{1,0:T(8,128)(2,1)} %bitcast.31, ...), custom_call_target="tpu_custom_call" | custom-call | tf_op jit(solution)/shard_map/pallas_call | solution.py:1188
  169.1 8.6 %shard_map.290 = (f32[192,1024]{1,0:T(8,128)}, f32[192,1024]{1,0:T(8,128)}, f32[768,768]{1,0:T(8,128)}, f32[768,768]{1,0:T(8,128)}, f32[768,768]{1,0:T(8,128)}, ...) custom-call(f32[192,1024]{1,0:T(8,128)} %get-tuple-element.36.out_in, ...), custom_call_target="tpu_custom_call" | custom-call | tf_op jit(solution)/shard_map/pallas_call | solution.py:1255

commit v5 on v4

--- a/solution.py
+++ b/solution.py
@@ -352,7 +352,7 @@
     cfg,
     x_hbm, g_hbm, outp_hbm, in_hbm, tab_hbm, wg_hbm, wu_hbm, wd_hbm, halves_ref, gain1_ref, gain2_ref, short_ref, cond_ref,
     rate_ref, fin_ref, fbias_ref, fout_ref, feat_ref,
-    out_hbm, igrad_hbm, big_hbm, proj_hbm, small_hbm, zsum_hbm, *scratch,
+    out_hbm, igrad_hbm, big_hbm, proj_hbm, small_hbm, *scratch,
 ):
     ways, seq, own, width, hidden, bits, all_bits = cfg
     (
@@ -361,7 +361,7 @@
         gb, rb, rbx, rb2, rbx2, n2own, inv2, rres, resown, pgb, mgb, mgf, pgo, sgr, kgr, sm, smbox, zbox, mom, gsum,
         load_sem, line_send, line_recv, piece_send, piece_recv, gain_send, gain_recv, save_sem,
         fs_send, fs_recv, es_send, es_recv, hs_send, hs_recv, sw_send, sw_recv,
-        ar_send, ar_recv, sm_send, sm_recv, z_send, z_recv, mom_send, mom_recv,
+        pace_sem, ar_send, ar_recv, sm_send, sm_recv, z_send, z_recv, mom_send, mom_recv,
     ) = scratch
     lags = 3 * seq // 4
     freq = lags
@@ -653,7 +653,7 @@
         return carry
 
     lax.fori_loop(0, ways, time_turn, 0)
-    mix_line.send_own(first_two, middle, inward=False)
+    mix_line.send_own([0], middle, inward=False)
     finish()
     finish, held, slot = piece_step(bit_list[1], held, slot)
     for index in first_two:
@@ -738,6 +738,9 @@
 
         tiles(hidden, hidden_tile)
 
+    def down(q):
+        at = token(q)
+
         def mlp_tile(ds):
             mbuf[ds, at] = tn(wd[:, ds], mid[:, at]).astype(bf16)
 
@@ -793,10 +796,20 @@
             @at_turn(which)
             def _():
                 if which == 0:
+                    mix_line.send_own([1], middle, inward=False)
                     mix_line.long_way(1)
                 elif which + 1 < ways:
                     for line in (g_line, mix_line):
                         line.settle(range(ways - 1), range(which + 1))
+
+                    @pl.when(jnp.logical_and(middle, r % 2 == 0))
+                    def _():
+                        pl.semaphore_signal(pace_sem, inc=1, device_id={"dp": flipped(r, 0)}, device_id_type=MESH)
+
+                    @pl.when(jnp.logical_and(middle, r % 2 == 1))
+                    def _():
+                        pl.semaphore_wait(pace_sem, 1)
+
                     pass_set(which + 1)
                 if which == ways - 3:
                     g_line.arrive(ways - 1)
@@ -817,6 +830,7 @@
                         f_sum.near(1, sub)
                     for sub in halves_of:
                         f_sum.far(0, sub)
+        pl.when(index < ways - 1)(lambda: down(q))
         seen = (index + ways - 1) // ways
         behind = seen * (1 - (index + ways - 2) // ways)
         lax.fori_loop(index - behind * index, seen * (index + 1), weight_grads, 0)
@@ -860,6 +874,7 @@
     swap_mix = Direct(lambda to: mgb.at[own_rows(to)], lambda at: mgf.at[:, token(at)], sw_send.at[0], sw_recv.at[0])
     swap_proj = Direct(lambda to: pgb.at[own_rows(to)], lambda at: pgo.at[:, token(at)], sw_send.at[1], sw_recv.at[1])
     swap_mix.start()
+    down(turn_tokens(ways - 1))
     mgf[:, token(z)] = mgb[span, :]
     pgo[:, token(z)] = pgb[span, :]
     ones = jnp.ones((8, block), bf16)
@@ -1008,17 +1023,21 @@
     two = RowSum(gb2, sum2, rb2, rbx2, ar_send.at[2], ar_recv.at[2], r, all_bits)
     two_tasks = two.tasks()
 
-    def small_copy(b):
+    dp_rows, all_rows = pl.ds(0, own), pl.ds(own, 80)
+
+    def small_copy(chain, b):
+        at = (dp_rows, all_rows)[chain]
         return pltpu.make_async_remote_copy(
-            src_ref=sm, dst_ref=smbox.at[b], send_sem=sm_send.at[b], recv_sem=sm_recv.at[b],
+            src_ref=sm.at[at], dst_ref=smbox.at[b, at], send_sem=sm_send.at[chain, b], recv_sem=sm_recv.at[chain, b],
             device_id={"dp": flipped(r, b)}, device_id_type=MESH,
         )
 
-    def small_step(b):
-        small_copy(b).wait()
-        sm[...] += smbox[b]
+    def small_step(chain, b):
+        at = (dp_rows, all_rows)[chain]
+        small_copy(chain, b).wait()
+        sm[at, :] += smbox[b, at, :]
         if b + 1 < all_bits:
-            small_copy(b + 1).start()
+            small_copy(chain, b + 1).start()
 
     def near(summer, k, index):
         summer.near(k, by_end(index) if summer is e_sum else plain_order[index])
@@ -1052,6 +1071,7 @@
         return carry
 
     lax.fori_loop(0, ways, in_turn, 0)
+    big_step(0)
     for index in every:
         h_sum.note_first(0, plain_order[index])
     mom_msg.start()
@@ -1065,11 +1085,12 @@
         far(e_sum, 0, index)
     for k in range(ways - 2):
         near(e_sum, k, 2)
+
+    wave_grad = tn(cols[:, 64:128], kgr[...], highest) * jnp.cos(arg[...])
+    finish_sums()
+    two_tasks.pop(0)()
     big_step(0)
     big_step(1)
-
-    wave_grad = tn(cols[:, 64:128], kgr[...], highest) * jnp.cos(arg[...])
-    finish_sums()
     for index in every:
         near(h_sum, 0, index)
     sm[0:own, 64:128] = nt(kgr[...], jnp.sin(arg[...]), highest)
@@ -1080,53 +1101,54 @@
         lanes = slice(128 * b, 128 * b + 128)
         sm[own + 64 + b : own + 65 + b, :] = sum(gsum[tile, 0:1, lanes] for tile in range(ways))
         sm[own + 72 + b : own + 73 + b, :] = gsum[ways, 0:1, lanes]
-    small_copy(0).start()
+    small_copy(0, 0).start()
+    z_msg = Direct(lambda to: zbox.at[z], lambda at: zbox.at[at], z_send, z_recv)
+    zbox[z] = sm[own:, :]
+    z_msg.start()
     two_tasks.pop(0)()
-    small_step(0)
+    small_step(0, 0)
     for k in range(ways - 2):
         e_sum.first(k, by_end(3))
     for index in every:
         far(h_sum, 0, index)
-    small_step(1)
+    two_tasks.pop(0)()
     for index in every:
         h_sum.first(2, plain_order[index])
     for index in every:
         near(h_sum, 1, index)
-    two_tasks.pop(0)()
-    big_step(0)
+    for k in range(ways - 2):
+        near(e_sum, k, 3)
     for index in every:
         e_sum.first(ways - 2, by_end(index))
+    two_tasks.pop(0)()
+    small_step(0, 1)
+    z_msg.wait_recv()
+    zsum = zbox[0]
+    for other in range(1, ways):
+        zsum = zsum + zbox[other]
+    sm[own:, :] = zsum
+    small_copy(1, 0).start()
+    small_step(1, 0)
     far(e_sum, 0, 2)
+    two_tasks.pop(0)()
+    for b in range(2, all_bits):
+        small_step(0, b)
+    far(e_sum, 0, 3)
     big_step(1)
-    for b in range(2, all_bits):
-        small_step(b)
-    z_msg = Direct(lambda to: zbox.at[z], lambda at: zbox.at[at], z_send, z_recv)
-    zbox[z] = sm[own:, :]
-    z_msg.start()
-    save(sm, small_hbm)
-    two_tasks.pop(0)()
-    for k in range(ways - 2):
-        near(e_sum, k, 3)
-    two_tasks.pop(0)()
+    small_step(1, 1)
     big_step(0)
     two_tasks.pop(0)()
-    far(e_sum, 0, 3)
+    save(sum2, proj_hbm)
+    for b in range(2, all_bits):
+        small_step(1, b)
+    save(sm, small_hbm)
     big_step(1)
     big_step(0)
     save(weights, big_hbm)
     mom_msg.wait_recv()
     input_part(0)
     input_part(1)
-    two_tasks.pop(0)()
-    save(sum2, proj_hbm)
     input_part(2)
-    z_msg.wait_recv()
-    zsum = zbox[0]
-    for s in range(1, ways):
-        zsum = zsum + zbox[s]
-    zout = kern.at[0 : zsum.shape[0], 0:128]
-    zout[...] = zsum
-    save(zout, zsum_hbm)
     input_part(3)
     def output_turn(tile, carry):
         output_part(tile)
@@ -1173,17 +1195,17 @@
     )
     hops = (3, 2, ways - 1, ways)
     sems = dict(
-        load_sem=(16,), line_send=hops, line_recv=hops, piece_send=(ways + (1 << bits),), piece_recv=(ways + (1 << bits),),
-        gain_send=(ways,), gain_recv=(ways,), save_sem=(24,), fs_send=(2, ways, 2), fs_recv=(2, ways, 2),
-        es_send=(2, ways, ways), es_recv=(2, ways, ways), hs_send=(2, ways, ways), hs_recv=(2, ways, ways),
-        sw_send=(2, ways), sw_recv=(2, ways), ar_send=(3, 3 + max(all_bits, 3)), ar_recv=(3, 3 + max(all_bits, 3)),
-        sm_send=(all_bits,), sm_recv=(all_bits,), z_send=(ways,), z_recv=(ways,), mom_send=(ways,), mom_recv=(ways,),
+        load_sem=(11,), line_send=hops, line_recv=hops, piece_send=(ways + (1 << bits),), piece_recv=(ways + (1 << bits),),
+        gain_send=(ways,), gain_recv=(ways,), save_sem=(8,), fs_send=(2, ways - 1, 2), fs_recv=(2, ways - 1, 2),
+        es_send=(2, ways - 1, ways), es_recv=(2, ways - 1, ways), hs_send=(2, ways - 1, ways), hs_recv=(2, ways - 1, ways),
+        sw_send=(2, ways), sw_recv=(2, ways), pace_sem=None, ar_send=(3, 3 + max(all_bits, 3)), ar_recv=(3, 3 + max(all_bits, 3)),
+        sm_send=(2, all_bits), sm_recv=(2, all_bits), z_send=(ways,), z_recv=(ways,), mom_send=(ways,), mom_recv=(ways,),
     )
     here = pl.BlockSpec(memory_space=pltpu.VMEM)
     there = pl.BlockSpec(memory_space=pl.ANY)
     outs = [
         ((own, seq), f32), ((own, seq), f32), ((big_rows, width), bf16), ((4 * own, width), bf16),
-        ((own + 80, 128), f32), ((80, 128), f32),
+        ((own + 80, 128), f32),
     ]
     return pl.pallas_call(
         functools.partial(layer_kernel, cfg),
@@ -1191,14 +1213,14 @@
         in_specs=[there] * 8 + [pl.BlockSpec(memory_space=pltpu.SMEM)] + [here] * 9,
         out_specs=[there] * len(outs),
         scratch_shapes=[pltpu.VMEM(s, t) for s, t in held.values()] + [
-            pltpu.SemaphoreType.DMA(s) for s in sems.values()],
+            pltpu.SemaphoreType.REGULAR if s is None else pltpu.SemaphoreType.DMA(s) for s in sems.values()],
         compiler_params=pltpu.CompilerParams(collective_id=0, has_side_effects=True, vmem_limit_bytes=64 << 20),
     )(x_own, g_own, out_t, in_t, table, w_gate, w_up, w_down, halves, gain1, gain2, short_taps, cond_taps, rates,
       filter_in, filter_bias, filter_out, feats)
 
 
 def widen_kernel(
-    cfg, count, out_in, igrad_in, big_in, two_in, small_ref, zsum_ref,
+    cfg, count, out_in, igrad_in, big_in, two_in, small_ref,
     out_hbm, igrad_hbm, wd_hbm, wg_hbm, wu_hbm, in_hbm, outp_hbm, gain1_ref, gain2_ref, short_ref, cond_ref, rate_ref,
     fin_ref, fbias_ref, fout_ref, low, wide, through, in_sem, out_sem, copy_sem,
 ):
@@ -1223,11 +1245,11 @@
     cond_ref[...] = stats[9:12, :]
     rate_ref[...] = stats[12:13, :]
     fout_ref[...] = stats[64:128, :]
-    fin_ref[...] = zsum_ref[0:count, 0:64]
-    fbias_ref[...] = zsum_ref[count : count + 1, 0:64]
+    fin_ref[...] = small_ref[own : own + count, 0:64]
+    fbias_ref[...] = small_ref[own + count : own + count + 1, 0:64]
     shift = (width - own * lax.axis_index("chan")) % width
     for first, ref in ((64, gain1_ref), (72, gain2_ref)):
-        row = jnp.concatenate([zsum_ref[first + b : first + b + 1, :] for b in range(width // 128)], axis=1)
+        row = jnp.concatenate([small_ref[own + first + b : own + first + b + 1, :] for b in range(width // 128)], axis=1)
         ref[...] = pltpu.roll(jnp.broadcast_to(row, (8, width)), shift, 1)[0:1, 0:own]
     for i, ref in enumerate((out_hbm, igrad_hbm)):
         ins[i].wait()
@@ -1244,7 +1266,7 @@
         copy.wait()
 
 
-def widen(cfg, count, output, input_grad, big, two, small, zsum):
+def widen(cfg, count, output, input_grad, big, two, small):
     ways, seq, own, width, hidden, bits, all_bits = cfg
     here = pl.BlockSpec(memory_space=pltpu.VMEM)
     there = pl.BlockSpec(memory_space=pl.ANY)
@@ -1255,13 +1277,13 @@
     return pl.pallas_call(
         functools.partial(widen_kernel, cfg, count),
         out_shape=[jax.ShapeDtypeStruct(shape, f32) for shape in far + near],
-        in_specs=[there] * 4 + [here] * 2,
+        in_specs=[there] * 4 + [here],
         out_specs=[there] * len(far) + [here] * len(near),
         scratch_shapes=[
             pltpu.VMEM((steps, own, width), bf16), pltpu.VMEM((steps, own, width), f32),
             pltpu.VMEM((2, own, seq), f32), dma((steps,)), dma((steps,)), dma((4,))],
         compiler_params=pltpu.CompilerParams(vmem_limit_bytes=64 << 20),
-    )(output, input_grad, big, two, small, zsum)
+    )(output, input_grad, big, two, small)
 
 
 def local(
@@ -1279,13 +1301,13 @@
         band_features(seq, count), np.ones((1, seq), np.float32), np.zeros((63 - count, seq), np.float32)])
     table = jnp.asarray(wave_matrix(seq).astype(np.float32)).astype(bf16)
 
-    output, input_grad, big, two, small, zsum = layer(
+    output, input_grad, big, two, small = layer(
         cfg, hidden_in[0].T, out_grad[0].T, out_proj.T, in_proj.transpose(1, 2, 0).reshape(3 * own, width), table,
         w_gate, w_up, w_down, halves, norm1_gain[None], norm2_gain[None], short_taps, cond_taps, decay_rate[None],
         filter_in, filter_bias[None], filter_out, jnp.asarray(feat_np))
 
     (output, input_grad, wd_sum, wg_sum, wu_sum, in_sum, out_sum, gain1, gain2, short, cond, rates, fin, fbias, fout) = widen(
-        cfg, count, output, input_grad, big, two, small, zsum)
+        cfg, count, output, input_grad, big, two, small)
     return (
         output.T[None], input_grad.T[None], gain1[0], in_sum.reshape(3, own, width).transpose(2, 0, 1), short, cond, fin,
         fbias[0], fout, rates[0], out_sum.T, gain2[0], wg_sum, wu_sum, wd_sum,

time: 178 us -> 174 us (0.978)
  Pallas kernels: 177 us -> 173 us
    pallas_call x1, Pallas kernels: 168 us -> 165 us  [layer(): pl.pallas_call(functools.partial(layer_kernel, cfg), out_shape=[jax.Shape...]
where the time goes in v5:
time: 174 us
  Pallas kernels  173 us (99%)
    pallas_call x1, Pallas kernels, layer(): pl.pallas_call(functools.partial(layer_kernel, cfg), out_shape=[jax.Shape...  165 us
    pallas_call x1, Pallas kernels, widen(): pl.pallas_call(functools.partial(widen_kernel, cfg, count), out_shape=[ja...  8.54 us

profile of v5, /device:TPU:0, one launch (start us, length us, event | category | flops | bytes accessed | tf_op | source)
XLA Modules:
  0.0 174.1 jit_solution(17356642635771920471)
XLA Ops:
  0.7 164.8 %shard_map.289 = (f32[192,1024]{1,0:T(8,128)}, f32[192,1024]{1,0:T(8,128)}, bf16[2304,768]{1,0:T(8,128)(2,1)}, bf16[768,768]{1,0:T(8,128)(2,1)}, f32[272,128]{1,0:T(8,128)}) custom-call(bf16[192,1024]{1,0:T(8,128)(2,1)} %bitcast.29, bf16[192,1024]{1,0:T(8,128)(2,1)} %bitcast.30, bf16[192,768]{1,0:T(8,128)(2,1)} %bitcast.31, bf16[576,768]{1,0:T(8,128)(2,1)} %bitcast.28, ...), custom_call_target="tpu_custom_call" | custom-call | tf_op jit(solution)/shard_map/pallas_call | solution.py:1210
  165.4 8.5 %shard_map.290 = (f32[192,1024]{1,0:T(8,128)}, f32[192,1024]{1,0:T(8,128)}, f32[768,768]{1,0:T(8,128)}, f32[768,768]{1,0:T(8,128)}, f32[768,768]{1,0:T(8,128)}, ...) custom-call(f32[192,1024]{1,0:T(8,128)} %get-tuple-element.35.out_in, ...), custom_call_target="tpu_custom_call" | custom-call | tf_op jit(solution)/shard_map/pallas_call | solution.py:1277

commit v6 on v5

--- a/solution.py
+++ b/solution.py
@@ -674,7 +674,6 @@
 
     def pass_set(index):
         for line in (g_line, mix_line):
-            line.send_own([index], middle, inward=False)
             line.long_way(index)
 
     mix_line.long_way(0, next_hops)
@@ -799,6 +798,8 @@
                     mix_line.send_own([1], middle, inward=False)
                     mix_line.long_way(1)
                 elif which + 1 < ways:
+                    for line in (g_line, mix_line):
+                        line.send_own([which + 1], middle, inward=False)
                     for line in (g_line, mix_line):
                         line.settle(range(ways - 1), range(which + 1))
 
@@ -928,6 +929,7 @@
         return carry
 
     lax.fori_loop(0, ways, grad_time, 0)
+    big_step(0)
 
     def sum_slot(index, at, size):
         if index < seq // 128:
@@ -973,7 +975,6 @@
         return carry
 
     lax.fori_loop(0, own // tall, chain_rows, 0)
-    big_step(0)
     big_step(1)
 
     def finish_sums():
@@ -1089,8 +1090,6 @@
     wave_grad = tn(cols[:, 64:128], kgr[...], highest) * jnp.cos(arg[...])
     finish_sums()
     two_tasks.pop(0)()
-    big_step(0)
-    big_step(1)
     for index in every:
         near(h_sum, 0, index)
     sm[0:own, 64:128] = nt(kgr[...], jnp.sin(arg[...]), highest)
@@ -1106,21 +1105,23 @@
     zbox[z] = sm[own:, :]
     z_msg.start()
     two_tasks.pop(0)()
+    big_step(0)
+    big_step(1)
     small_step(0, 0)
     for k in range(ways - 2):
         e_sum.first(k, by_end(3))
-    for index in every:
-        far(h_sum, 0, index)
     two_tasks.pop(0)()
     for index in every:
         h_sum.first(2, plain_order[index])
     for index in every:
+        e_sum.first(ways - 2, by_end(index))
+    two_tasks.pop(0)()
+    for index in every:
         near(h_sum, 1, index)
+    for index in every:
+        far(h_sum, 0, index)
     for k in range(ways - 2):
         near(e_sum, k, 3)
-    for index in every:
-        e_sum.first(ways - 2, by_end(index))
-    two_tasks.pop(0)()
     small_step(0, 1)
     z_msg.wait_recv()
     zsum = zbox[0]

time: 174 us -> 173 us (level)
  no operation moved by 1% of the time
where the time goes in v6:
time: 173 us
  Pallas kernels  172 us (99%)
    pallas_call x1, Pallas kernels, layer(): pl.pallas_call(functools.partial(layer_kernel, cfg), out_shape=[jax.Shape...  163 us
    pallas_call x1, Pallas kernels, widen(): pl.pallas_call(functools.partial(widen_kernel, cfg, count), out_shape=[ja...  8.54 us

profile of v6, /device:TPU:0, one launch (start us, length us, event | category | flops | bytes accessed | tf_op | source)
XLA Modules:
  0.0 172.7 jit_solution(17032206944443375344)
XLA Ops:
  0.7 163.3 %shard_map.289 = (f32[192,1024]{1,0:T(8,128)}, f32[192,1024]{1,0:T(8,128)}, bf16[2304,768]{1,0:T(8,128)(2,1)}, bf16[768,768]{1,0:T(8,128)(2,1)}, f32[272,128]{1,0:T(8,128)}) custom-call(bf16[192,1024]{1,0:T(8,128)(2,1)} %bitcast.29, bf16[192,1024]{1,0:T(8,128)(2,1)} %bitcast.30, bf16[192,768]{1,0:T(8,128)(2,1)} %bitcast.31, bf16[576,768]{1,0:T(8,128)(2,1)} %bitcast.28, ...), custom_call_target="tpu_custom_call" | custom-call | tf_op jit(solution)/shard_map/pallas_call | solution.py:1211
  164.0 8.5 %shard_map.290 = (f32[192,1024]{1,0:T(8,128)}, f32[192,1024]{1,0:T(8,128)}, f32[768,768]{1,0:T(8,128)}, f32[768,768]{1,0:T(8,128)}, f32[768,768]{1,0:T(8,128)}, ...) custom-call(f32[192,1024]{1,0:T(8,128)} %get-tuple-element.35.out_in, ...), custom_call_target="tpu_custom_call" | custom-call | tf_op jit(solution)/shard_map/pallas_call | solution.py:1278

commit v7 on v6

--- a/solution.py
+++ b/solution.py
@@ -784,9 +784,14 @@
         q = turn_tokens(index)
         mix_line.take(index)
 
+        @at_turn(2)
+        def _():
+            for k in range(ways - 1):
+                e_sum.first(k, by_end(0))
+
         @at_turn(ways - 1)
         def _():
-            for early_index in first_two:
+            for early_index in (1, 2):
                 for k in range(ways - 2):
                     e_sum.first(k, by_end(early_index))
 
@@ -885,8 +890,6 @@
     big_step(1)
     swap_mix.wait_recv()
     swap_proj.start()
-    for k in range(ways - 2):
-        e_sum.first(k, by_end(2))
     for index in first_two:
         for k in range(ways - 2):
             e_sum.near(k, by_end(index))
@@ -1113,7 +1116,7 @@
     two_tasks.pop(0)()
     for index in every:
         h_sum.first(2, plain_order[index])
-    for index in every:
+    for index in range(1, ways):
         e_sum.first(ways - 2, by_end(index))
     two_tasks.pop(0)()
     for index in every:
@@ -1122,13 +1125,13 @@
         far(h_sum, 0, index)
     for k in range(ways - 2):
         near(e_sum, k, 3)
-    small_step(0, 1)
     z_msg.wait_recv()
     zsum = zbox[0]
     for other in range(1, ways):
         zsum = zsum + zbox[other]
     sm[own:, :] = zsum
     small_copy(1, 0).start()
+    small_step(0, 1)
     small_step(1, 0)
     far(e_sum, 0, 2)
     two_tasks.pop(0)()

time: 173 us -> 173 us (level)
  no operation moved by 1% of the time
where the time goes in v7:
time: 173 us
  Pallas kernels  172 us (99%)
    pallas_call x1, Pallas kernels, layer(): pl.pallas_call(functools.partial(layer_kernel, cfg), out_shape=[jax.Shape...  163 us
    pallas_call x1, Pallas kernels, widen(): pl.pallas_call(functools.partial(widen_kernel, cfg, count), out_shape=[ja...  8.54 us

profile of v7, /device:TPU:0, one launch (start us, length us, event | category | flops | bytes accessed | tf_op | source)
XLA Modules:
  0.0 172.5 jit_solution(16814546637950118753)
XLA Ops:
  0.7 163.1 %shard_map.289 = (f32[192,1024]{1,0:T(8,128)}, f32[192,1024]{1,0:T(8,128)}, bf16[2304,768]{1,0:T(8,128)(2,1)}, bf16[768,768]{1,0:T(8,128)(2,1)}, f32[272,128]{1,0:T(8,128)}) custom-call(bf16[192,1024]{1,0:T(8,128)(2,1)} %bitcast.29, bf16[192,1024]{1,0:T(8,128)(2,1)} %bitcast.30, bf16[192,768]{1,0:T(8,128)(2,1)} %bitcast.31, bf16[576,768]{1,0:T(8,128)(2,1)} %bitcast.28, ...), custom_call_target="tpu_custom_call" | custom-call | tf_op jit(solution)/shard_map/pallas_call | solution.py:1214
  163.8 8.5 %shard_map.290 = (f32[192,1024]{1,0:T(8,128)}, f32[192,1024]{1,0:T(8,128)}, f32[768,768]{1,0:T(8,128)}, f32[768,768]{1,0:T(8,128)}, f32[768,768]{1,0:T(8,128)}, ...) custom-call(f32[192,1024]{1,0:T(8,128)} %get-tuple-element.35.out_in, ...), custom_call_target="tpu_custom_call" | custom-call | tf_op jit(solution)/shard_map/pallas_call | solution.py:1281
